TPU v7x, 128 devices: a whole 4x4x4 slice. The times are simulated.
128 devices in a mesh: ctx: 8 (over y, core), head: 16 (over z, x).
Axes of the slice: x: 4, y: 4, z: 4, core: 2. Of those that a mesh axis runs over, the one named last changes fastest.
Arguments:
- tokens: bfloat16 [8192, 2048], P('ctx', 'head'), may hold values from -6 to 6
- beta: float32 [8192, 16], P('ctx', 'head'), may hold values from 0 to 2
- w_query: bfloat16 [2048, 2048], P(None, 'head'), may hold values from -0.125 to 0.125
- w_key: bfloat16 [2048, 2048], P(None, 'head'), may hold values from -0.125 to 0.125
- w_value: bfloat16 [2048, 2048], P(None, 'head'), may hold values from -0.125 to 0.125
- gain: float32 [128], replicated, may hold values from 0.25 to 1.75
- w_out: bfloat16 [2048, 2048], P('head'), may hold values from -0.125 to 0.125
Outputs:
- mixed: bfloat16 [8192, 2048], P(('ctx', 'head'))
All inputs are finite; a program needn't handle non-finite values.
Results may differ from a plain program's by a relative error of at most 0.023.
Values may be sent and summed in bfloat16 or wider, within the bound.
No kernel may reach another device: no remote copies, remote signals or barrier semaphores. Data moves between devices by JAX's collectives and lax.ppermute only.
A program may use at most 64 MiB of HBM per device.

v0:
```python
import jax
import jax.numpy as jnp
from jax import lax
from jax.sharding import PartitionSpec as P

DK = 128
BLOCK = 64


def passed_along(value, axis, steps):
    count = lax.axis_size(axis)
    first, last = (max(0, -steps), min(count, count - steps))
    return lax.ppermute(value, axis, [(source, source + steps) for source in range(first, last)])


def matmul(left, right):
    return jnp.dot(left, right, precision=lax.Precision.HIGHEST, preferred_element_type=jnp.float32)


def unit_rows(matrix):
    return matrix * lax.rsqrt(jnp.sum(matrix * matrix, axis=-1, keepdims=True) + 1e-06)


def block_factors(block_key, block_value, block_rate):
    lower_tri = jnp.tril(block_rate[:, None] * matmul(block_key, block_key.T), -1) + jnp.eye(
        BLOCK, dtype=jnp.float32
    )
    key_factor = jax.scipy.linalg.solve_triangular(
        lower_tri, block_rate[:, None] * block_key, lower=True, unit_diagonal=True
    )
    value_factor = jax.scipy.linalg.solve_triangular(
        lower_tri, block_rate[:, None] * block_value, lower=True, unit_diagonal=True
    )
    return (key_factor, value_factor)


def shard_transition(keys, value_rows, rates):
    count = keys.shape[0] // BLOCK
    block_keys = keys.reshape(count, BLOCK, DK)
    key_factor, value_factor = jax.vmap(block_factors)(
        block_keys, value_rows.reshape(count, BLOCK, DK), rates.reshape(count, BLOCK)
    )
    identity_mat = jnp.eye(DK, dtype=jnp.float32)
    block_mult = identity_mat - jnp.einsum(
        "nck,ncj->nkj", key_factor, block_keys, precision=lax.Precision.HIGHEST
    )
    block_add = jnp.einsum(
        "ncv,nck->nvk", value_factor, block_keys, precision=lax.Precision.HIGHEST
    )

    def compose(carried, block_map):
        multiplier, addend = carried
        next_mult, next_add = block_map
        return ((matmul(multiplier, next_mult), matmul(addend, next_mult) + next_add), None)

    start_pair = (identity_mat, jnp.zeros((DK, DK), jnp.float32))
    (multiplier, addend), _ = lax.scan(compose, start_pair, (block_mult, block_add))
    return (key_factor, value_factor, multiplier, addend)


def shard_outputs(queries, keys, key_factor, value_factor, memory_state):
    count = keys.shape[0] // BLOCK

    def advance(current, block_data):
        block_query, block_key, block_kf, block_vf = block_data
        written = block_vf - matmul(block_kf, current.T)
        output_rows = matmul(block_query, current.T) + matmul(
            jnp.tril(matmul(block_query, block_key.T)), written
        )
        return (current + matmul(written.T, block_key), output_rows)

    blocked = (
        queries.reshape(count, BLOCK, DK),
        keys.reshape(count, BLOCK, DK),
        key_factor,
        value_factor,
    )
    _, outputs = lax.scan(advance, memory_state, blocked)
    return outputs.reshape(count * BLOCK, DK)


def local(tokens, beta, w_query, w_key, w_value, gain, w_out):
    tok_rows = tokens.shape[0]
    head_width = w_query.shape[1]
    heads_here = beta.shape[1]
    portion = lax.all_gather(tokens, "head", axis=1, tiled=True)
    raw_query, raw_key, raw_value = tuple(
        (
            jnp.dot(portion, weight, preferred_element_type=jnp.float32)
            for index, weight in enumerate((w_query, w_key, w_value))
        )
    )

    def split_heads(matrix):
        return matrix.reshape(tok_rows, heads_here, DK).transpose(1, 0, 2)

    queries = unit_rows(jax.nn.silu(split_heads(raw_query)))
    keys = unit_rows(jax.nn.silu(split_heads(raw_key)))
    value_rows = split_heads(raw_value)
    key_factor, value_factor, multiplier, addend = jax.vmap(shard_transition)(
        keys, value_rows, beta.T
    )

    def relay_turn(counter, carried):
        incoming, outgoing = carried
        incoming = passed_along(outgoing.astype(jnp.bfloat16), "ctx", 1).astype(outgoing.dtype)
        outgoing = (
            jnp.einsum("hij,hjk->hik", incoming, multiplier, precision=lax.Precision.HIGHEST)
            + addend
        )
        return (incoming, outgoing)

    state_in, _ = lax.fori_loop(
        0, lax.axis_size("ctx") - 1, relay_turn, (jnp.zeros_like(addend), addend)
    )
    recurrent = jax.vmap(shard_outputs)(queries, keys, key_factor, value_factor, state_in)
    scale_inv = lax.rsqrt(jnp.mean(recurrent * recurrent, axis=-1, keepdims=True) + 1e-05)
    normed = (recurrent * scale_inv * gain).astype(jnp.bfloat16)
    normed = normed.transpose(1, 0, 2).reshape(tok_rows, head_width)
    portion = normed
    return lax.psum_scatter(
        jnp.dot(portion, w_out, preferred_element_type=jnp.float32).astype(jnp.bfloat16),
        "head",
        scatter_dimension=0,
        tiled=True,
    )


def solution(mesh):
    placed = (
        P("ctx", "head"),
        P("ctx", "head"),
        P(None, "head"),
        P(None, "head"),
        P(None, "head"),
        P(),
        P("head", None),
    )
    return jax.shard_map(
        local, mesh=mesh, in_specs=placed, out_specs=P(("ctx", "head"), None), check_vma=False
    )
```

profile of v0, /device:TPU:0, one launch (start us, length us, event | category | flops | bytes accessed | tf_op | source)
XLA Modules:
  0.0 403.8 jit_solution(17128297159430794123)
XLA Ops:
  7.9 1.3 reduce.9
  9.4 60.2 %all-gather.2.cloned.1.call-done = bf16[1024,2048]{1,0:T(8,128)(2,1)} async-done(((bf16[1024,128]{1,0:T(8,128)(2,1)}), bf16[1024,2048]{1,0:T(8,128)(2,1)}) %all-gather.2.cloned.1.call-update) | async-done | bytes 4194320 | tf_op jit(solution)/shard_map/all_gather | solution.py:86
  69.7 3.8 multiply_reduce_fusion.2
  73.5 2.1 multiply_reduce_fusion.1
  76.7 78.8 %custom-call.4 = f32[1,16,1,64,64]{3,4,2,1,0:T(8,128)S(1)} custom-call(f32[1,16,1,64,64]{4,3,2,1,0:T(8,128)S(1)} %fusion.39), custom_call_target="InvertDiagBlocksLowerTriangular" | custom-call | tf_op jit(solution)/shard_map/vmap(vmap(jit(_solve_triangular)))/triangular_solve | solution.py:28
  155.6 3.4 fusion.56
  159.0 1.1 fusion.42
  160.2 1.1 fusion.44
  161.3 2.8 convolution_bitcast_fusion.3
  164.1 1.8 fusion.33
  166.0 25.5 %while.36 = (s32[]{:T(128)}, f32[1,128,128]{1,2,0:T(8,128)S(1)}, f32[1,128,128]{1,2,0:T(8,128)S(1)}, f32[16,1,128,128]{3,2,1,0:T(8,128)S(1)}, f32[16,1,128,128]{3,2,0,1:T(8,128)}, /*index=5*/s32[]{:T(128)}) while((s32[]{:T(128)}, f32[1,128,128]{1,2,0:T(8,128)S(1)}, f32[1,128,128]{1,2,0:T(8,128)S(1)}, f32[16,1,128,128]{3,2,1,0:T(8,128)S(1)}, ...), condition=%wide.region_2.4_spmd, body=%wide.region_1.0_spmd.sunk | while | flops 50348032 | bytes 983129 | solution.py:57
  191.7 1.2 broadcast_multiply_fusion
  192.9 39.3 %while.37 = (s32[]{:T(128)}, f32[1,128,128]{2,1,0:T(8,128)}, bf16[1,128,128]{2,1,0:T(8,128)(2,1)S(1)}, f32[1,128,128]{2,1,0:T(8,128)S(1)}, f32[1,128,128]{2,1,0:T(8,128)S(1)}, /*index=5*/s32[]{:T(128)}) while((s32[]{:T(128)}, f32[1,128,128]{2,1,0:T(8,128)}, bf16[1,128,128]{2,1,0:T(8,128)(2,1)S(1)}, f32[1,128,128]{2,1,0:T(8,128)S(1)}, ...), condition=%wide.region_4.6_spmd, body=%wide.region_3.5_spmd.sunk | while | flops 25214976 | bytes 426093 | solution.py:113
  192.9 1.3 collective-permute-start
  195.9 4.3 %collective-permute-start = (bf16[1,128,128]{2,1,0:T(8,128)(2,1)S(1)}, bf16[1,128,128]{2,1,0:T(8,128)(2,1)S(1)}, u32[]{:S(2)}, u32[]{:S(2)}) collective-permute-start(bf16[1,128,128]{2,1,0:T(8,128)(2,1)S(1)} %get-tuple-element.287), channel_id=1, source_target_pairs={{0,16},{16,32},{32,48},{48,64},{64,80},{80,96},{96,112},{1,17},{17... | collective-permute-start | bytes 98312 | tf_op jit(solution)/shard_map/while/body/eval_jaxpr/ppermute | solution.py:13
  201.9 4.4 %collective-permute-start = (bf16[1,128,128]{2,1,0:T(8,128)(2,1)S(1)}, bf16[1,128,128]{2,1,0:T(8,128)(2,1)S(1)}, u32[]{:S(2)}, u32[]{:S(2)}) collective-permute-start(bf16[1,128,128]{2,1,0:T(8,128)(2,1)S(1)} %get-tuple-element.287), channel_id=1, source_target_pairs={{0,16},{16,32},{32,48},{48,64},{64,80},{80,96},{96,112},{1,17},{17... | collective-permute-start | bytes 98312 | tf_op jit(solution)/shard_map/while/body/eval_jaxpr/ppermute | solution.py:13
  208.0 4.4 %collective-permute-start = (bf16[1,128,128]{2,1,0:T(8,128)(2,1)S(1)}, bf16[1,128,128]{2,1,0:T(8,128)(2,1)S(1)}, u32[]{:S(2)}, u32[]{:S(2)}) collective-permute-start(bf16[1,128,128]{2,1,0:T(8,128)(2,1)S(1)} %get-tuple-element.287), channel_id=1, source_target_pairs={{0,16},{16,32},{32,48},{48,64},{64,80},{80,96},{96,112},{1,17},{17... | collective-permute-start | bytes 98312 | tf_op jit(solution)/shard_map/while/body/eval_jaxpr/ppermute | solution.py:13
  214.0 4.4 %collective-permute-start = (bf16[1,128,128]{2,1,0:T(8,128)(2,1)S(1)}, bf16[1,128,128]{2,1,0:T(8,128)(2,1)S(1)}, u32[]{:S(2)}, u32[]{:S(2)}) collective-permute-start(bf16[1,128,128]{2,1,0:T(8,128)(2,1)S(1)} %get-tuple-element.287), channel_id=1, source_target_pairs={{0,16},{16,32},{32,48},{48,64},{64,80},{80,96},{96,112},{1,17},{17... | collective-permute-start | bytes 98312 | tf_op jit(solution)/shard_map/while/body/eval_jaxpr/ppermute | solution.py:13
  220.1 4.4 %collective-permute-start = (bf16[1,128,128]{2,1,0:T(8,128)(2,1)S(1)}, bf16[1,128,128]{2,1,0:T(8,128)(2,1)S(1)}, u32[]{:S(2)}, u32[]{:S(2)}) collective-permute-start(bf16[1,128,128]{2,1,0:T(8,128)(2,1)S(1)} %get-tuple-element.287), channel_id=1, source_target_pairs={{0,16},{16,32},{32,48},{48,64},{64,80},{80,96},{96,112},{1,17},{17... | collective-permute-start | bytes 98312 | tf_op jit(solution)/shard_map/while/body/eval_jaxpr/ppermute | solution.py:13
  226.2 4.4 %collective-permute-start = (bf16[1,128,128]{2,1,0:T(8,128)(2,1)S(1)}, bf16[1,128,128]{2,1,0:T(8,128)(2,1)S(1)}, u32[]{:S(2)}, u32[]{:S(2)}) collective-permute-start(bf16[1,128,128]{2,1,0:T(8,128)(2,1)S(1)} %get-tuple-element.287), channel_id=1, source_target_pairs={{0,16},{16,32},{32,48},{48,64},{64,80},{80,96},{96,112},{1,17},{17... | collective-permute-start | bytes 98312 | tf_op jit(solution)/shard_map/while/body/eval_jaxpr/ppermute | solution.py:13
  232.2 78.5 %while.38 = (s32[]{:T(128)}, f32[1,128,128]{2,1,0:T(8,128)}, f32[16,1,64,128]{3,2,1,0:T(8,128)}, f32[16,1,64,128]{3,2,1,0:T(8,128)S(1)}, f32[16,1,64,128]{3,2,1,...) while((s32[]{:T(128)}, f32[1,128,128]{2,1,0:T(8,128)}, ...), condition=%wide.region_7.9_spmd, body=%wide.region_6.8_spmd.sunk | while | flops 50372608 | bytes 690281 | solution.py:78
  232.3 1.1 convolution_subtract_fusion.3
  233.3 1.1 fusion.114
  234.6 1.8 fusion.113
  237.2 1.1 convolution_subtract_fusion.3
  238.3 1.1 fusion.114
  239.5 1.8 fusion.113
  242.1 1.1 convolution_subtract_fusion.3
  243.2 1.1 fusion.114
  244.4 1.8 fusion.113
  247.0 1.1 convolution_subtract_fusion.3
  248.1 1.1 fusion.114
  249.3 1.8 fusion.113
  253.0 1.1 fusion.114
  254.2 1.8 fusion.113
  257.9 1.1 fusion.114
  259.1 1.8 fusion.113
  261.7 1.1 convolution_subtract_fusion.3
  262.8 1.1 fusion.114
  264.0 1.8 fusion.113
  266.6 1.1 convolution_subtract_fusion.3
  267.7 1.1 fusion.114
  268.9 1.8 fusion.113
  271.5 1.1 convolution_subtract_fusion.3
  272.6 1.1 fusion.114
  273.9 1.8 fusion.113
  277.5 1.1 fusion.114
  278.8 1.8 fusion.113
  282.4 1.1 fusion.114
  283.7 1.8 fusion.113
  287.3 1.1 fusion.114
  288.6 1.8 fusion.113
  292.2 1.1 fusion.114
  293.5 1.8 fusion.113
  297.1 1.1 fusion.114
  298.4 1.8 fusion.113
  302.0 1.1 fusion.114
  303.3 1.8 fusion.113
  306.9 1.1 fusion.114
  308.2 1.8 fusion.113
  310.7 1.2 multiply_reduce_fusion
  312.1 1.2 fusion.41
  313.3 3.2 convolution_convert_fusion
  316.5 80.4 %reduce-scatter.2.cloned.1.call-done = bf16[64,2048]{1,0:T(8,128)(2,1)} async-done(((bf16[1024,2048]{1,0:T(8,128)(2,1)}), bf16[64,2048]{1,0:T(8,128)(2,1)}) %reduce-scatter.2.cloned.1.call-update) | async-done | bytes 262160 | tf_op jit(solution)/shard_map/reduce_scatter | solution.py:121
  (191 shorter events, 64.1 us)
Async XLA Ops:
  6.5 306.8 %copy-start = (bf16[128,2048]{1,0:T(8,128)(2,1)S(1)}, bf16[128,2048]{1,0:T(8,128)(2,1)}, u32[]{:S(2)}) copy-start(bf16[128,2048]{1,0:T(8,128)(2,1)} %param.21) | copy-start | bytes 1572868
  6.5 63.1 %all-gather.2.cloned.1.call-start = ((), (), s32[]{:S(2)}) async-start(), calls=%async_computation.1 | async-start | bytes 4456448 | tf_op jit(solution)/shard_map/all_gather | solution.py:86
  7.3 389.7 %reduce-scatter.2.cloned.1.call-start = ((), (), s32[]{:S(2)}) async-start(), calls=%async_computation.2 | async-start | bytes 4456448 | tf_op jit(solution)/shard_map/reduce_scatter | solution.py:121
  9.4 64.0 %copy-start.4 = (bf16[2048,128]{1,0:T(8,128)(2,1)S(1)}, bf16[2048,128]{1,0:T(8,128)(2,1)}, u32[]{:S(2)}) copy-start(bf16[2048,128]{1,0:T(8,128)(2,1)} %param.17) | copy-start | bytes 1572868
  69.7 3.8 copy-start.1
  73.5 82.1 %copy-start.2 = (bf16[2048,128]{1,0:T(8,128)(2,1)S(1)}, bf16[2048,128]{1,0:T(8,128)(2,1)}, u32[]{:S(2)}) copy-start(bf16[2048,128]{1,0:T(8,128)(2,1)} %param.19) | copy-start | bytes 1572868
  191.5 120.6 %copy-start.3 = (f32[128]{0:T(128)S(1)}, f32[128]{0:T(128)}, u32[]{:S(2)}) copy-start(f32[128]{0:T(128)} %param.20) | copy-start | bytes 1540
  192.9 2.1 collective-permute-start
  195.9 5.1 %collective-permute-start = (bf16[1,128,128]{2,1,0:T(8,128)(2,1)S(1)}, bf16[1,128,128]{2,1,0:T(8,128)(2,1)S(1)}, u32[]{:S(2)}, u32[]{:S(2)}) collective-permute-start(bf16[1,128,128]{2,1,0:T(8,128)(2,1)S(1)} %get-tuple-element.287), channel_id=1, source_target_pairs={{0,16},{16,32},{32,48},{48,64},{64,80},{80,96},{96,112},{1,17},{17... | collective-permute-start | bytes 98312 | tf_op jit(solution)/shard_map/while/body/eval_jaxpr/ppermute | solution.py:13
  201.9 5.2 %collective-permute-start = (bf16[1,128,128]{2,1,0:T(8,128)(2,1)S(1)}, bf16[1,128,128]{2,1,0:T(8,128)(2,1)S(1)}, u32[]{:S(2)}, u32[]{:S(2)}) collective-permute-start(bf16[1,128,128]{2,1,0:T(8,128)(2,1)S(1)} %get-tuple-element.287), channel_id=1, source_target_pairs={{0,16},{16,32},{32,48},{48,64},{64,80},{80,96},{96,112},{1,17},{17... | collective-permute-start | bytes 98312 | tf_op jit(solution)/shard_map/while/body/eval_jaxpr/ppermute | solution.py:13
  208.0 5.2 %collective-permute-start = (bf16[1,128,128]{2,1,0:T(8,128)(2,1)S(1)}, bf16[1,128,128]{2,1,0:T(8,128)(2,1)S(1)}, u32[]{:S(2)}, u32[]{:S(2)}) collective-permute-start(bf16[1,128,128]{2,1,0:T(8,128)(2,1)S(1)} %get-tuple-element.287), channel_id=1, source_target_pairs={{0,16},{16,32},{32,48},{48,64},{64,80},{80,96},{96,112},{1,17},{17... | collective-permute-start | bytes 98312 | tf_op jit(solution)/shard_map/while/body/eval_jaxpr/ppermute | solution.py:13
  214.0 5.2 %collective-permute-start = (bf16[1,128,128]{2,1,0:T(8,128)(2,1)S(1)}, bf16[1,128,128]{2,1,0:T(8,128)(2,1)S(1)}, u32[]{:S(2)}, u32[]{:S(2)}) collective-permute-start(bf16[1,128,128]{2,1,0:T(8,128)(2,1)S(1)} %get-tuple-element.287), channel_id=1, source_target_pairs={{0,16},{16,32},{32,48},{48,64},{64,80},{80,96},{96,112},{1,17},{17... | collective-permute-start | bytes 98312 | tf_op jit(solution)/shard_map/while/body/eval_jaxpr/ppermute | solution.py:13
  220.1 5.2 %collective-permute-start = (bf16[1,128,128]{2,1,0:T(8,128)(2,1)S(1)}, bf16[1,128,128]{2,1,0:T(8,128)(2,1)S(1)}, u32[]{:S(2)}, u32[]{:S(2)}) collective-permute-start(bf16[1,128,128]{2,1,0:T(8,128)(2,1)S(1)} %get-tuple-element.287), channel_id=1, source_target_pairs={{0,16},{16,32},{32,48},{48,64},{64,80},{80,96},{96,112},{1,17},{17... | collective-permute-start | bytes 98312 | tf_op jit(solution)/shard_map/while/body/eval_jaxpr/ppermute | solution.py:13
  226.2 5.2 %collective-permute-start = (bf16[1,128,128]{2,1,0:T(8,128)(2,1)S(1)}, bf16[1,128,128]{2,1,0:T(8,128)(2,1)S(1)}, u32[]{:S(2)}, u32[]{:S(2)}) collective-permute-start(bf16[1,128,128]{2,1,0:T(8,128)(2,1)S(1)} %get-tuple-element.287), channel_id=1, source_target_pairs={{0,16},{16,32},{32,48},{48,64},{64,80},{80,96},{96,112},{1,17},{17... | collective-permute-start | bytes 98312 | tf_op jit(solution)/shard_map/while/body/eval_jaxpr/ppermute | solution.py:13
Sparse Core Ops, SparseCore 0:
  9.5 60.1 all-gather.1
  316.6 80.2 reduce-scatter.1
where the time goes:
time: 407 us; the launch traced here: 404 us
  waiting for transfers between devices  147 us (36%)
  matrix products  109 us (27%)
  other arithmetic  88.7 us (22%)
  starting transfers between devices  27.5 us (7%)
  local copies, waits for them, and re-layouts  16.1 us (4%)
  between operations  13.6 us (3%)
    dot_general x113, matrix products, matmul(): jnp.dot(left, right, precision=lax.Precision.HIGHEST, preferred_element_t...  88.4 us
    reduce_scatter x1, waiting for transfers between devices, local(): lax.psum_scatter(jnp.dot(portion, w_out, preferred_element_type=jnp.float...  80.4 us
    another operation x4, other arithmetic, block_factors(): jax.scipy.linalg.solve_triangular(lower_tri, block_rate[:, None] * block_...  78.9 us
    all_gather x1, waiting for transfers between devices, local(): portion = lax.all_gather(tokens, 'head', axis=1, tiled=True)  60.2 us
    ppermute x7, starting transfers between devices, passed_along(): lax.ppermute(value, axis, [(source, source + steps) for source in range(f...  27.5 us
    dynamic_slice x32, local copies, waits for them, and re-layouts, shard_transition(): lax.scan(compose, start_pair, (block_mult, block_add))  15 us
    dot_general x3, matrix products, local(): jnp.dot(portion, weight, preferred_element_type=jnp.float32)  9.29 us
  transfers between devices with their start and end apart: 9, of which 9 were waited for; matrix products, arithmetic and copies ran while one was open for 1% of the time, Pallas kernels for 0%

commit v1 on v0

v1 whole, which is shorter than its diff:
```python
import jax
import jax.numpy as jnp
from jax import lax
from jax.experimental import pallas as pl
from jax.experimental.pallas import tpu as pltpu
from jax.sharding import PartitionSpec as P

DK = 128
CHUNK = 128
F32 = jnp.float32
BF16 = jnp.bfloat16
SMEM = pl.BlockSpec(memory_space=pltpu.SMEM)
VMEM = pl.BlockSpec(memory_space=pltpu.VMEM)
LIMIT = 40 << 20


def dot(left, right, contract=((1,), (0,))):
    return lax.dot_general(
        left.astype(BF16), right.astype(BF16), (contract, ((), ())), preferred_element_type=F32
    )


def swap(value, even, odd, ctx, heads):
    pairs = [
        (c * heads + h, c * heads + (h ^ (odd if c % 2 else even)))
        for c in range(ctx)
        for h in range(heads)
    ]
    return lax.ppermute(value, ("ctx", "head"), pairs)


ALONG_X = ((1, 3), (3, 1))
ALONG_Z = ((4, 12), (12, 4))


def doubled(value, masks, ctx, heads):
    return swap(value, *masks, ctx, heads)


def piece_heads(first, second):
    me = lax.axis_index("head")
    core = lax.axis_index("ctx") % 2

    def of_core(c):
        orders = []
        for axis in (first, second):
            one, two = axis[0][c], axis[1][c]
            orders.append([0, one, two, one ^ two])
        return jnp.array([b ^ a for b in orders[1] for a in orders[0]], jnp.int32)

    own = me ^ jnp.where(core == 0, of_core(0), of_core(1))
    other = me ^ jnp.where(core == 0, of_core(1), of_core(0))
    return own, other


def project_part(heads_ref, pieces_ref, weights, base):
    total = None
    for p in range(0, 8, 2):
        left = jnp.concatenate([pieces_ref[p], pieces_ref[p + 1]], axis=1)
        rows = []
        for q in (p, p + 1):
            start = pl.multiple_of(heads_ref[base + q] * DK, DK)
            rows.append(
                jnp.concatenate([w[pl.ds(start, DK), :] for w in weights], axis=1)
            )
        term = jnp.dot(left, jnp.concatenate(rows, axis=0), preferred_element_type=F32)
        total = term if total is None else total + term
    return total


def first_half_kernel(ha, hb, a_ref, b_ref, wq, wk, wv, raw_ref):
    half = a_ref.shape[1]
    raw_ref[:half, :] = project_part(ha, a_ref, (wq, wk, wv), 0)
    raw_ref[half:, :] = project_part(hb, b_ref, (wq, wk, wv), 0)


def unit_silu(raw):
    act = raw / (1.0 + jnp.exp(jnp.minimum(-raw, 80.0)))
    return act * lax.rsqrt(jnp.sum(act * act, axis=-1, keepdims=True) + 1e-6)


def transition_kernel(
    ha, hb, raw_ref, a_ref, b_ref, wq, wk, wv, beta_ref,
    q_ref, k_ref, wu_ref, states_ref, last_ref, total_ref,
):
    rows = raw_ref.shape[0]
    half = rows // 2
    count = rows // CHUNK
    total_ref[:half, :] = raw_ref[:half, :] + project_part(ha, a_ref, (wq, wk, wv), 8)
    total_ref[half:, :] = raw_ref[half:, :] + project_part(hb, b_ref, (wq, wk, wv), 8)
    row = lax.broadcasted_iota(jnp.int32, (CHUNK, CHUNK), 0)
    col = lax.broadcasted_iota(jnp.int32, (CHUNK, CHUNK), 1)
    eye = (row == col).astype(F32)

    def below(size):
        return (row // (2 * size) == col // (2 * size)) & (
            (row // size) % 2 == 1
        ) & ((col // size) % 2 == 0)

    keys, rates, lowers, inverses = [], [], [], []
    for b in range(count):
        part = slice(b * CHUNK, (b + 1) * CHUNK)
        q_ref[part, :] = unit_silu(total_ref[part, :DK]).astype(BF16)
        key = unit_silu(total_ref[part, DK : 2 * DK])
        key16 = key.astype(BF16)
        k_ref[part, :] = key16
        rate = jnp.transpose(jnp.broadcast_to(beta_ref[b : b + 1, :], (CHUNK, CHUNK)))
        gram = dot(key16, key16, ((1,), (1,)))
        lower = jnp.where(row > col, rate * gram, 0.0)
        keys.append(key)
        rates.append(rate)
        lowers.append(lower)
        inverses.append(eye - jnp.where(below(1), lower, 0.0))
    size = 2
    while size < CHUNK:
        mask = below(size)
        inner = [dot(jnp.where(mask, lo, 0.0), inv) for lo, inv in zip(lowers, inverses)]
        inverses = [inv - dot(inv, x) for inv, x in zip(inverses, inner)]
        size *= 2
    maps = []
    for b in range(count):
        part = slice(b * CHUNK, (b + 1) * CHUNK)
        value = total_ref[part, 2 * DK :]
        both = jnp.concatenate([rates[b] * keys[b], rates[b] * value], axis=1)
        wu = dot(inverses[b], both).astype(BF16)
        wu_ref[part, :] = wu
        maps.append(dot(k_ref[part, :], wu, ((0,), (0,))))
    zeros = jnp.zeros((DK, DK), F32)
    state = jnp.concatenate([eye, zeros], axis=1)
    for b in range(count):
        state16 = state.astype(BF16)
        states_ref[b] = state16
        state = (
            state
            - dot(maps[b][:, :DK], state16)
            + jnp.concatenate([zeros, maps[b][:, DK:]], axis=1)
        )
    last_ref[...] = state


def outputs_kernel(q_ref, k_ref, wu_ref, states_ref, query_ref, out_ref):
    rows = q_ref.shape[0]
    row = lax.broadcasted_iota(jnp.int32, (CHUNK, CHUNK), 0)
    col = lax.broadcasted_iota(jnp.int32, (CHUNK, CHUNK), 1)
    for b in range(rows // CHUNK):
        part = slice(b * CHUNK, (b + 1) * CHUNK)
        query = q_ref[part, :]
        scores = jnp.where(row >= col, dot(query, k_ref[part, :], ((1,), (1,))), 0.0)
        local = dot(scores, wu_ref[part, :])
        effective = query.astype(F32) - local[:, :DK]
        result = dot(effective, states_ref[b])
        query_ref[part, :] = result[:, :DK].astype(BF16)
        out_ref[part, :] = result[:, DK:] + local[:, DK:]


def compose(later, earlier):
    return dot(later[:, :DK], earlier) + jnp.concatenate(
        [jnp.zeros((DK, DK), F32), later[:, DK:]], axis=1
    )


def merge_kernel(upper_ref, span_ref, prefix_ref, other_ref, new_span_ref, new_prefix_ref):
    span, prefix = span_ref[...], prefix_ref[...]
    other = other_ref[...].astype(F32)
    upper = upper_ref[0] == 1
    later = jnp.where(upper, span, other)
    earlier = jnp.where(upper, other, span)
    new_span_ref[...] = compose(later, earlier)
    new_prefix_ref[...] = jnp.where(upper, compose(prefix, other), prefix)


def finish_kernel(upper_ref, prefix_ref, other_ref, query_ref, out_ref, gain_ref, normed_ref):
    prefix = prefix_ref[...]
    other = other_ref[...].astype(F32)
    entering = jnp.where(
        upper_ref[0] == 1,
        dot(prefix[:, :DK], other[:, DK:]) + prefix[:, DK:],
        prefix[:, DK:],
    )
    recurrent = out_ref[...] + dot(query_ref[...], entering)
    scale = lax.rsqrt(jnp.mean(recurrent * recurrent, axis=-1, keepdims=True) + 1e-5)
    normed_ref[...] = (recurrent * scale * gain_ref[...]).astype(BF16)


def mix_kernel(h0, h1, h2, h3, x_ref, *refs):
    pieces, mixed_ref, total_ref = refs[:8], refs[8], refs[9]
    step = pl.program_id(0)
    heads = (h0, h1, h2, h3)
    width = total_ref.shape[1] // 4

    @pl.when(step == 0)
    def _():
        total_ref[...] = jnp.zeros_like(total_ref)

    for quarter in range(4):
        term = None
        for late in range(2):
            piece = pieces[2 * quarter + late]
            j = 8 * late + 2 * step
            left = jnp.concatenate(
                [x_ref[heads[quarter][j]], x_ref[heads[quarter][j + 1]]], axis=1
            )
            right = jnp.concatenate([piece[0], piece[1]], axis=0)
            part = jnp.dot(left, right, preferred_element_type=F32)
            term = part if term is None else term + part
        total_ref[:, quarter * width : (quarter + 1) * width] += term

    @pl.when(step == pl.num_programs(0) - 1)
    def _():
        mixed_ref[...] = total_ref[...].astype(BF16)


def call(kernel, shapes, n_smem, n_vmem, scratch=(), flops=0, size=0):
    return pl.pallas_call(
        kernel,
        out_shape=shapes,
        in_specs=[SMEM] * n_smem + [VMEM] * n_vmem,
        out_specs=jax.tree.map(lambda _: VMEM, shapes),
        scratch_shapes=list(scratch),
        compiler_params=pltpu.CompilerParams(vmem_limit_bytes=LIMIT),
        cost_estimate=pl.CostEstimate(flops=flops, bytes_accessed=size, transcendentals=0),
    )


def struct(shape, dtype):
    return jax.ShapeDtypeStruct(shape, dtype)


def local(tokens, beta, w_query, w_key, w_value, gain, w_out):
    ctx, heads = lax.axis_size("ctx"), lax.axis_size("head")
    rows = tokens.shape[0]
    half = rows // 2
    me_ctx = lax.axis_index("ctx")
    weights = (w_query, w_key, w_value)
    ha, other_a = piece_heads(ALONG_X, ALONG_Z)
    hb, other_b = piece_heads(ALONG_Z, ALONG_X)

    def spread(a, b):
        a, b = a[None], b[None]
        for step in range(4):
            am = (ALONG_X + ALONG_Z)[step]
            bm = (ALONG_Z + ALONG_X)[step]
            na, nb = swap(a, *am, ctx, heads), swap(b, *bm, ctx, heads)
            if step < 3:
                a = jnp.concatenate([a, na], axis=0)
                b = jnp.concatenate([b, nb], axis=0)
        return a, b, na, nb

    ta, tb, na, nb = spread(tokens[:half], tokens[half:])
    raw = call(
        first_half_kernel, struct((rows, 3 * DK), F32), 2, 5, flops=rows * 1024 * 768, size=5 << 20
    )(ha, hb, ta, tb, *weights)
    query, key, wu, states, last = call(
        transition_kernel,
        (
            struct((rows, DK), BF16),
            struct((rows, DK), BF16),
            struct((rows, 2 * DK), BF16),
            struct((rows // CHUNK, DK, 2 * DK), BF16),
            struct((DK, 2 * DK), F32),
        ),
        2, 7,
        scratch=[pltpu.VMEM((rows, 3 * DK), F32)],
        flops=rows * 4096 * 768, size=8 << 20,
    )(ha, hb, raw, na, nb, *weights, beta.reshape(rows // CHUNK, CHUNK))

    core = me_ctx % 2
    width = w_out.shape[1] // 4
    mine = lax.dynamic_slice_in_dim(w_out, core * 2 * width, 2 * width, axis=1)
    oa, ob, pa, pb = spread(mine[:, :width], mine[:, width:])
    flip = [(c, c ^ 1) for c in range(ctx)]
    theirs = [lax.ppermute(v, "ctx", flip) for v in (oa, pa, ob, pb)]
    ours = [oa, pa, ob, pb]

    eff_query, partial = call(
        outputs_kernel,
        (struct((rows, DK), BF16), struct((rows, DK), F32)),
        0, 4,
        flops=rows * 2048 * 256, size=4 << 20,
    )(query, key, wu, states)

    span = last
    prefix = jnp.concatenate([jnp.eye(DK, dtype=F32), jnp.zeros((DK, DK), F32)], axis=1)
    bits = (1, 2)
    for bit in bits:
        other = lax.ppermute(span.astype(BF16), "ctx", [(c, c ^ bit) for c in range(ctx)])
        upper = ((me_ctx // bit) % 2).astype(jnp.int32)[None]
        span, prefix = call(
            merge_kernel, (struct((DK, 2 * DK), F32),) * 2, 1, 3, flops=1 << 24, size=1 << 19
        )(upper, span, prefix, other)
    other = lax.ppermute(span.astype(BF16), "ctx", [(c, c ^ 6) for c in range(ctx)])
    upper = (me_ctx // 4).astype(jnp.int32)[None]
    normed = call(
        finish_kernel, struct((rows, DK), BF16), 1, 5, flops=rows * 128 * 256, size=2 << 20
    )(upper, prefix, other, eff_query, partial, gain[None, :])

    spread_rows = lax.all_to_all(normed, "head", 0, 0, tiled=True).reshape(
        heads, rows // heads, DK
    )

    def mix(blocks_lo, heads_lo, blocks_hi, heads_hi):
        piece = pl.BlockSpec((2, DK, width), lambda i: (i, 0, 0))
        return pl.pallas_call(
            mix_kernel,
            grid=(4,),
            out_shape=struct((rows // heads, 4 * width), BF16),
            in_specs=[SMEM] * 4
            + [pl.BlockSpec((heads, rows // heads, DK), lambda i: (0, 0, 0))]
            + [piece] * 8,
            out_specs=pl.BlockSpec((rows // heads, 4 * width), lambda i: (0, 0)),
            scratch_shapes=[pltpu.VMEM((rows // heads, 4 * width), F32)],
            compiler_params=pltpu.CompilerParams(vmem_limit_bytes=LIMIT),
            cost_estimate=pl.CostEstimate(
                flops=64 * 2048 * 4096, bytes_accessed=9 << 20, transcendentals=0
            ),
        )(*heads_lo, *heads_hi, spread_rows, *blocks_lo, *blocks_hi)

    return lax.cond(
        core == 0,
        lambda: mix(ours, (ha, hb), theirs, (other_a, other_b)),
        lambda: mix(theirs, (other_a, other_b), ours, (ha, hb)),
    )


def solution(mesh):
    placed = (
        P("ctx", "head"),
        P("ctx", "head"),
        P(None, "head"),
        P(None, "head"),
        P(None, "head"),
        P(),
        P("head", None),
    )
    return jax.shard_map(
        local, mesh=mesh, in_specs=placed, out_specs=P(("ctx", "head"), None), check_vma=False
    )
```

time: 407 us -> 99.9 us (0.25)
  waiting for transfers between devices: 147 us -> 36.1 us
  matrix products: 109 us -> 0 us
  other arithmetic: 88.7 us -> 2.77 us
  Pallas kernels: 0 us -> 15.9 us
  between operations: 13.6 us -> 0.28 us
  starting transfers between devices: 27.5 us -> 40.7 us
  local copies, waits for them, and re-layouts: 16.1 us -> 3.74 us
    dot_general x126 -> x0, matrix products: 107 us -> none  [the longest x113 88.4 us: matmul(): jnp.dot(left, right, precision=lax.Precision.HIGHEST, preferred_element_t...]
    reduce_scatter x1 -> x0, waiting for transfers between devices: 80.4 us -> none  [local(): lax.psum_scatter(jnp.dot(portion, w_out, preferred_element_type=jnp.float...]
    another operation x5 -> x0, other arithmetic: 78.9 us -> none  [the longest x4 78.9 us: block_factors(): jax.scipy.linalg.solve_triangular(lower_tri, block_rate[:, None] * block_...]
    all_gather x1 -> x0, waiting for transfers between devices: 60.2 us -> none  [local(): portion = lax.all_gather(tokens, 'head', axis=1, tiled=True)]
    ppermute x7 -> x23, waiting for transfers between devices: 5.88 us -> 27.5 us  [the longest x16 22.7 us: swap(): return lax.ppermute(value, ('ctx', 'head'), pairs)]
    pallas_call x0 -> x7, Pallas kernels: none -> 15.9 us  [the longest x1 6.23 us: local(): call(transition_kernel, (struct((rows, DK), BF16), struct((rows, DK), BF1...]
    dynamic_slice x32 -> x0, local copies, waits for them, and re-layouts: 15 us -> none  [shard_transition(): lax.scan(compose, start_pair, (block_mult, block_add))]
    all_to_all x0 -> x1, waiting for transfers between devices: none -> 8.67 us  [local(): lax.all_to_all(normed, 'head', 0, 0, tiled=True)]
  transfers between devices with their start and end apart: 9 -> 24, of which waited for: 9 -> 13; matrix products, arithmetic and copies ran while one was open for 1% -> 4% of each run, Pallas kernels for 0% -> 11%
where the time goes in v1:
time: 99.9 us; the launch traced here: 99.6 us
  starting transfers between devices  40.7 us (41%)
  waiting for transfers between devices  36.1 us (36%)
  Pallas kernels  15.9 us (16%)
  local copies, waits for them, and re-layouts  3.74 us (4%)
  other arithmetic  2.77 us (3%)
    ppermute x16, starting transfers between devices, swap(): return lax.ppermute(value, ('ctx', 'head'), pairs)  28.9 us
    ppermute x16, waiting for transfers between devices, swap(): return lax.ppermute(value, ('ctx', 'head'), pairs)  22.7 us
    all_to_all x1, waiting for transfers between devices, local(): lax.all_to_all(normed, 'head', 0, 0, tiled=True)  8.67 us
    pallas_call x1, Pallas kernels, local(): call(transition_kernel, (struct((rows, DK), BF16), struct((rows, DK), BF1...  6.23 us
    all_to_all x1, starting transfers between devices, local(): lax.all_to_all(normed, 'head', 0, 0, tiled=True)  5.55 us
    pallas_call x1, Pallas kernels, mix(): pl.pallas_call(mix_kernel, grid=(4,), out_shape=struct((rows // heads, 4...  4.88 us
    ppermute x2, waiting for transfers between devices, local(): lax.ppermute(span.astype(BF16), 'ctx', [(c, c ^ bit) for c in range(ctx)])  3.79 us
    ppermute x1, starting transfers between devices, local(): lax.ppermute(span.astype(BF16), 'ctx', [(c, c ^ 6) for c in range(ctx)])  3.1 us
  transfers between devices with their start and end apart: 24, of which 13 were waited for; matrix products, arithmetic and copies ran while one was open for 4% of the time, Pallas kernels for 11%

profile of v1, /device:TPU:0, one launch (start us, length us, event | category | flops | bytes accessed | tf_op | source)
XLA Modules:
  0.0 99.6 jit_solution(9258913931882208762)
XLA Ops:
  0.0 1.0 slice_bitcast_fusion
  1.0 2.1 %collective-permute-start.3 = (bf16[1,512,128]{2,1,0:T(8,128)(2,1)S(1)}, bf16[1,512,128]{2,1,0:T(8,128)(2,1)S(1)}, u32[]{:S(2)}, u32[]{:S(2)}) collective-permute-start(bf16[1,512,128]{2,1,0:T(8,128)(2,1)S(1)} %get-tuple-element.111), channel_id=1, source_target_pairs={{0,4},{1,5},{2,6},{3,7},{4,0},{5,1},{6,2},{7,3},{8,12},{9,13},{10,... | collective-permute-start | bytes 393224 | tf_op jit(solution)/shard_map/ppermute | solution.py:29
  3.1 1.0 dynamic-slice_bitcast_fusion
  4.1 1.6 %collective-permute-start.11 = (bf16[1,128,512]{2,1,0:T(8,128)(2,1)S(1)}, bf16[1,128,512]{2,1,0:T(8,128)(2,1)S(1)}, u32[]{:S(2)}, u32[]{:S(2)}) collective-permute-start(bf16[1,128,512]{2,1,0:T(8,128)(2,1)S(1)} %get-tuple-element.110), channel_id=1, source_target_pairs={{0,1},{1,0},{2,3},{3,2},{4,5},{5,4},{6,7},{7,6},{8,9},{9,8},{10,11... | collective-permute-start | bytes 393224 | tf_op jit(solution)/shard_map/ppermute | solution.py:29
  5.6 0.4 collective-permute-done.3
  6.1 4.2 %collective-permute-start.4 = (bf16[2,512,128]{2,1,0:T(8,128)(2,1)S(1)}, bf16[2,512,128]{2,1,0:T(8,128)(2,1)S(1)}, u32[]{:S(2)}, u32[]{:S(2)}) collective-permute-start(bf16[2,512,128]{2,1,0:T(8,128)(2,1)S(1)} %pad_maximum_fusion.9), channel_id=1, source_target_pairs={{0,12},{1,13},{2,14},{3,15},{4,8},{5,9},{6,10},{7,11},{8,4},{9,5},... | collective-permute-start | bytes 786440 | tf_op jit(solution)/shard_map/ppermute | solution.py:29
  10.3 1.5 %collective-permute-start = (bf16[1,512,128]{2,1,0:T(8,128)(2,1)S(1)}, bf16[1,512,128]{2,1,0:T(8,128)(2,1)S(1)}, u32[]{:S(2)}, u32[]{:S(2)}) collective-permute-start(bf16[1,512,128]{2,1,0:T(8,128)(2,1)S(1)} %get-tuple-element.112), channel_id=1, source_target_pairs={{0,1},{1,0},{2,3},{3,2},{4,5},{5,4},{6,7},{7,6},{8,9},{9,8},{10,11... | collective-permute-start | bytes 393224 | tf_op jit(solution)/shard_map/ppermute | solution.py:29
  11.8 0.0 collective-permute-done.11
  11.8 2.2 %collective-permute-start.12 = (bf16[2,128,512]{2,1,0:T(8,128)(2,1)S(1)}, bf16[2,128,512]{2,1,0:T(8,128)(2,1)S(1)}, u32[]{:S(2)}, u32[]{:S(2)}) collective-permute-start(bf16[2,128,512]{2,1,0:T(8,128)(2,1)S(1)} %pad_maximum_fusion.10), channel_id=1, source_target_pairs={{0,3},{1,2},{2,1},{3,0},{4,7},{5,6},{6,5},{7,4},{8,11},{9,10},{10,... | collective-permute-start | bytes 786440 | tf_op jit(solution)/shard_map/ppermute | solution.py:29
  14.0 1.3 %collective-permute-done.17 = bf16[1,128,512]{2,1,0:T(8,128)(2,1)S(1)} collective-permute-done((bf16[1,128,512]{2,1,0:T(8,128)(2,1)S(1)}, bf16[1,128,512]{2,1,0:T(8,128)(2,1)S(1)}, u32[]{:S(2)}, u32[]{:S(2)}) %collective-permute-start.17) | collective-permute-done | bytes 131104 | tf_op jit(solution)/shard_map/ppermute | solution.py:29
  15.3 1.6 %collective-permute-start.18 = (bf16[2,128,512]{2,1,0:T(8,128)(2,1)S(1)}, bf16[2,128,512]{2,1,0:T(8,128)(2,1)S(1)}, u32[]{:S(2)}, u32[]{:S(2)}) collective-permute-start(bf16[2,128,512]{2,1,0:T(8,128)(2,1)S(1)} %pad_maximum_fusion.11), channel_id=1, source_target_pairs={{0,12},{1,13},{2,14},{3,15},{4,8},{5,9},{6,10},{7,11},{8,4},{9,5},... | collective-permute-start | bytes 786440 | tf_op jit(solution)/shard_map/ppermute | solution.py:29
  16.9 0.0 collective-permute-done.4
  16.9 0.1 pad_maximum_fusion.5
  16.9 1.6 %collective-permute-start.5 = (bf16[4,512,128]{2,1,0:T(8,128)(2,1)S(1)}, bf16[4,512,128]{2,1,0:T(8,128)(2,1)S(1)}, u32[]{:S(2)}, u32[]{:S(2)}) collective-permute-start(bf16[4,512,128]{2,1,0:T(8,128)(2,1)S(1)} %pad_maximum_fusion.5), channel_id=1, source_target_pairs={{0,1},{1,0},{2,3},{3,2},{4,5},{5,4},{6,7},{7,6},{8,9},{9,8},{10,11... | collective-permute-start | bytes 1572872 | tf_op jit(solution)/shard_map/ppermute | solution.py:29
  18.5 2.2 %collective-permute-start.1 = (bf16[2,512,128]{2,1,0:T(8,128)(2,1)S(1)}, bf16[2,512,128]{2,1,0:T(8,128)(2,1)S(1)}, u32[]{:S(2)}, u32[]{:S(2)}) collective-permute-start(bf16[2,512,128]{2,1,0:T(8,128)(2,1)S(1)} %pad_maximum_fusion.8), channel_id=1, source_target_pairs={{0,3},{1,2},{2,1},{3,0},{4,7},{5,6},{6,5},{7,4},{8,11},{9,10},{10,... | collective-permute-start | bytes 786440 | tf_op jit(solution)/shard_map/ppermute | solution.py:29
  20.7 0.1 pad_maximum_fusion.6
  20.8 1.3 %collective-permute-start.13 = (bf16[4,128,512]{2,1,0:T(8,128)(2,1)S(1)}, bf16[4,128,512]{2,1,0:T(8,128)(2,1)S(1)}, u32[]{:S(2)}, u32[]{:S(2)}) collective-permute-start(bf16[4,128,512]{2,1,0:T(8,128)(2,1)S(1)} %pad_maximum_fusion.6), channel_id=1, source_target_pairs={{0,4},{1,5},{2,6},{3,7},{4,0},{5,1},{6,2},{7,3},{8,12},{9,13},{10,... | collective-permute-start | bytes 1572872 | tf_op jit(solution)/shard_map/ppermute | solution.py:29
  22.1 1.6 %collective-permute-done.18 = bf16[2,128,512]{2,1,0:T(8,128)(2,1)S(1)} collective-permute-done((bf16[2,128,512]{2,1,0:T(8,128)(2,1)S(1)}, bf16[2,128,512]{2,1,0:T(8,128)(2,1)S(1)}, u32[]{:S(2)}, u32[]{:S(2)}) %collective-permute-start.18) | collective-permute-done | bytes 262176 | tf_op jit(solution)/shard_map/ppermute | solution.py:29
  23.7 0.1 pad_maximum_fusion.7
  23.7 1.9 %collective-permute-start.19 = (bf16[4,128,512]{2,1,0:T(8,128)(2,1)S(1)}, bf16[4,128,512]{2,1,0:T(8,128)(2,1)S(1)}, u32[]{:S(2)}, u32[]{:S(2)}) collective-permute-start(bf16[4,128,512]{2,1,0:T(8,128)(2,1)S(1)} %pad_maximum_fusion.7), channel_id=1, source_target_pairs={{0,1},{1,0},{2,3},{3,2},{4,5},{5,4},{6,7},{7,6},{8,9},{9,8},{10,11... | collective-permute-start | bytes 1572872 | tf_op jit(solution)/shard_map/ppermute | solution.py:29
  25.6 3.4 %collective-permute-done.1 = bf16[2,512,128]{2,1,0:T(8,128)(2,1)S(1)} collective-permute-done((bf16[2,512,128]{2,1,0:T(8,128)(2,1)S(1)}, bf16[2,512,128]{2,1,0:T(8,128)(2,1)S(1)}, u32[]{:S(2)}, u32[]{:S(2)}) %collective-permute-start.1) | collective-permute-done | bytes 262176 | tf_op jit(solution)/shard_map/ppermute | solution.py:29
  29.1 0.1 pad_maximum_fusion.4
  29.1 0.1 collective-permute-start.2
  29.2 0.1 pad_maximum_fusion.1.b_ref
  29.3 2.5 %collective-permute-start.7 = (bf16[8,512,128]{2,1,0:T(8,128)(2,1)S(1)}, bf16[8,512,128]{2,1,0:T(8,128)(2,1)}, u32[]{:S(2)}, u32[]{:S(2)}) collective-permute-start(bf16[8,512,128]{2,1,0:T(8,128)(2,1)S(1)} %pad_maximum_fusion.1.b_ref), channel_id=1, source_target_pairs={{0,3},{1,2},{2,1},{3,0},{4,7},{5,6},{6,5},{7,4},{8,11},{9,10},{10,... | collective-permute-start | bytes 3145736 | tf_op jit(solution)/shard_map/ppermute | solution.py:29
  31.8 1.1 %pad_maximum_fusion.2 = bf16[8,128,512]{2,1,0:T(8,128)(2,1)} fusion(bf16[4,128,512]{2,1,0:T(8,128)(2,1)S(1)} %collective-permute-done.13, bf16[2,128,512]{2,1,0:T(8,128)(2,1)S(1)} %collective-permute-done.12, bf16[1,128,512]{2,1,0:T(8,128)(2,1)S(1)} %collective-permute-done.11, bf16[1,128,512]{2,1,0:T(8,128)(2,1)S(1)} %get-tuple-element.110), kind=kLoop, calls=%fused_computation.2 | loop fusion | flops 1572864 | bytes 2097152 | tf_op jit(solution)/shard_map/concatenate | solution.py:245
  32.9 1.4 %collective-permute-start.15 = (bf16[8,128,512]{2,1,0:T(8,128)(2,1)}, bf16[8,128,512]{2,1,0:T(8,128)(2,1)}, u32[]{:S(2)}, u32[]{:S(2)}) collective-permute-start(bf16[8,128,512]{2,1,0:T(8,128)(2,1)} %pad_maximum_fusion.2), channel_id=1, source_target_pairs={{0,12},{1,13},{2,14},{3,15},{4,8},{5,9},{6,10},{7,11},{8,4},{9,5},... | collective-permute-start | bytes 3145736 | tf_op jit(solution)/shard_map/ppermute | solution.py:29
  34.3 3.0 %collective-permute-done.19 = bf16[4,128,512]{2,1,0:T(8,128)(2,1)S(1)} collective-permute-done((bf16[4,128,512]{2,1,0:T(8,128)(2,1)S(1)}, bf16[4,128,512]{2,1,0:T(8,128)(2,1)S(1)}, u32[]{:S(2)}, u32[]{:S(2)}) %collective-permute-start.19) | collective-permute-done | bytes 524320 | tf_op jit(solution)/shard_map/ppermute | solution.py:29
  37.4 1.1 %pad_maximum_fusion.3 = bf16[8,128,512]{2,1,0:T(8,128)(2,1)} fusion(bf16[4,128,512]{2,1,0:T(8,128)(2,1)S(1)} %collective-permute-done.19, bf16[2,128,512]{2,1,0:T(8,128)(2,1)S(1)} %collective-permute-done.18, bf16[1,128,512]{2,1,0:T(8,128)(2,1)S(1)} %collective-permute-done.17, bf16[1,128,512]{2,1,0:T(8,128)(2,1)S(1)} %get-tuple-element.109), kind=kLoop, calls=%fused_computation.3 | loop fusion | flops 1572864 | bytes 2097152 | tf_op jit(solution)/shard_map/concatenate | solution.py:246
  38.5 0.0 copy-start
  38.5 0.0 copy-start.1
  38.5 3.2 %collective-permute-start.21 = (bf16[8,128,512]{2,1,0:T(8,128)(2,1)}, bf16[8,128,512]{2,1,0:T(8,128)(2,1)}, u32[]{:S(2)}, u32[]{:S(2)}) collective-permute-start(bf16[8,128,512]{2,1,0:T(8,128)(2,1)} %pad_maximum_fusion.3), channel_id=1, source_target_pairs={{0,3},{1,2},{2,1},{3,0},{4,7},{5,6},{6,5},{7,4},{8,11},{9,10},{10,... | collective-permute-start | bytes 3145736 | tf_op jit(solution)/shard_map/ppermute | solution.py:29
  41.7 2.3 %collective-permute-done.2 = bf16[4,512,128]{2,1,0:T(8,128)(2,1)S(1)} collective-permute-done((bf16[4,512,128]{2,1,0:T(8,128)(2,1)S(1)}, bf16[4,512,128]{2,1,0:T(8,128)(2,1)S(1)}, u32[]{:S(2)}, u32[]{:S(2)}) %collective-permute-start.2) | collective-permute-done | bytes 524320 | tf_op jit(solution)/shard_map/ppermute | solution.py:29
  44.0 0.1 pad_maximum_fusion.a_ref
  44.1 1.7 %collective-permute-start.6 = (bf16[8,512,128]{2,1,0:T(8,128)(2,1)S(1)}, bf16[8,512,128]{2,1,0:T(8,128)(2,1)}, u32[]{:S(2)}, u32[]{:S(2)}) collective-permute-start(bf16[8,512,128]{2,1,0:T(8,128)(2,1)S(1)} %pad_maximum_fusion.a_ref), channel_id=1, source_target_pairs={{0,12},{1,13},{2,14},{3,15},{4,8},{5,9},{6,10},{7,11},{8,4},{9,5},... | collective-permute-start | bytes 3145736 | tf_op jit(solution)/shard_map/ppermute | solution.py:29
  45.8 0.1 collective-permute-start.14
  45.9 0.0 collective-permute-done.7.b_ref
  45.9 0.5 collective-permute-start.20
  46.4 2.8 %collective-permute-done.15 = bf16[8,128,512]{2,1,0:T(8,128)(2,1)} collective-permute-done((bf16[8,128,512]{2,1,0:T(8,128)(2,1)}, bf16[8,128,512]{2,1,0:T(8,128)(2,1)}, u32[]{:S(2)}, u32[]{:S(2)}) %collective-permute-start.15) | collective-permute-done | bytes 1048608 | tf_op jit(solution)/shard_map/ppermute | solution.py:29
  49.2 0.4 collective-permute-start.16
  49.6 7.1 %collective-permute-done.21 = bf16[8,128,512]{2,1,0:T(8,128)(2,1)} collective-permute-done((bf16[8,128,512]{2,1,0:T(8,128)(2,1)}, bf16[8,128,512]{2,1,0:T(8,128)(2,1)}, u32[]{:S(2)}, u32[]{:S(2)}) %collective-permute-start.21) | collective-permute-done | bytes 1048608 | tf_op jit(solution)/shard_map/ppermute | solution.py:29
  56.8 0.1 collective-permute-start.22
  56.9 0.0 copy-start.2
  56.9 1.0 %copy-done.2 = bf16[2048,128]{1,0:T(8,128)(2,1)S(1)} copy-done((bf16[2048,128]{1,0:T(8,128)(2,1)S(1)}, bf16[2048,128]{1,0:T(8,128)(2,1)}, u32[]{:S(2)}) %copy-start.2) | copy-done | bytes 524312
  58.0 1.8 %shard_map.147.raw_ref = f32[1024,384]{1,0:T(8,128)S(1)} custom-call(s32[16]{0:T(128)S(1)} %get-tuple-element.115.ha, s32[16]{0:T(128)S(1)} %get-tuple-element.118.hb, bf16[8,512,128]{2,1,0:T(8,128)(2,1)S(1)} %pad_maximum_fusion.a_ref, bf16[8,512,128]{2,1,0:T(8,128)(2,1)S(1)} %pad_maximum_fusion.1.b_ref, bf16[2048,128]{1,0:T(8,128)(2,1)S(1)} %copy-done, ...), custom_call_target="tpu_custom_call" | custom-call | flops 805306368 | bytes 5242880 | tf_op jit(solution)/shard_map/pallas_call | solution.py:250
  59.8 0.7 collective-permute-done.6.a_ref
  60.5 6.2 %shard_map.148 = (bf16[1024,128]{1,0:T(8,128)(2,1)S(1)}, bf16[1024,128]{1,0:T(8,128)(2,1)S(1)}, bf16[1024,256]{1,0:T(8,128)(2,1)S(1)}, bf16[8,128,256]{2,1,0:T(8,128)(2,1)S(1)}, f32[128,256]{1,0:T(8,128)S(1)}) custom-call(s32[16]{0:T(128)S(1)} %get-tuple-element.115.ha, s32[16]{0:T(128)S(1)} %get-tuple-element.118.hb, f32[1024,384]{1,0:T(8,128)S(1)} %shard_map.147.raw_ref, ...), custom_call_target="tpu_custom_call" | custom-call | flops 3221225472 | bytes 8388608 | tf_op jit(solution)/shard_map/pallas_call | solution.py:253
  66.7 0.2 collective-permute-start.8
  66.9 0.0 copy-start.3
  66.9 1.1 %collective-permute-done.8.other_ref = bf16[128,256]{1,0:T(8,128)(2,1)S(1)} collective-permute-done((bf16[128,256]{1,0:T(8,128)(2,1)S(1)}, bf16[128,256]{1,0:T(8,128)(2,1)S(1)}, u32[]{:S(2)}, u32[]{:S(2)}) %collective-permute-start.8) | collective-permute-done | bytes 65568 | tf_op jit(solution)/shard_map/ppermute | solution.py:286
  68.0 0.2 shard_map.149
  68.2 1.8 %collective-permute-start.9 = (bf16[128,256]{1,0:T(8,128)(2,1)S(1)}, bf16[128,256]{1,0:T(8,128)(2,1)S(1)}, u32[]{:S(2)}, u32[]{:S(2)}) collective-permute-start(bf16[128,256]{1,0:T(8,128)(2,1)S(1)} %convert_element_type.15), channel_id=1, source_target_pairs={{0,32},{16,48},{32,0},{48,16},{64,96},{80,112},{96,64},{112,80},{1... | collective-permute-start | bytes 196616 | tf_op jit(solution)/shard_map/ppermute | solution.py:286
  70.1 2.7 %collective-permute-done.9.other_ref = bf16[128,256]{1,0:T(8,128)(2,1)S(1)} collective-permute-done((bf16[128,256]{1,0:T(8,128)(2,1)S(1)}, bf16[128,256]{1,0:T(8,128)(2,1)S(1)}, u32[]{:S(2)}, u32[]{:S(2)}) %collective-permute-start.9) | collective-permute-done | bytes 65568 | tf_op jit(solution)/shard_map/ppermute | solution.py:286
  72.8 0.2 shard_map.150
  73.0 3.1 %collective-permute-start.10 = (bf16[128,256]{1,0:T(8,128)(2,1)S(1)}, bf16[128,256]{1,0:T(8,128)(2,1)S(1)}, u32[]{:S(2)}, u32[]{:S(2)}) collective-permute-start(bf16[128,256]{1,0:T(8,128)(2,1)S(1)} %convert_element_type.16), channel_id=1, source_target_pairs={{0,96},{16,112},{32,64},{48,80},{64,32},{80,48},{96,0},{112,16},{1... | collective-permute-start | bytes 196616 | tf_op jit(solution)/shard_map/ppermute | solution.py:291
  76.1 1.5 %shard_map.151 = (bf16[1024,128]{1,0:T(8,128)(2,1)S(1)}, f32[1024,128]{1,0:T(8,128)S(1)}) custom-call(bf16[1024,128]{1,0:T(8,128)(2,1)S(1)} %get-tuple-element.102.q_ref, bf16[1024,128]{1,0:T(8,128)(2,1)S(1)} %get-tuple-element.103.k_ref, bf16[1024,256]{1,0:T(8,128)(2,1)S(1)} %get-tuple-element.104.wu_ref, bf16[8,128,256]{2,1,0:T(8,128)(2,1)S(1)} %get-tuple-element.105.states_ref), custom_call_target="tpu_custom_call" | custom-call | flops 536870912 | bytes 4194304 | tf_op jit(solution)/shard_map/pallas_call | solution.py:275
  77.6 1.0 collective-permute-done.10.other_ref
  78.5 1.2 %shard_map.152 = bf16[1024,128]{1,0:T(8,128)(2,1)} custom-call(s32[1]{0:T(128)} %bitcast.upper_ref, f32[128,256]{1,0:T(8,128)S(1)} %get-tuple-element.100.prefix_ref, bf16[128,256]{1,0:T(8,128)(2,1)S(1)} %collective-permute-done.10.other_ref, bf16[1024,128]{1,0:T(8,128)(2,1)S(1)} %get-tuple-element.106.query_ref, ...), custom_call_target="tpu_custom_call" | custom-call | flops 33554432 | bytes 2097152 | tf_op jit(solution)/shard_map/pallas_call | solution.py:293
  79.7 5.6 %all-to-all-start = ((bf16[16,64,128]{2,1,0:T(8,128)(2,1)}), bf16[16,64,128]{2,1,0:T(8,128)(2,1)S(1)}, u32[]{:S(2)}, u32[]{:S(2)}) async-start(bf16[16,64,128]{2,1,0:T(8,128)(2,1)} %bitcast.7), calls=%async_computation | async-start | bytes 524288 | tf_op jit(solution)/shard_map/all_to_all | solution.py:297
  85.3 8.7 %all-to-all-done = bf16[16,64,128]{2,1,0:T(8,128)(2,1)S(1)} async-done(((bf16[16,64,128]{2,1,0:T(8,128)(2,1)}), bf16[16,64,128]{2,1,0:T(8,128)(2,1)S(1)}, u32[]{:S(2)}, u32[]{:S(2)}) %all-to-all-start) | async-done | bytes 262176 | tf_op jit(solution)/shard_map/all_to_all | solution.py:297
  94.0 4.9 %conditional.1 = (bf16[64,2048]{1,0:T(8,128)(2,1)S(1)}) conditional(s32[]{:T(128)} %convert_element_type.13, (s32[16]{0:T(128)S(1)}, s32[16]{0:T(128)S(1)}, s32[16]{0:T(128)S(1)}, s32[16]{0:T(128)S(1)}, bf16[16,64,128]{2,1,0:T(8,128)(2,1)S(1)}, /*index=5*/bf16[8,128,512]{2,1,0:T(8,128)(2,1)}, bf16[8,128,512]{2,1,0:T(8,128)(2,1)}, ...), branch_computations={%region_0.1_spmd, %region_1.2_spmd} | conditional | flops 536870912 | bytes 9437192 | solution.py:318
  94.0 4.9 %branch_1_fun.1 = bf16[64,2048]{1,0:T(8,128)(2,1)S(1)} custom-call(s32[16]{0:T(128)S(1)} %get-tuple-element.73.h0, s32[16]{0:T(128)S(1)} %get-tuple-element.74.h1, s32[16]{0:T(128)S(1)} %get-tuple-element.75.h2, s32[16]{0:T(128)S(1)} %get-tuple-element.76.h3, bf16[16,64,128]{2,1,0:T(8,128)(2,1)S(1)} %get-tuple-element.77.x_ref, ...), custom_call_target="tpu_custom_call" | custom-call | flops 536870912 | bytes 9437184 | tf_op jit(solution)/shard_map/cond/branch_1_fun/pallas_call | solution.py:303
  98.9 0.0 copy-start.5
  98.9 0.7 copy-done.5
  (32 shorter events, 0.2 us)
Async XLA Ops:
  1.0 5.0 %collective-permute-start.3 = (bf16[1,512,128]{2,1,0:T(8,128)(2,1)S(1)}, bf16[1,512,128]{2,1,0:T(8,128)(2,1)S(1)}, u32[]{:S(2)}, u32[]{:S(2)}) collective-permute-start(bf16[1,512,128]{2,1,0:T(8,128)(2,1)S(1)} %get-tuple-element.111), channel_id=1, source_target_pairs={{0,4},{1,5},{2,6},{3,7},{4,0},{5,1},{6,2},{7,3},{8,12},{9,13},{10,... | collective-permute-start | bytes 393224 | tf_op jit(solution)/shard_map/ppermute | solution.py:29
  4.1 7.7 %collective-permute-start.11 = (bf16[1,128,512]{2,1,0:T(8,128)(2,1)S(1)}, bf16[1,128,512]{2,1,0:T(8,128)(2,1)S(1)}, u32[]{:S(2)}, u32[]{:S(2)}) collective-permute-start(bf16[1,128,512]{2,1,0:T(8,128)(2,1)S(1)} %get-tuple-element.110), channel_id=1, source_target_pairs={{0,1},{1,0},{2,3},{3,2},{4,5},{5,4},{6,7},{7,6},{8,9},{9,8},{10,11... | collective-permute-start | bytes 393224 | tf_op jit(solution)/shard_map/ppermute | solution.py:29
  6.1 10.8 %collective-permute-start.4 = (bf16[2,512,128]{2,1,0:T(8,128)(2,1)S(1)}, bf16[2,512,128]{2,1,0:T(8,128)(2,1)S(1)}, u32[]{:S(2)}, u32[]{:S(2)}) collective-permute-start(bf16[2,512,128]{2,1,0:T(8,128)(2,1)S(1)} %pad_maximum_fusion.9), channel_id=1, source_target_pairs={{0,12},{1,13},{2,14},{3,15},{4,8},{5,9},{6,10},{7,11},{8,4},{9,5},... | collective-permute-start | bytes 786440 | tf_op jit(solution)/shard_map/ppermute | solution.py:29
  10.3 5.0 %collective-permute-start.17 = (bf16[1,128,512]{2,1,0:T(8,128)(2,1)S(1)}, bf16[1,128,512]{2,1,0:T(8,128)(2,1)S(1)}, u32[]{:S(2)}, u32[]{:S(2)}) collective-permute-start(bf16[1,128,512]{2,1,0:T(8,128)(2,1)S(1)} %get-tuple-element.109), channel_id=1, source_target_pairs={{0,4},{1,5},{2,6},{3,7},{4,0},{5,1},{6,2},{7,3},{8,12},{9,13},{10,... | collective-permute-start | bytes 393224 | tf_op jit(solution)/shard_map/ppermute | solution.py:29
  10.3 8.2 %collective-permute-start = (bf16[1,512,128]{2,1,0:T(8,128)(2,1)S(1)}, bf16[1,512,128]{2,1,0:T(8,128)(2,1)S(1)}, u32[]{:S(2)}, u32[]{:S(2)}) collective-permute-start(bf16[1,512,128]{2,1,0:T(8,128)(2,1)S(1)} %get-tuple-element.112), channel_id=1, source_target_pairs={{0,1},{1,0},{2,3},{3,2},{4,5},{5,4},{6,7},{7,6},{8,9},{9,8},{10,11... | collective-permute-start | bytes 393224 | tf_op jit(solution)/shard_map/ppermute | solution.py:29
  11.8 8.9 %collective-permute-start.12 = (bf16[2,128,512]{2,1,0:T(8,128)(2,1)S(1)}, bf16[2,128,512]{2,1,0:T(8,128)(2,1)S(1)}, u32[]{:S(2)}, u32[]{:S(2)}) collective-permute-start(bf16[2,128,512]{2,1,0:T(8,128)(2,1)S(1)} %pad_maximum_fusion.10), channel_id=1, source_target_pairs={{0,3},{1,2},{2,1},{3,0},{4,7},{5,6},{6,5},{7,4},{8,11},{9,10},{10,... | collective-permute-start | bytes 786440 | tf_op jit(solution)/shard_map/ppermute | solution.py:29
  15.3 8.4 %collective-permute-start.18 = (bf16[2,128,512]{2,1,0:T(8,128)(2,1)S(1)}, bf16[2,128,512]{2,1,0:T(8,128)(2,1)S(1)}, u32[]{:S(2)}, u32[]{:S(2)}) collective-permute-start(bf16[2,128,512]{2,1,0:T(8,128)(2,1)S(1)} %pad_maximum_fusion.11), channel_id=1, source_target_pairs={{0,12},{1,13},{2,14},{3,15},{4,8},{5,9},{6,10},{7,11},{8,4},{9,5},... | collective-permute-start | bytes 786440 | tf_op jit(solution)/shard_map/ppermute | solution.py:29
  16.9 12.3 %collective-permute-start.5 = (bf16[4,512,128]{2,1,0:T(8,128)(2,1)S(1)}, bf16[4,512,128]{2,1,0:T(8,128)(2,1)S(1)}, u32[]{:S(2)}, u32[]{:S(2)}) collective-permute-start(bf16[4,512,128]{2,1,0:T(8,128)(2,1)S(1)} %pad_maximum_fusion.5), channel_id=1, source_target_pairs={{0,1},{1,0},{2,3},{3,2},{4,5},{5,4},{6,7},{7,6},{8,9},{9,8},{10,11... | collective-permute-start | bytes 1572872 | tf_op jit(solution)/shard_map/ppermute | solution.py:29
  18.5 10.5 %collective-permute-start.1 = (bf16[2,512,128]{2,1,0:T(8,128)(2,1)S(1)}, bf16[2,512,128]{2,1,0:T(8,128)(2,1)S(1)}, u32[]{:S(2)}, u32[]{:S(2)}) collective-permute-start(bf16[2,512,128]{2,1,0:T(8,128)(2,1)S(1)} %pad_maximum_fusion.8), channel_id=1, source_target_pairs={{0,3},{1,2},{2,1},{3,0},{4,7},{5,6},{6,5},{7,4},{8,11},{9,10},{10,... | collective-permute-start | bytes 786440 | tf_op jit(solution)/shard_map/ppermute | solution.py:29
  20.8 11.0 %collective-permute-start.13 = (bf16[4,128,512]{2,1,0:T(8,128)(2,1)S(1)}, bf16[4,128,512]{2,1,0:T(8,128)(2,1)S(1)}, u32[]{:S(2)}, u32[]{:S(2)}) collective-permute-start(bf16[4,128,512]{2,1,0:T(8,128)(2,1)S(1)} %pad_maximum_fusion.6), channel_id=1, source_target_pairs={{0,4},{1,5},{2,6},{3,7},{4,0},{5,1},{6,2},{7,3},{8,12},{9,13},{10,... | collective-permute-start | bytes 1572872 | tf_op jit(solution)/shard_map/ppermute | solution.py:29
  23.7 13.6 %collective-permute-start.19 = (bf16[4,128,512]{2,1,0:T(8,128)(2,1)S(1)}, bf16[4,128,512]{2,1,0:T(8,128)(2,1)S(1)}, u32[]{:S(2)}, u32[]{:S(2)}) collective-permute-start(bf16[4,128,512]{2,1,0:T(8,128)(2,1)S(1)} %pad_maximum_fusion.7), channel_id=1, source_target_pairs={{0,1},{1,0},{2,3},{3,2},{4,5},{5,4},{6,7},{7,6},{8,9},{9,8},{10,11... | collective-permute-start | bytes 1572872 | tf_op jit(solution)/shard_map/ppermute | solution.py:29
  29.1 14.9 %collective-permute-start.2 = (bf16[4,512,128]{2,1,0:T(8,128)(2,1)S(1)}, bf16[4,512,128]{2,1,0:T(8,128)(2,1)S(1)}, u32[]{:S(2)}, u32[]{:S(2)}) collective-permute-start(bf16[4,512,128]{2,1,0:T(8,128)(2,1)S(1)} %pad_maximum_fusion.4), channel_id=1, source_target_pairs={{0,4},{1,5},{2,6},{3,7},{4,0},{5,1},{6,2},{7,3},{8,12},{9,13},{10,... | collective-permute-start | bytes 1572872 | tf_op jit(solution)/shard_map/ppermute | solution.py:29
  29.3 16.6 %collective-permute-start.7 = (bf16[8,512,128]{2,1,0:T(8,128)(2,1)S(1)}, bf16[8,512,128]{2,1,0:T(8,128)(2,1)}, u32[]{:S(2)}, u32[]{:S(2)}) collective-permute-start(bf16[8,512,128]{2,1,0:T(8,128)(2,1)S(1)} %pad_maximum_fusion.1.b_ref), channel_id=1, source_target_pairs={{0,3},{1,2},{2,1},{3,0},{4,7},{5,6},{6,5},{7,4},{8,11},{9,10},{10,... | collective-permute-start | bytes 3145736 | tf_op jit(solution)/shard_map/ppermute | solution.py:29
  32.9 16.3 %collective-permute-start.15 = (bf16[8,128,512]{2,1,0:T(8,128)(2,1)}, bf16[8,128,512]{2,1,0:T(8,128)(2,1)}, u32[]{:S(2)}, u32[]{:S(2)}) collective-permute-start(bf16[8,128,512]{2,1,0:T(8,128)(2,1)} %pad_maximum_fusion.2), channel_id=1, source_target_pairs={{0,12},{1,13},{2,14},{3,15},{4,8},{5,9},{6,10},{7,11},{8,4},{9,5},... | collective-permute-start | bytes 3145736 | tf_op jit(solution)/shard_map/ppermute | solution.py:29
  38.4 18.4 %copy-start.6 = (s32[16]{0:T(128)S(1)}, s32[16]{0:T(128)}, u32[]{:S(2)}) copy-start(s32[16]{0:T(128)} %constant.81.clone) | copy-start | bytes 196
  38.4 18.4 %copy-start.7 = (s32[16]{0:T(128)S(1)}, s32[16]{0:T(128)}, u32[]{:S(2)}) copy-start(s32[16]{0:T(128)} %constant.82.clone) | copy-start | bytes 196
  38.4 18.4 %copy-start.8 = (s32[16]{0:T(128)S(1)}, s32[16]{0:T(128)}, u32[]{:S(2)}) copy-start(s32[16]{0:T(128)} %constant.83.clone) | copy-start | bytes 196
  38.5 18.4 %copy-start.9 = (s32[16]{0:T(128)S(1)}, s32[16]{0:T(128)}, u32[]{:S(2)}) copy-start(s32[16]{0:T(128)} %constant.84.clone) | copy-start | bytes 196
  38.5 18.5 %copy-start = (bf16[2048,128]{1,0:T(8,128)(2,1)S(1)}, bf16[2048,128]{1,0:T(8,128)(2,1)}, u32[]{:S(2)}) copy-start(bf16[2048,128]{1,0:T(8,128)(2,1)} %wq.3) | copy-start | bytes 1572868
  38.5 18.5 %copy-start.1 = (bf16[2048,128]{1,0:T(8,128)(2,1)S(1)}, bf16[2048,128]{1,0:T(8,128)(2,1)}, u32[]{:S(2)}) copy-start(bf16[2048,128]{1,0:T(8,128)(2,1)} %wk.3) | copy-start | bytes 1572868
  38.5 18.3 %collective-permute-start.21 = (bf16[8,128,512]{2,1,0:T(8,128)(2,1)}, bf16[8,128,512]{2,1,0:T(8,128)(2,1)}, u32[]{:S(2)}, u32[]{:S(2)}) collective-permute-start(bf16[8,128,512]{2,1,0:T(8,128)(2,1)} %pad_maximum_fusion.3), channel_id=1, source_target_pairs={{0,3},{1,2},{2,1},{3,0},{4,7},{5,6},{6,5},{7,4},{8,11},{9,10},{10,... | collective-permute-start | bytes 3145736 | tf_op jit(solution)/shard_map/ppermute | solution.py:29
  44.1 16.4 %collective-permute-start.6 = (bf16[8,512,128]{2,1,0:T(8,128)(2,1)S(1)}, bf16[8,512,128]{2,1,0:T(8,128)(2,1)}, u32[]{:S(2)}, u32[]{:S(2)}) collective-permute-start(bf16[8,512,128]{2,1,0:T(8,128)(2,1)S(1)} %pad_maximum_fusion.a_ref), channel_id=1, source_target_pairs={{0,12},{1,13},{2,14},{3,15},{4,8},{5,9},{6,10},{7,11},{8,4},{9,5},... | collective-permute-start | bytes 3145736 | tf_op jit(solution)/shard_map/ppermute | solution.py:29
  45.8 39.5 %collective-permute-start.14 = (bf16[8,128,512]{2,1,0:T(8,128)(2,1)}, bf16[8,128,512]{2,1,0:T(8,128)(2,1)}, u32[]{:S(2)}, u32[]{:S(2)}) collective-permute-start(bf16[8,128,512]{2,1,0:T(8,128)(2,1)} %pad_maximum_fusion.2), channel_id=1, source_target_pairs={{0,16},{16,0},{32,48},{48,32},{64,80},{80,64},{96,112},{112,96},{1... | collective-permute-start | bytes 3145736 | tf_op jit(solution)/shard_map/ppermute | solution.py:272
  45.9 39.4 %collective-permute-start.20 = (bf16[8,128,512]{2,1,0:T(8,128)(2,1)}, bf16[8,128,512]{2,1,0:T(8,128)(2,1)}, u32[]{:S(2)}, u32[]{:S(2)}) collective-permute-start(bf16[8,128,512]{2,1,0:T(8,128)(2,1)} %pad_maximum_fusion.3), channel_id=1, source_target_pairs={{0,16},{16,0},{32,48},{48,32},{64,80},{80,64},{96,112},{112,96},{1... | collective-permute-start | bytes 3145736 | tf_op jit(solution)/shard_map/ppermute | solution.py:272
  49.2 44.8 %collective-permute-start.16 = (bf16[8,128,512]{2,1,0:T(8,128)(2,1)}, bf16[8,128,512]{2,1,0:T(8,128)(2,1)}, u32[]{:S(2)}, u32[]{:S(2)}) collective-permute-start(bf16[8,128,512]{2,1,0:T(8,128)(2,1)} %collective-permute-done.15), channel_id=1, source_target_pairs={{0,16},{16,0},{32,48},{48,32},{64,80},{80,64},{96,112},{112,96},{1... | collective-permute-start | bytes 3145736 | tf_op jit(solution)/shard_map/ppermute | solution.py:272
  56.8 37.2 %collective-permute-start.22 = (bf16[8,128,512]{2,1,0:T(8,128)(2,1)}, bf16[8,128,512]{2,1,0:T(8,128)(2,1)}, u32[]{:S(2)}, u32[]{:S(2)}) collective-permute-start(bf16[8,128,512]{2,1,0:T(8,128)(2,1)} %collective-permute-done.21), channel_id=1, source_target_pairs={{0,16},{16,0},{32,48},{48,32},{64,80},{80,64},{96,112},{112,96},{1... | collective-permute-start | bytes 3145736 | tf_op jit(solution)/shard_map/ppermute | solution.py:272
  56.9 1.0 %copy-start.2 = (bf16[2048,128]{1,0:T(8,128)(2,1)S(1)}, bf16[2048,128]{1,0:T(8,128)(2,1)}, u32[]{:S(2)}) copy-start(bf16[2048,128]{1,0:T(8,128)(2,1)} %wv.3) | copy-start | bytes 1572868
  58.0 2.5 %copy-start.4 = (f32[1024,1]{0,1:T(1,128)S(1)}, f32[1024,1]{0,1:T(1,128)}, u32[]{:S(2)}) copy-start(f32[1024,1]{0,1:T(1,128)} %param.18) | copy-start | bytes 12292
  66.7 1.3 %collective-permute-start.8 = (bf16[128,256]{1,0:T(8,128)(2,1)S(1)}, bf16[128,256]{1,0:T(8,128)(2,1)S(1)}, u32[]{:S(2)}, u32[]{:S(2)}) collective-permute-start(bf16[128,256]{1,0:T(8,128)(2,1)S(1)} %convert_element_type.14), channel_id=1, source_target_pairs={{0,16},{16,0},{32,48},{48,32},{64,80},{80,64},{96,112},{112,96},{1... | collective-permute-start | bytes 196616 | tf_op jit(solution)/shard_map/ppermute | solution.py:286
  66.9 11.6 %copy-start.3 = (f32[128]{0:T(128)S(1)}, f32[128]{0:T(128)}, u32[]{:S(2)}) copy-start(f32[128]{0:T(128)} %param.22) | copy-start | bytes 1540
  68.2 4.5 %collective-permute-start.9 = (bf16[128,256]{1,0:T(8,128)(2,1)S(1)}, bf16[128,256]{1,0:T(8,128)(2,1)S(1)}, u32[]{:S(2)}, u32[]{:S(2)}) collective-permute-start(bf16[128,256]{1,0:T(8,128)(2,1)S(1)} %convert_element_type.15), channel_id=1, source_target_pairs={{0,32},{16,48},{32,0},{48,16},{64,96},{80,112},{96,64},{112,80},{1... | collective-permute-start | bytes 196616 | tf_op jit(solution)/shard_map/ppermute | solution.py:286
  73.0 5.6 %collective-permute-start.10 = (bf16[128,256]{1,0:T(8,128)(2,1)S(1)}, bf16[128,256]{1,0:T(8,128)(2,1)S(1)}, u32[]{:S(2)}, u32[]{:S(2)}) collective-permute-start(bf16[128,256]{1,0:T(8,128)(2,1)S(1)} %convert_element_type.16), channel_id=1, source_target_pairs={{0,96},{16,112},{32,64},{48,80},{64,32},{80,48},{96,0},{112,16},{1... | collective-permute-start | bytes 196616 | tf_op jit(solution)/shard_map/ppermute | solution.py:291
  79.7 14.3 %all-to-all-start = ((bf16[16,64,128]{2,1,0:T(8,128)(2,1)}), bf16[16,64,128]{2,1,0:T(8,128)(2,1)S(1)}, u32[]{:S(2)}, u32[]{:S(2)}) async-start(bf16[16,64,128]{2,1,0:T(8,128)(2,1)} %bitcast.7), calls=%async_computation | async-start | bytes 524288 | tf_op jit(solution)/shard_map/all_to_all | solution.py:297
  98.9 0.7 copy-start.5

commit v2 on v1

v2 whole, which is shorter than its diff:
```python
import jax
import jax.numpy as jnp
from jax import lax
from jax.experimental import pallas as pl
from jax.experimental.pallas import tpu as pltpu
from jax.sharding import PartitionSpec as P

DK = 128
CHUNK = 128
F32 = jnp.float32
BF16 = jnp.bfloat16
VMEM = pl.BlockSpec(memory_space=pltpu.VMEM)
LIMIT = 14 << 20


def dot(left, right, contract=((1,), (0,))):
    return lax.dot_general(
        left.astype(BF16), right.astype(BF16), (contract, ((), ())), preferred_element_type=F32
    )


ALONG_X = ((1, 3), (3, 1))
ALONG_Z = ((4, 12), (12, 4))


OPPOSITE = (12, 4)


def flipped(masks):
    return tuple((odd, even) for even, odd in masks)


STREAMS = (
    ALONG_X + ALONG_Z,
    ALONG_Z + ALONG_X,
    flipped(ALONG_X + ALONG_Z),
    flipped(ALONG_Z + ALONG_X),
)


def swap(value, masks, ctx, heads):
    pairs = [
        (c * heads + h, c * heads + (h ^ masks[c % 2])) for c in range(ctx) for h in range(heads)
    ]
    return lax.ppermute(value, ("ctx", "head"), pairs)


def offsets(masks, core):
    order = [0]
    for step in masks:
        order = order + [o ^ step[core] for o in order]
    return order


class Place:
    def __init__(self):
        ctx, head = lax.axis_index("ctx"), lax.axis_index("head")
        self.core, self.y = lax.rem(ctx, 2), lax.div(ctx, 2)
        self.head, self.z, self.x = head, lax.div(head, 4), lax.rem(head, 4)
        self.first_core = self.core == 0

    def by_core(self, first, second):
        return jnp.where(self.first_core, first, second)

    def piece_heads(self, masks):
        return [self.head ^ self.by_core(a, b) for a, b in zip(offsets(masks, 0), offsets(masks, 1))]


def pack_kernel(tokens_ref, w_ref, p0, p1, p2, p3, sems):
    place = Place()
    quarter = place.core * 2 + lax.rem(place.y, 2)
    copies = []
    for stream, out in enumerate((p0, p1, p2, p3)):
        for i in range(2):
            start = (2 * stream + i) * DK
            copies.append(
                (tokens_ref.at[start : start + DK, :], out.at[0, :, i * DK : (i + 1) * DK])
            )
    for i in range(2):
        start = pl.multiple_of(quarter * 512 + i * 256, 256)
        copies.append((w_ref.at[:, pl.ds(start, 256)], p0.at[1 + i]))
    started = []
    for n, (source, target) in enumerate(copies):
        copy = pltpu.make_async_copy(source, target, sems.at[n])
        copy.start()
        started.append(copy)
    for copy in started:
        copy.wait()


def join_kernel(*refs):
    out_ref, at = refs[-1], 0
    for ref in refs[:-1]:
        out_ref[at : at + ref.shape[0]] = ref[...]
        at += ref.shape[0]


def split_kernel(one_ref, two_ref, tokens_ref, w_ref):
    for i in range(4):
        source, at = (one_ref, two_ref)[i // 2], 3 * (i % 2)
        tokens_ref[i] = source[at]
        w_ref[2 * i] = source[at + 1]
        w_ref[2 * i + 1] = source[at + 2]


def project_part(heads, pieces_ref, weights):
    total = None
    for p in range(0, 8, 2):
        left = jnp.concatenate(
            [
                jnp.concatenate(
                    [pieces_ref[q, :, i * DK : (i + 1) * DK] for q in (p, p + 1)], axis=1
                )
                for i in range(2)
            ],
            axis=0,
        )
        rows = []
        for q in (p, p + 1):
            start = pl.multiple_of(heads[q] * DK, DK)
            rows.append(jnp.concatenate([w[pl.ds(start, DK), :] for w in weights], axis=1))
        term = jnp.dot(left, jnp.concatenate(rows, axis=0), preferred_element_type=F32)
        total = term if total is None else total + term
    return total


def first_half_kernel(t0, t1, t2, t3, wq, wk, wv, raw_ref):
    place = Place()
    for i, pieces in enumerate((t0, t1, t2, t3)):
        heads = place.piece_heads(STREAMS[i])[:8]
        raw_ref[i * 256 : (i + 1) * 256, :] = project_part(heads, pieces, (wq, wk, wv))


def unit_silu(raw):
    act = raw / (1.0 + jnp.exp(jnp.minimum(-raw, 80.0)))
    return act * lax.rsqrt(jnp.sum(act * act, axis=-1, keepdims=True) + 1e-6)


def transition_kernel(
    raw_ref, t0, t1, t2, t3, wq, wk, wv, beta_ref,
    q_ref, k_ref, wu_ref, states_ref, last_ref, sent_ref, total_ref,
):
    rows = raw_ref.shape[0]
    count = rows // CHUNK
    place = Place()
    for i, pieces in enumerate((t0, t1, t2, t3)):
        part = slice(i * 256, (i + 1) * 256)
        heads = place.piece_heads(STREAMS[i])[8:]
        total_ref[part, :] = raw_ref[part, :] + project_part(heads, pieces, (wq, wk, wv))
    row = lax.broadcasted_iota(jnp.int32, (CHUNK, CHUNK), 0)
    col = lax.broadcasted_iota(jnp.int32, (CHUNK, CHUNK), 1)
    eye = (row == col).astype(F32)

    def below(size):
        return (row // (2 * size) == col // (2 * size)) & (
            (row // size) % 2 == 1
        ) & ((col // size) % 2 == 0)

    keys, rates, lowers, inverses = [], [], [], []
    for b in range(count):
        part = slice(b * CHUNK, (b + 1) * CHUNK)
        q_ref[part, :] = unit_silu(total_ref[part, :DK]).astype(BF16)
        key = unit_silu(total_ref[part, DK : 2 * DK])
        key16 = key.astype(BF16)
        k_ref[part, :] = key16
        rate = jnp.transpose(jnp.broadcast_to(beta_ref[b : b + 1, :], (CHUNK, CHUNK)))
        gram = dot(key16, key16, ((1,), (1,)))
        lower = jnp.where(row > col, rate * gram, 0.0)
        keys.append(key)
        rates.append(rate)
        lowers.append(lower)
        inverses.append(eye - jnp.where(below(1), lower, 0.0))
    size = 2
    while size < CHUNK:
        mask = below(size)
        inner = [dot(jnp.where(mask, lo, 0.0), inv) for lo, inv in zip(lowers, inverses)]
        inverses = [inv - dot(inv, x) for inv, x in zip(inverses, inner)]
        size *= 2
    maps = []
    for b in range(count):
        part = slice(b * CHUNK, (b + 1) * CHUNK)
        value = total_ref[part, 2 * DK :]
        both = jnp.concatenate([rates[b] * keys[b], rates[b] * value], axis=1)
        wu = dot(inverses[b], both).astype(BF16)
        wu_ref[part, :] = wu
        maps.append(dot(k_ref[part, :], wu, ((0,), (0,))))
    zeros = jnp.zeros((DK, DK), F32)
    state = jnp.concatenate([eye, zeros], axis=1)
    for b in range(count):
        state16 = state.astype(BF16)
        states_ref[b] = state16
        state = (
            state
            - dot(maps[b][:, :DK], state16)
            + jnp.concatenate([zeros, maps[b][:, DK:]], axis=1)
        )
    last_ref[...] = state
    sent_ref[...] = state.astype(BF16)


def outputs_kernel(q_ref, k_ref, wu_ref, states_ref, query_ref, out_ref):
    rows = q_ref.shape[0]
    row = lax.broadcasted_iota(jnp.int32, (CHUNK, CHUNK), 0)
    col = lax.broadcasted_iota(jnp.int32, (CHUNK, CHUNK), 1)
    for b in range(rows // CHUNK):
        part = slice(b * CHUNK, (b + 1) * CHUNK)
        query = q_ref[part, :]
        scores = jnp.where(row >= col, dot(query, k_ref[part, :], ((1,), (1,))), 0.0)
        local = dot(scores, wu_ref[part, :])
        effective = query.astype(F32) - local[:, :DK]
        result = dot(effective, states_ref[b])
        query_ref[part, :] = result[:, :DK].astype(BF16)
        out_ref[part, :] = result[:, DK:] + local[:, DK:]


def compose(later, earlier):
    return dot(later[:, :DK], earlier) + jnp.concatenate(
        [jnp.zeros((DK, DK), F32), later[:, DK:]], axis=1
    )


def chip_kernel(mine_ref, other_ref, chip_ref):
    mine, other = mine_ref[...], other_ref[...].astype(F32)
    second = Place().core == 1
    chip_ref[...] = compose(
        jnp.where(second, mine, other), jnp.where(second, other, mine)
    ).astype(BF16)


def finish_kernel(
    third_ref, second_ref, first_ref, other_ref, query_ref, out_ref, gain_ref, normed_ref
):
    place = Place()
    entering = third_ref[:, DK:].astype(F32)
    for earlier in (second_ref, first_ref):
        entering = dot(earlier[:, :DK], entering) + earlier[:, DK:].astype(F32)
    after_other = dot(other_ref[:, :DK], entering) + other_ref[:, DK:].astype(F32)
    entering = jnp.where(place.core == 1, after_other, entering)
    recurrent = out_ref[...] + dot(query_ref[...], entering)
    scale = lax.rsqrt(jnp.mean(recurrent * recurrent, axis=-1, keepdims=True) + 1e-5)
    normed = (recurrent * scale * gain_ref[...]).astype(BF16)
    for b in range(16):
        z, x = b // 4, b % 4
        inside = place.by_core(
            lax.div(place.z, 2) == z // 2, (place.z == z) | (place.z == 3 - z)
        )
        seat = place.by_core(jnp.where(inside, z % 2, 1 - z % 2), z // 2)
        slot = (seat * 4 + x) * 2 + jnp.where(inside, 0, 1)
        start = pl.multiple_of(slot * 64, 64)
        normed_ref[pl.ds(start, 64), :] = normed[b * 64 : (b + 1) * 64, :]


def mix_rows(x_ref, near_ref, far_ref, rows, out_ref, dtype):
    place = Place()
    seat = place.by_core(lax.rem(place.z, 2), lax.div(place.z, 2))
    along_x = [offsets(STREAMS[0][:2], core) for core in range(2)]
    even = lax.rem(place.y, 2)
    for side in range(2):
        core = place.core if side == 0 else 1 - place.core
        order = [
            place.x ^ place.by_core(along_x[side][j], along_x[1 - side][j]) for j in range(4)
        ]
        lefts = {}
        for group in range(2):
            base = (seat if group == 0 else 1 - seat) * 4
            for j in (0, 2):
                lefts[group, j] = jnp.concatenate(
                    [x_ref[base + order[j], rows, :], x_ref[base + order[j + 1], rows, :]], axis=1
                )
        for quarter in range(2):
            column = (core * 2 + (even if quarter == 0 else 1 - even)) * 512
            for slab in range(2):
                total = None
                for group, ref in enumerate((near_ref, far_ref)):
                    at = side * 16 + quarter * 8 + slab
                    for j in (0, 2):
                        right = jnp.concatenate([ref[at + 2 * j], ref[at + 2 * j + 2]], axis=0)
                        term = jnp.dot(lefts[group, j], right, preferred_element_type=F32)
                        total = term if total is None else total + term
                start = pl.multiple_of(column + slab * 256, 256)
                out_ref[:, pl.ds(start, 256)] = total.astype(dtype)


def mix_partner_kernel(x_ref, near_ref, far_ref, out_ref):
    mix_rows(x_ref, near_ref, far_ref, slice(64, 128), out_ref, BF16)


def mix_own_kernel(x_ref, near_ref, far_ref, out_ref):
    mix_rows(x_ref, near_ref, far_ref, slice(0, 64), out_ref, F32)


def sum_kernel(own_ref, other_ref, mixed_ref):
    mixed_ref[...] = (own_ref[...] + other_ref[...].astype(F32)).astype(BF16)


def call(kernel, shapes, n_vmem, scratch=(), flops=0, size=0):
    return pl.pallas_call(
        kernel,
        out_shape=shapes,
        in_specs=[VMEM] * n_vmem,
        out_specs=jax.tree.map(lambda _: VMEM, shapes),
        scratch_shapes=list(scratch),
        compiler_params=pltpu.CompilerParams(vmem_limit_bytes=LIMIT),
        cost_estimate=pl.CostEstimate(flops=flops, bytes_accessed=size, transcendentals=0),
    )


def struct(shape, dtype):
    return jax.ShapeDtypeStruct(shape, dtype)


def join(*parts):
    shape = (sum(p.shape[0] for p in parts),) + parts[0].shape[1:]
    return call(join_kernel, struct(shape, BF16), len(parts), size=1 << 20)(*parts)


def local(tokens, beta, w_query, w_key, w_value, gain, w_out):
    ctx, heads = lax.axis_size("ctx"), lax.axis_size("head")
    rows = tokens.shape[0]
    weights = (w_query, w_key, w_value)

    slab = (DK, 2 * DK)
    pieces = pl.pallas_call(
        pack_kernel,
        out_shape=tuple(struct((n,) + slab, BF16) for n in (3, 1, 1, 1)),
        in_specs=[pl.BlockSpec(memory_space=pltpu.HBM)] * 2,
        out_specs=(VMEM,) * 4,
        scratch_shapes=[pltpu.SemaphoreType.DMA((10,))],
        compiler_params=pltpu.CompilerParams(vmem_limit_bytes=LIMIT),
    )(tokens, w_out)
    arrived = [swap(p, masks[0], ctx, heads) for p, masks in zip(pieces, STREAMS)]
    arrived = lax.optimization_barrier(arrived)
    pieces = [join(p, n) for p, n in zip(pieces, arrived)]
    arrived = [swap(p, masks[1], ctx, heads) for p, masks in zip(pieces, STREAMS)]
    arrived = lax.optimization_barrier(arrived)
    first, w = call(
        split_kernel, (struct((4,) + slab, BF16), struct((8,) + slab, BF16)), 2, size=2 << 20
    )(pieces[0], arrived[0])
    pieces = [first] + [join(p, n) for p, n in zip(pieces[1:], arrived[1:])]
    w_next = lax.ppermute(w, "ctx", [(c, c ^ 2) for c in range(ctx)])
    arrived = [swap(p, masks[2], ctx, heads) for p, masks in zip(pieces, STREAMS)]
    *arrived, w_next = lax.optimization_barrier((*arrived, w_next))
    w = join(w, w_next)
    other_core = [(c, c ^ 1) for c in range(ctx)]
    pieces = [join(p, n) for p, n in zip(pieces, arrived)]
    arrived = [swap(p, masks[3], ctx, heads) for p, masks in zip(pieces, STREAMS)]
    raw = call(
        first_half_kernel, struct((rows, 3 * DK), F32), 7, flops=rows * 1024 * 768, size=5 << 20
    )(*pieces, *weights)
    w_next = lax.ppermute(w, "ctx", other_core)
    *arrived, w_next, raw = lax.optimization_barrier((*arrived, w_next, raw))
    near = join(w, w_next)
    far = swap(near, (4, 12), ctx, heads)

    query, key, wu, states, last, sent = call(
        transition_kernel,
        (
            struct((rows, DK), BF16),
            struct((rows, DK), BF16),
            struct((rows, 2 * DK), BF16),
            struct((rows // CHUNK, DK, 2 * DK), BF16),
            struct((DK, 2 * DK), F32),
            struct((DK, 2 * DK), BF16),
        ),
        9,
        scratch=[pltpu.VMEM((rows, 3 * DK), F32)],
        flops=rows * 4096 * 768, size=8 << 20,
    )(raw, *arrived, *weights, beta.reshape(rows // CHUNK, CHUNK))
    eff_query, partial = call(
        outputs_kernel,
        (struct((rows, DK), BF16), struct((rows, DK), F32)),
        4,
        flops=rows * 2048 * 256, size=4 << 20,
    )(query, key, wu, states)

    other = lax.ppermute(sent, "ctx", other_core)
    other, eff_query, partial = lax.optimization_barrier((other, eff_query, partial))
    chip = call(
        chip_kernel, struct((DK, 2 * DK), BF16), 2, flops=1 << 23, size=1 << 18
    )(last, other)
    one, two, three = [
        lax.ppermute(chip, "ctx", [(c, c + 2 * k) for c in range(ctx - 2 * k)])
        for k in (1, 2, 3)
    ]

    normed = call(
        finish_kernel, struct((rows, DK), BF16), 7, flops=rows * 128 * 256, size=2 << 20
    )(three, two, one, other, eff_query, partial, gain[None, :])
    pairs = (((0, 1), (2, 3)), ((0, 3), (1, 2)))
    groups = [
        [c * heads + z * 4 + x for z in pair for x in range(4)]
        for c in range(ctx)
        for pair in pairs[c % 2]
    ]
    spread_rows = lax.all_to_all(
        normed, ("ctx", "head"), 0, 0, tiled=True, axis_index_groups=groups
    ).reshape(8, 2 * rows // heads, DK)

    operands = (spread_rows, near, far)
    leaving = call(
        mix_partner_kernel, struct((64, 2048), BF16), 3, flops=64 * 2048 * 2048, size=4 << 20
    )(*operands)
    entering = swap(leaving, OPPOSITE, ctx, heads)
    own = call(
        mix_own_kernel, struct((64, 2048), F32), 3, flops=64 * 2048 * 2048, size=4 << 20
    )(*operands)
    return call(sum_kernel, struct((64, 2048), BF16), 2, size=1 << 20)(own, entering)


def solution(mesh):
    placed = (
        P("ctx", "head"),
        P("ctx", "head"),
        P(None, "head"),
        P(None, "head"),
        P(None, "head"),
        P(),
        P("head", None),
    )
    return jax.shard_map(
        local, mesh=mesh, in_specs=placed, out_specs=P(("ctx", "head"), None), check_vma=False
    )
```

time: 99.9 us -> 93.1 us (0.932)
  blocking collectives: 0 us -> 11.6 us
  starting transfers between devices: 40.7 us -> 33.3 us
  Pallas kernels: 15.9 us -> 11.5 us
  other arithmetic: 2.77 us -> 0 us
  waiting for transfers between devices: 36.1 us -> 33.6 us
  local copies, waits for them, and re-layouts: 3.74 us -> 2.02 us
    all_to_all x0 -> x1, blocking collectives: none -> 11.6 us  [local(): lax.all_to_all(normed, ('ctx', 'head'), 0, 0, tiled=True, axis_index_grou...]
    ppermute x16 -> x18, waiting for transfers between devices: 22.7 us -> 31.7 us  [swap(): return lax.ppermute(value, ('ctx', 'head'), pairs)]
    all_to_all x1 -> x0, waiting for transfers between devices: 8.67 us -> none  [local(): lax.all_to_all(normed, 'head', 0, 0, tiled=True)]
    ppermute x16 -> x18, starting transfers between devices: 28.9 us -> 22.5 us  [swap(): return lax.ppermute(value, ('ctx', 'head'), pairs)]
    all_to_all x1 -> x0, starting transfers between devices: 5.55 us -> none  [local(): lax.all_to_all(normed, 'head', 0, 0, tiled=True)]
    ppermute x7 -> x6, starting transfers between devices: 6.24 us -> 10.8 us  [the longest x3 8.75 us: local(): lax.ppermute(chip, 'ctx', [(c, c + 2 * k) for c in range(ctx - 2 * k)])]
    pallas_call x5 -> x21, Pallas kernels: 8.22 us -> 5.33 us  [the longest x1 1.26 us: local(): call(first_half_kernel, struct((rows, 3 * DK), F32), 7, flops=rows * 1024...]
    ppermute x7 -> x6, waiting for transfers between devices: 4.77 us -> 1.88 us  [the longest x3 1.88 us: local(): lax.ppermute(chip, 'ctx', [(c, c + 2 * k) for c in range(ctx - 2 * k)])]
  transfers between devices with their start and end apart: 24 -> 24, of which waited for: 13 -> 17; matrix products, arithmetic and copies ran while one was open for 4% -> 0% of each run, Pallas kernels for 11% -> 10%
where the time goes in v2:
time: 93.1 us; the launch traced here: 92.3 us
  waiting for transfers between devices  33.6 us (36%)
  starting transfers between devices  33.3 us (36%)
  blocking collectives  11.6 us (12%)
  Pallas kernels  11.5 us (12%)
  local copies, waits for them, and re-layouts  2.02 us (2%)
    ppermute x18, waiting for transfers between devices, swap(): return lax.ppermute(value, ('ctx', 'head'), pairs)  31.7 us
    ppermute x18, starting transfers between devices, swap(): return lax.ppermute(value, ('ctx', 'head'), pairs)  22.5 us
    all_to_all x1, blocking collectives, local(): lax.all_to_all(normed, ('ctx', 'head'), 0, 0, tiled=True, axis_index_grou...  11.6 us
    ppermute x3, starting transfers between devices, local(): lax.ppermute(chip, 'ctx', [(c, c + 2 * k) for c in range(ctx - 2 * k)])  8.75 us
    pallas_call x1, Pallas kernels, local(): call(transition_kernel, (struct((rows, DK), BF16), struct((rows, DK), BF1...  4.69 us
    unnamed x14, local copies, waits for them, and re-layouts  2.02 us
    ppermute x3, waiting for transfers between devices, local(): lax.ppermute(chip, 'ctx', [(c, c + 2 * k) for c in range(ctx - 2 * k)])  1.88 us
  transfers between devices with their start and end apart: 24, of which 17 were waited for; matrix products, arithmetic and copies ran while one was open for 0% of the time, Pallas kernels for 10%

profile of v2, /device:TPU:0, one launch (start us, length us, event | category | flops | bytes accessed | tf_op | source)
XLA Modules:
  0.0 92.3 jit_solution(11886409093882617350)
XLA Ops:
  0.0 1.0 %copy-done.3 = bf16[128,2048]{1,0:T(8,128)(2,1)S(1)} copy-done((bf16[128,2048]{1,0:T(8,128)(2,1)S(1)}, bf16[128,2048]{1,0:T(8,128)(2,1)}, u32[]{:S(2)}) %copy-start.3) | copy-done | bytes 524312
  1.0 0.9 %copy-done.4 = bf16[1024,128]{1,0:T(8,128)(2,1)S(1)} copy-done((bf16[1024,128]{1,0:T(8,128)(2,1)S(1)}, bf16[1024,128]{1,0:T(8,128)(2,1)}, u32[]{:S(2)}) %copy-start.4) | copy-done | bytes 262168
  2.0 0.2 shard_map.73
  2.2 1.7 %collective-permute-start = (bf16[3,128,256]{2,1,0:T(8,128)(2,1)S(1)}, bf16[3,128,256]{2,1,0:T(8,128)(2,1)S(1)}, u32[]{:S(2)}, u32[]{:S(2)}) collective-permute-start(bf16[3,128,256]{2,1,0:T(8,128)(2,1)S(1)} %get-tuple-element.41.refs_0_), channel_id=1, source_target_pairs={{0,1},{1,0},{2,3},{3,2},{4,5},{5,4},{6,7},{7,6},{8,9},{9,8},{10,11... | collective-permute-start | bytes 589832 | tf_op jit(solution)/shard_map/ppermute | solution.py:45
  3.8 1.9 %collective-permute-start.1 = (bf16[1,128,256]{2,1,0:T(8,128)(2,1)S(1)}, bf16[1,128,256]{2,1,0:T(8,128)(2,1)S(1)}, u32[]{:S(2)}, u32[]{:S(2)}) collective-permute-start(bf16[1,128,256]{2,1,0:T(8,128)(2,1)S(1)} %get-tuple-element.42.refs_0_), channel_id=1, source_target_pairs={{0,4},{1,5},{2,6},{3,7},{4,0},{5,1},{6,2},{7,3},{8,12},{9,13},{10,... | collective-permute-start | bytes 196616 | tf_op jit(solution)/shard_map/ppermute | solution.py:45
  5.7 2.1 %collective-permute-start.2 = (bf16[1,128,256]{2,1,0:T(8,128)(2,1)S(1)}, bf16[1,128,256]{2,1,0:T(8,128)(2,1)S(1)}, u32[]{:S(2)}, u32[]{:S(2)}) collective-permute-start(bf16[1,128,256]{2,1,0:T(8,128)(2,1)S(1)} %get-tuple-element.43.refs_0_), channel_id=1, source_target_pairs={{0,3},{1,2},{2,1},{3,0},{4,7},{5,6},{6,5},{7,4},{8,11},{9,10},{10,... | collective-permute-start | bytes 196616 | tf_op jit(solution)/shard_map/ppermute | solution.py:45
  7.8 2.5 %collective-permute-start.3 = (bf16[1,128,256]{2,1,0:T(8,128)(2,1)S(1)}, bf16[1,128,256]{2,1,0:T(8,128)(2,1)S(1)}, u32[]{:S(2)}, u32[]{:S(2)}) collective-permute-start(bf16[1,128,256]{2,1,0:T(8,128)(2,1)S(1)} %get-tuple-element.44.refs_0_), channel_id=1, source_target_pairs={{0,12},{1,13},{2,14},{3,15},{4,8},{5,9},{6,10},{7,11},{8,4},{9,5},... | collective-permute-start | bytes 196616 | tf_op jit(solution)/shard_map/ppermute | solution.py:45
  10.4 0.0 collective-permute-done.1.refs_1_
  10.4 0.9 collective-permute-done.2.refs_1_
  11.2 2.1 %collective-permute-done.3.refs_1_ = bf16[1,128,256]{2,1,0:T(8,128)(2,1)S(1)} collective-permute-done((bf16[1,128,256]{2,1,0:T(8,128)(2,1)S(1)}, bf16[1,128,256]{2,1,0:T(8,128)(2,1)S(1)}, u32[]{:S(2)}, u32[]{:S(2)}) %collective-permute-start.3) | collective-permute-done | bytes 65568 | tf_op jit(solution)/shard_map/ppermute | solution.py:45
  13.3 0.0 collective-permute-done.refs_1_
  13.4 1.2 %collective-permute-start.4 = (bf16[6,128,256]{2,1,0:T(8,128)(2,1)S(1)}, bf16[6,128,256]{2,1,0:T(8,128)(2,1)S(1)}, u32[]{:S(2)}, u32[]{:S(2)}) collective-permute-start(bf16[6,128,256]{2,1,0:T(8,128)(2,1)S(1)} %shard_map.74.one_ref), channel_id=1, source_target_pairs={{0,3},{1,2},{2,1},{3,0},{4,7},{5,6},{6,5},{7,4},{8,11},{9,10},{10,... | collective-permute-start | bytes 1179656 | tf_op jit(solution)/shard_map/ppermute | solution.py:45
  14.6 0.4 collective-permute-start.7
  15.0 2.7 %collective-permute-start.5 = (bf16[2,128,256]{2,1,0:T(8,128)(2,1)S(1)}, bf16[2,128,256]{2,1,0:T(8,128)(2,1)S(1)}, u32[]{:S(2)}, u32[]{:S(2)}) collective-permute-start(bf16[2,128,256]{2,1,0:T(8,128)(2,1)S(1)} %shard_map.75.refs_0_), channel_id=1, source_target_pairs={{0,12},{1,13},{2,14},{3,15},{4,8},{5,9},{6,10},{7,11},{8,4},{9,5},... | collective-permute-start | bytes 393224 | tf_op jit(solution)/shard_map/ppermute | solution.py:45
  17.7 2.1 %collective-permute-done.7.refs_1_ = bf16[2,128,256]{2,1,0:T(8,128)(2,1)S(1)} collective-permute-done((bf16[2,128,256]{2,1,0:T(8,128)(2,1)S(1)}, bf16[2,128,256]{2,1,0:T(8,128)(2,1)S(1)}, u32[]{:S(2)}, u32[]{:S(2)}) %collective-permute-start.7) | collective-permute-done | bytes 131104 | tf_op jit(solution)/shard_map/ppermute | solution.py:45
  19.8 0.3 collective-permute-done.6.refs_1_
  20.2 1.0 %collective-permute-done.5.refs_1_ = bf16[2,128,256]{2,1,0:T(8,128)(2,1)S(1)} collective-permute-done((bf16[2,128,256]{2,1,0:T(8,128)(2,1)S(1)}, bf16[2,128,256]{2,1,0:T(8,128)(2,1)S(1)}, u32[]{:S(2)}, u32[]{:S(2)}) %collective-permute-start.5) | collective-permute-done | bytes 131104 | tf_op jit(solution)/shard_map/ppermute | solution.py:45
  21.2 1.9 %collective-permute-done.4.two_ref = bf16[6,128,256]{2,1,0:T(8,128)(2,1)S(1)} collective-permute-done((bf16[6,128,256]{2,1,0:T(8,128)(2,1)S(1)}, bf16[6,128,256]{2,1,0:T(8,128)(2,1)S(1)}, u32[]{:S(2)}, u32[]{:S(2)}) %collective-permute-start.4) | collective-permute-done | bytes 393248 | tf_op jit(solution)/shard_map/ppermute | solution.py:45
  23.0 0.1 shard_map.78
  23.1 1.7 %collective-permute-start.12 = (bf16[8,128,256]{2,1,0:T(8,128)(2,1)S(1)}, bf16[8,128,256]{2,1,0:T(8,128)(2,1)S(1)}, u32[]{:S(2)}, u32[]{:S(2)}) collective-permute-start(bf16[8,128,256]{2,1,0:T(8,128)(2,1)S(1)} %get-tuple-element.54.refs_0_), channel_id=1, source_target_pairs={{0,32},{16,48},{32,0},{48,16},{64,96},{80,112},{96,64},{112,80},{1... | collective-permute-start | bytes 1572872 | tf_op jit(solution)/shard_map/ppermute | solution.py:340
  24.8 1.1 %collective-permute-start.11 = (bf16[4,128,256]{2,1,0:T(8,128)(2,1)S(1)}, bf16[4,128,256]{2,1,0:T(8,128)(2,1)S(1)}, u32[]{:S(2)}, u32[]{:S(2)}) collective-permute-start(bf16[4,128,256]{2,1,0:T(8,128)(2,1)S(1)} %shard_map.81.refs_0_), channel_id=1, source_target_pairs={{0,3},{1,2},{2,1},{3,0},{4,7},{5,6},{6,5},{7,4},{8,11},{9,10},{10,... | collective-permute-start | bytes 786440 | tf_op jit(solution)/shard_map/ppermute | solution.py:45
  26.0 2.3 %collective-permute-start.10 = (bf16[4,128,256]{2,1,0:T(8,128)(2,1)S(1)}, bf16[4,128,256]{2,1,0:T(8,128)(2,1)S(1)}, u32[]{:S(2)}, u32[]{:S(2)}) collective-permute-start(bf16[4,128,256]{2,1,0:T(8,128)(2,1)S(1)} %shard_map.80.refs_0_), channel_id=1, source_target_pairs={{0,12},{1,13},{2,14},{3,15},{4,8},{5,9},{6,10},{7,11},{8,4},{9,5},... | collective-permute-start | bytes 786440 | tf_op jit(solution)/shard_map/ppermute | solution.py:45
  28.3 1.0 %collective-permute-start.9 = (bf16[4,128,256]{2,1,0:T(8,128)(2,1)S(1)}, bf16[4,128,256]{2,1,0:T(8,128)(2,1)S(1)}, u32[]{:S(2)}, u32[]{:S(2)}) collective-permute-start(bf16[4,128,256]{2,1,0:T(8,128)(2,1)S(1)} %shard_map.79.refs_0_), channel_id=1, source_target_pairs={{0,1},{1,0},{2,3},{3,2},{4,5},{5,4},{6,7},{7,6},{8,9},{9,8},{10,11... | collective-permute-start | bytes 786440 | tf_op jit(solution)/shard_map/ppermute | solution.py:45
  29.2 3.5 %collective-permute-done.11.refs_1_ = bf16[4,128,256]{2,1,0:T(8,128)(2,1)S(1)} collective-permute-done((bf16[4,128,256]{2,1,0:T(8,128)(2,1)S(1)}, bf16[4,128,256]{2,1,0:T(8,128)(2,1)S(1)}, u32[]{:S(2)}, u32[]{:S(2)}) %collective-permute-start.11) | collective-permute-done | bytes 262176 | tf_op jit(solution)/shard_map/ppermute | solution.py:45
  32.7 0.8 collective-permute-done.10.refs_1_
  33.6 1.1 %collective-permute-done.9.refs_1_ = bf16[4,128,256]{2,1,0:T(8,128)(2,1)S(1)} collective-permute-done((bf16[4,128,256]{2,1,0:T(8,128)(2,1)S(1)}, bf16[4,128,256]{2,1,0:T(8,128)(2,1)S(1)}, u32[]{:S(2)}, u32[]{:S(2)}) %collective-permute-start.9) | collective-permute-done | bytes 262176 | tf_op jit(solution)/shard_map/ppermute | solution.py:45
  34.6 1.0 %collective-permute-done.8.refs_1_ = bf16[4,128,256]{2,1,0:T(8,128)(2,1)S(1)} collective-permute-done((bf16[4,128,256]{2,1,0:T(8,128)(2,1)S(1)}, bf16[4,128,256]{2,1,0:T(8,128)(2,1)S(1)}, u32[]{:S(2)}, u32[]{:S(2)}) %collective-permute-start.8) | collective-permute-done | bytes 262176 | tf_op jit(solution)/shard_map/ppermute | solution.py:45
  35.6 0.0 collective-permute-done.12.refs_1_
  35.6 0.1 shard_map.86.refs_0_
  35.7 0.0 copy-start
  35.7 0.0 copy-start.1
  35.7 0.0 copy-start.2
  35.7 0.1 collective-permute-start.17
  36.0 1.2 %collective-permute-start.16 = (bf16[8,128,256]{2,1,0:T(8,128)(2,1)S(1)}, bf16[8,128,256]{2,1,0:T(8,128)(2,1)S(1)}, u32[]{:S(2)}, u32[]{:S(2)}) collective-permute-start(bf16[8,128,256]{2,1,0:T(8,128)(2,1)S(1)} %shard_map.85.t3), channel_id=1, source_target_pairs={{0,1},{1,0},{2,3},{3,2},{4,5},{5,4},{6,7},{7,6},{8,9},{9,8},{10,11... | collective-permute-start | bytes 1572872 | tf_op jit(solution)/shard_map/ppermute | solution.py:45
  37.1 0.0 collective-permute-start.15
  37.1 2.8 %collective-permute-start.14 = (bf16[8,128,256]{2,1,0:T(8,128)(2,1)S(1)}, bf16[8,128,256]{2,1,0:T(8,128)(2,1)S(1)}, u32[]{:S(2)}, u32[]{:S(2)}) collective-permute-start(bf16[8,128,256]{2,1,0:T(8,128)(2,1)S(1)} %shard_map.83.t1), channel_id=1, source_target_pairs={{0,3},{1,2},{2,1},{3,0},{4,7},{5,6},{6,5},{7,4},{8,11},{9,10},{10,... | collective-permute-start | bytes 1572872 | tf_op jit(solution)/shard_map/ppermute | solution.py:45
  39.9 0.4 collective-permute-start.13
  40.3 1.3 %shard_map.87.raw_ref = f32[1024,384]{1,0:T(8,128)S(1)} custom-call(bf16[8,128,256]{2,1,0:T(8,128)(2,1)S(1)} %shard_map.82.t0, bf16[8,128,256]{2,1,0:T(8,128)(2,1)S(1)} %shard_map.83.t1, bf16[8,128,256]{2,1,0:T(8,128)(2,1)S(1)} %shard_map.84.t2, bf16[8,128,256]{2,1,0:T(8,128)(2,1)S(1)} %shard_map.85.t3, bf16[2048,128]{1,0:T(8,128)(2,1)S(1)} %copy-done, ...), custom_call_target="tpu_custom_call" | custom-call | flops 805306368 | bytes 5242880 | tf_op jit(solution)/shard_map/pallas_call | solution.py:347
  41.5 0.0 copy-start.6
  41.5 7.2 %collective-permute-done.16.t3 = bf16[8,128,256]{2,1,0:T(8,128)(2,1)S(1)} collective-permute-done((bf16[8,128,256]{2,1,0:T(8,128)(2,1)S(1)}, bf16[8,128,256]{2,1,0:T(8,128)(2,1)S(1)}, u32[]{:S(2)}, u32[]{:S(2)}) %collective-permute-start.16) | collective-permute-done | bytes 524320 | tf_op jit(solution)/shard_map/ppermute | solution.py:45
  48.8 1.9 %collective-permute-done.15.t2 = bf16[8,128,256]{2,1,0:T(8,128)(2,1)S(1)} collective-permute-done((bf16[8,128,256]{2,1,0:T(8,128)(2,1)S(1)}, bf16[8,128,256]{2,1,0:T(8,128)(2,1)S(1)}, u32[]{:S(2)}, u32[]{:S(2)}) %collective-permute-start.15) | collective-permute-done | bytes 524320 | tf_op jit(solution)/shard_map/ppermute | solution.py:45
  50.7 0.9 collective-permute-done.14.t1
  51.6 1.5 %collective-permute-done.13.t0 = bf16[8,128,256]{2,1,0:T(8,128)(2,1)S(1)} collective-permute-done((bf16[8,128,256]{2,1,0:T(8,128)(2,1)S(1)}, bf16[8,128,256]{2,1,0:T(8,128)(2,1)S(1)}, u32[]{:S(2)}, u32[]{:S(2)}) %collective-permute-start.13) | collective-permute-done | bytes 524320 | tf_op jit(solution)/shard_map/ppermute | solution.py:45
  53.1 0.0 collective-permute-done.17.refs_1_
  53.1 0.1 shard_map.92.near_ref
  53.2 0.1 collective-permute-start.22
  53.4 4.7 %shard_map.88 = (bf16[1024,128]{1,0:T(8,128)(2,1)S(1)}, bf16[1024,128]{1,0:T(8,128)(2,1)S(1)}, bf16[1024,256]{1,0:T(8,128)(2,1)S(1)}, bf16[8,128,256]{2,1,0:T(8,...) custom-call(f32[1024,384]{1,0:T(8,128)S(1)} %shard_map.87.raw_ref, ...), custom_call_target="tpu_custom_call" | custom-call | flops 3221225472 | bytes 8388608 | tf_op jit(solution)/shard_map/pallas_call | solution.py:355
  58.0 0.0 copy-start.5
  58.1 0.3 collective-permute-start.18
  58.3 1.5 %shard_map.89 = (bf16[1024,128]{1,0:T(8,128)(2,1)S(1)}, f32[1024,128]{1,0:T(8,128)S(1)}) custom-call(bf16[1024,128]{1,0:T(8,128)(2,1)S(1)} %get-tuple-element.67.q_ref, bf16[1024,128]{1,0:T(8,128)(2,1)S(1)} %get-tuple-element.68.k_ref, bf16[1024,256]{1,0:T(8,128)(2,1)S(1)} %get-tuple-element.69.wu_ref, bf16[8,128,256]{2,1,0:T(8,128)(2,1)S(1)} %get-tuple-element.70.states_ref), custom_call_target="tpu_custom_call" | custom-call | flops 536870912 | bytes 4194304 | tf_op jit(solution)/shard_map/pallas_call | solution.py:369
  59.8 0.0 collective-permute-done.18.other_ref
  59.8 0.2 shard_map.90
  60.0 2.6 %collective-permute-start.21 = (bf16[128,256]{1,0:T(8,128)(2,1)S(1)}, bf16[128,256]{1,0:T(8,128)(2,1)S(1)}, u32[]{:S(2)}, u32[]{:S(2)}) collective-permute-start(bf16[128,256]{1,0:T(8,128)(2,1)S(1)} %shard_map.90), channel_id=1, source_target_pairs={{0,32},{16,48},{32,64},{48,80},{64,96},{80,112},{1,33},{17,49},{33... | collective-permute-start | bytes 196616 | tf_op jit(solution)/shard_map/ppermute | solution.py:382
  62.6 4.8 %collective-permute-start.20 = (bf16[128,256]{1,0:T(8,128)(2,1)S(1)}, bf16[128,256]{1,0:T(8,128)(2,1)S(1)}, u32[]{:S(2)}, u32[]{:S(2)}) collective-permute-start(bf16[128,256]{1,0:T(8,128)(2,1)S(1)} %shard_map.90), channel_id=1, source_target_pairs={{0,64},{16,80},{32,96},{48,112},{1,65},{17,81},{33,97},{49,113},{2... | collective-permute-start | bytes 196616 | tf_op jit(solution)/shard_map/ppermute | solution.py:382
  67.5 1.3 %collective-permute-start.19 = (bf16[128,256]{1,0:T(8,128)(2,1)S(1)}, bf16[128,256]{1,0:T(8,128)(2,1)S(1)}, u32[]{:S(2)}, u32[]{:S(2)}) collective-permute-start(bf16[128,256]{1,0:T(8,128)(2,1)S(1)} %shard_map.90), channel_id=1, source_target_pairs={{0,96},{16,112},{1,97},{17,113},{2,98},{18,114},{3,99},{19,115},{4... | collective-permute-start | bytes 196616 | tf_op jit(solution)/shard_map/ppermute | solution.py:382
  68.8 0.6 collective-permute-done.20.second_ref
  69.4 1.3 %collective-permute-done.19.third_ref = bf16[128,256]{1,0:T(8,128)(2,1)S(1)} collective-permute-done((bf16[128,256]{1,0:T(8,128)(2,1)S(1)}, bf16[128,256]{1,0:T(8,128)(2,1)S(1)}, u32[]{:S(2)}, u32[]{:S(2)}) %collective-permute-start.19) | collective-permute-done | bytes 65568 | tf_op jit(solution)/shard_map/ppermute | solution.py:382
  70.7 0.8 shard_map.91
  71.4 11.6 %all_to_all.9.x_ref = bf16[8,128,128]{2,1,0:T(8,128)(2,1)S(1)} all-to-all(bf16[8,128,128]{2,1,0:T(8,128)(2,1)S(1)} %bitcast.3), channel_id=1, replica_groups={{0,1,2,3,4,5,6,7},{8,9,10,11,12,13,14,15},{16,17,18,19,28,29,30,31},{20..., dimensions={0} | all-to-all | bytes 524288 | tf_op jit(solution)/shard_map/all_to_all | solution.py:395
  83.0 0.9 shard_map.94
  83.9 1.3 %collective-permute-start.23 = (bf16[64,2048]{1,0:T(8,128)(2,1)S(1)}, bf16[64,2048]{1,0:T(8,128)(2,1)S(1)}, u32[]{:S(2)}, u32[]{:S(2)}) collective-permute-start(bf16[64,2048]{1,0:T(8,128)(2,1)S(1)} %shard_map.94), channel_id=1, source_target_pairs={{0,12},{1,13},{2,14},{3,15},{4,8},{5,9},{6,10},{7,11},{8,4},{9,5},... | collective-permute-start | bytes 786440 | tf_op jit(solution)/shard_map/ppermute | solution.py:45
  85.2 0.9 shard_map.93.own_ref
  86.0 5.5 %collective-permute-done.23.other_ref = bf16[64,2048]{1,0:T(8,128)(2,1)S(1)} collective-permute-done((bf16[64,2048]{1,0:T(8,128)(2,1)S(1)}, bf16[64,2048]{1,0:T(8,128)(2,1)S(1)}, u32[]{:S(2)}, u32[]{:S(2)}) %collective-permute-start.23) | collective-permute-done | bytes 262176 | tf_op jit(solution)/shard_map/ppermute | solution.py:45
  91.6 0.7 shard_map.95
  (22 shorter events, 0.3 us)
Async XLA Ops:
  0.0 1.0 %copy-start.3 = (bf16[128,2048]{1,0:T(8,128)(2,1)S(1)}, bf16[128,2048]{1,0:T(8,128)(2,1)}, u32[]{:S(2)}) copy-start(bf16[128,2048]{1,0:T(8,128)(2,1)} %w_ref.1) | copy-start | bytes 1572868
  1.0 0.9 %copy-start.4 = (bf16[1024,128]{1,0:T(8,128)(2,1)S(1)}, bf16[1024,128]{1,0:T(8,128)(2,1)}, u32[]{:S(2)}) copy-start(bf16[1024,128]{1,0:T(8,128)(2,1)} %tokens_ref.1) | copy-start | bytes 786436
  2.2 11.1 %collective-permute-start = (bf16[3,128,256]{2,1,0:T(8,128)(2,1)S(1)}, bf16[3,128,256]{2,1,0:T(8,128)(2,1)S(1)}, u32[]{:S(2)}, u32[]{:S(2)}) collective-permute-start(bf16[3,128,256]{2,1,0:T(8,128)(2,1)S(1)} %get-tuple-element.41.refs_0_), channel_id=1, source_target_pairs={{0,1},{1,0},{2,3},{3,2},{4,5},{5,4},{6,7},{7,6},{8,9},{9,8},{10,11... | collective-permute-start | bytes 589832 | tf_op jit(solution)/shard_map/ppermute | solution.py:45
  3.8 6.5 %collective-permute-start.1 = (bf16[1,128,256]{2,1,0:T(8,128)(2,1)S(1)}, bf16[1,128,256]{2,1,0:T(8,128)(2,1)S(1)}, u32[]{:S(2)}, u32[]{:S(2)}) collective-permute-start(bf16[1,128,256]{2,1,0:T(8,128)(2,1)S(1)} %get-tuple-element.42.refs_0_), channel_id=1, source_target_pairs={{0,4},{1,5},{2,6},{3,7},{4,0},{5,1},{6,2},{7,3},{8,12},{9,13},{10,... | collective-permute-start | bytes 196616 | tf_op jit(solution)/shard_map/ppermute | solution.py:45
  5.7 5.5 %collective-permute-start.2 = (bf16[1,128,256]{2,1,0:T(8,128)(2,1)S(1)}, bf16[1,128,256]{2,1,0:T(8,128)(2,1)S(1)}, u32[]{:S(2)}, u32[]{:S(2)}) collective-permute-start(bf16[1,128,256]{2,1,0:T(8,128)(2,1)S(1)} %get-tuple-element.43.refs_0_), channel_id=1, source_target_pairs={{0,3},{1,2},{2,1},{3,0},{4,7},{5,6},{6,5},{7,4},{8,11},{9,10},{10,... | collective-permute-start | bytes 196616 | tf_op jit(solution)/shard_map/ppermute | solution.py:45
  7.8 5.5 %collective-permute-start.3 = (bf16[1,128,256]{2,1,0:T(8,128)(2,1)S(1)}, bf16[1,128,256]{2,1,0:T(8,128)(2,1)S(1)}, u32[]{:S(2)}, u32[]{:S(2)}) collective-permute-start(bf16[1,128,256]{2,1,0:T(8,128)(2,1)S(1)} %get-tuple-element.44.refs_0_), channel_id=1, source_target_pairs={{0,12},{1,13},{2,14},{3,15},{4,8},{5,9},{6,10},{7,11},{8,4},{9,5},... | collective-permute-start | bytes 196616 | tf_op jit(solution)/shard_map/ppermute | solution.py:45
  13.4 9.7 %collective-permute-start.4 = (bf16[6,128,256]{2,1,0:T(8,128)(2,1)S(1)}, bf16[6,128,256]{2,1,0:T(8,128)(2,1)S(1)}, u32[]{:S(2)}, u32[]{:S(2)}) collective-permute-start(bf16[6,128,256]{2,1,0:T(8,128)(2,1)S(1)} %shard_map.74.one_ref), channel_id=1, source_target_pairs={{0,3},{1,2},{2,1},{3,0},{4,7},{5,6},{6,5},{7,4},{8,11},{9,10},{10,... | collective-permute-start | bytes 1179656 | tf_op jit(solution)/shard_map/ppermute | solution.py:45
  14.6 5.2 %collective-permute-start.7 = (bf16[2,128,256]{2,1,0:T(8,128)(2,1)S(1)}, bf16[2,128,256]{2,1,0:T(8,128)(2,1)S(1)}, u32[]{:S(2)}, u32[]{:S(2)}) collective-permute-start(bf16[2,128,256]{2,1,0:T(8,128)(2,1)S(1)} %shard_map.77.refs_0_), channel_id=1, source_target_pairs={{0,4},{1,5},{2,6},{3,7},{4,0},{5,1},{6,2},{7,3},{8,12},{9,13},{10,... | collective-permute-start | bytes 393224 | tf_op jit(solution)/shard_map/ppermute | solution.py:45
  15.0 5.1 %collective-permute-start.6 = (bf16[2,128,256]{2,1,0:T(8,128)(2,1)S(1)}, bf16[2,128,256]{2,1,0:T(8,128)(2,1)S(1)}, u32[]{:S(2)}, u32[]{:S(2)}) collective-permute-start(bf16[2,128,256]{2,1,0:T(8,128)(2,1)S(1)} %shard_map.76.refs_0_), channel_id=1, source_target_pairs={{0,1},{1,0},{2,3},{3,2},{4,5},{5,4},{6,7},{7,6},{8,9},{9,8},{10,11... | collective-permute-start | bytes 393224 | tf_op jit(solution)/shard_map/ppermute | solution.py:45
  15.0 6.2 %collective-permute-start.5 = (bf16[2,128,256]{2,1,0:T(8,128)(2,1)S(1)}, bf16[2,128,256]{2,1,0:T(8,128)(2,1)S(1)}, u32[]{:S(2)}, u32[]{:S(2)}) collective-permute-start(bf16[2,128,256]{2,1,0:T(8,128)(2,1)S(1)} %shard_map.75.refs_0_), channel_id=1, source_target_pairs={{0,12},{1,13},{2,14},{3,15},{4,8},{5,9},{6,10},{7,11},{8,4},{9,5},... | collective-permute-start | bytes 393224 | tf_op jit(solution)/shard_map/ppermute | solution.py:45
  23.1 12.5 %collective-permute-start.12 = (bf16[8,128,256]{2,1,0:T(8,128)(2,1)S(1)}, bf16[8,128,256]{2,1,0:T(8,128)(2,1)S(1)}, u32[]{:S(2)}, u32[]{:S(2)}) collective-permute-start(bf16[8,128,256]{2,1,0:T(8,128)(2,1)S(1)} %get-tuple-element.54.refs_0_), channel_id=1, source_target_pairs={{0,32},{16,48},{32,0},{48,16},{64,96},{80,112},{96,64},{112,80},{1... | collective-permute-start | bytes 1572872 | tf_op jit(solution)/shard_map/ppermute | solution.py:340
  24.8 7.9 %collective-permute-start.11 = (bf16[4,128,256]{2,1,0:T(8,128)(2,1)S(1)}, bf16[4,128,256]{2,1,0:T(8,128)(2,1)S(1)}, u32[]{:S(2)}, u32[]{:S(2)}) collective-permute-start(bf16[4,128,256]{2,1,0:T(8,128)(2,1)S(1)} %shard_map.81.refs_0_), channel_id=1, source_target_pairs={{0,3},{1,2},{2,1},{3,0},{4,7},{5,6},{6,5},{7,4},{8,11},{9,10},{10,... | collective-permute-start | bytes 786440 | tf_op jit(solution)/shard_map/ppermute | solution.py:45
  26.0 7.6 %collective-permute-start.10 = (bf16[4,128,256]{2,1,0:T(8,128)(2,1)S(1)}, bf16[4,128,256]{2,1,0:T(8,128)(2,1)S(1)}, u32[]{:S(2)}, u32[]{:S(2)}) collective-permute-start(bf16[4,128,256]{2,1,0:T(8,128)(2,1)S(1)} %shard_map.80.refs_0_), channel_id=1, source_target_pairs={{0,12},{1,13},{2,14},{3,15},{4,8},{5,9},{6,10},{7,11},{8,4},{9,5},... | collective-permute-start | bytes 786440 | tf_op jit(solution)/shard_map/ppermute | solution.py:45
  28.3 6.4 %collective-permute-start.9 = (bf16[4,128,256]{2,1,0:T(8,128)(2,1)S(1)}, bf16[4,128,256]{2,1,0:T(8,128)(2,1)S(1)}, u32[]{:S(2)}, u32[]{:S(2)}) collective-permute-start(bf16[4,128,256]{2,1,0:T(8,128)(2,1)S(1)} %shard_map.79.refs_0_), channel_id=1, source_target_pairs={{0,1},{1,0},{2,3},{3,2},{4,5},{5,4},{6,7},{7,6},{8,9},{9,8},{10,11... | collective-permute-start | bytes 786440 | tf_op jit(solution)/shard_map/ppermute | solution.py:45
  29.2 6.4 %collective-permute-start.8 = (bf16[4,128,256]{2,1,0:T(8,128)(2,1)S(1)}, bf16[4,128,256]{2,1,0:T(8,128)(2,1)S(1)}, u32[]{:S(2)}, u32[]{:S(2)}) collective-permute-start(bf16[4,128,256]{2,1,0:T(8,128)(2,1)S(1)} %get-tuple-element.50.refs_0_), channel_id=1, source_target_pairs={{0,4},{1,5},{2,6},{3,7},{4,0},{5,1},{6,2},{7,3},{8,12},{9,13},{10,... | collective-permute-start | bytes 786440 | tf_op jit(solution)/shard_map/ppermute | solution.py:45
  35.7 4.6 %copy-start = (bf16[2048,128]{1,0:T(8,128)(2,1)S(1)}, bf16[2048,128]{1,0:T(8,128)(2,1)}, u32[]{:S(2)}) copy-start(bf16[2048,128]{1,0:T(8,128)(2,1)} %wq.3) | copy-start | bytes 1572868
  35.7 4.6 %copy-start.1 = (bf16[2048,128]{1,0:T(8,128)(2,1)S(1)}, bf16[2048,128]{1,0:T(8,128)(2,1)}, u32[]{:S(2)}) copy-start(bf16[2048,128]{1,0:T(8,128)(2,1)} %wk.3) | copy-start | bytes 1572868
  35.7 4.6 %copy-start.2 = (bf16[2048,128]{1,0:T(8,128)(2,1)S(1)}, bf16[2048,128]{1,0:T(8,128)(2,1)}, u32[]{:S(2)}) copy-start(bf16[2048,128]{1,0:T(8,128)(2,1)} %wv.3) | copy-start | bytes 1572868
  35.7 17.4 %collective-permute-start.17 = (bf16[16,128,256]{2,1,0:T(8,128)(2,1)S(1)}, bf16[16,128,256]{2,1,0:T(8,128)(2,1)S(1)}, u32[]{:S(2)}, u32[]{:S(2)}) collective-permute-start(bf16[16,128,256]{2,1,0:T(8,128)(2,1)S(1)} %shard_map.86.refs_0_), channel_id=1, source_target_pairs={{0,16},{16,0},{32,48},{48,32},{64,80},{80,64},{96,112},{112,96},{1... | collective-permute-start | bytes 3145736 | tf_op jit(solution)/shard_map/ppermute | solution.py:350
  36.0 12.8 %collective-permute-start.16 = (bf16[8,128,256]{2,1,0:T(8,128)(2,1)S(1)}, bf16[8,128,256]{2,1,0:T(8,128)(2,1)S(1)}, u32[]{:S(2)}, u32[]{:S(2)}) collective-permute-start(bf16[8,128,256]{2,1,0:T(8,128)(2,1)S(1)} %shard_map.85.t3), channel_id=1, source_target_pairs={{0,1},{1,0},{2,3},{3,2},{4,5},{5,4},{6,7},{7,6},{8,9},{9,8},{10,11... | collective-permute-start | bytes 1572872 | tf_op jit(solution)/shard_map/ppermute | solution.py:45
  37.1 13.6 %collective-permute-start.15 = (bf16[8,128,256]{2,1,0:T(8,128)(2,1)S(1)}, bf16[8,128,256]{2,1,0:T(8,128)(2,1)S(1)}, u32[]{:S(2)}, u32[]{:S(2)}) collective-permute-start(bf16[8,128,256]{2,1,0:T(8,128)(2,1)S(1)} %shard_map.84.t2), channel_id=1, source_target_pairs={{0,4},{1,5},{2,6},{3,7},{4,0},{5,1},{6,2},{7,3},{8,12},{9,13},{10,... | collective-permute-start | bytes 1572872 | tf_op jit(solution)/shard_map/ppermute | solution.py:45
  37.1 14.5 %collective-permute-start.14 = (bf16[8,128,256]{2,1,0:T(8,128)(2,1)S(1)}, bf16[8,128,256]{2,1,0:T(8,128)(2,1)S(1)}, u32[]{:S(2)}, u32[]{:S(2)}) collective-permute-start(bf16[8,128,256]{2,1,0:T(8,128)(2,1)S(1)} %shard_map.83.t1), channel_id=1, source_target_pairs={{0,3},{1,2},{2,1},{3,0},{4,7},{5,6},{6,5},{7,4},{8,11},{9,10},{10,... | collective-permute-start | bytes 1572872 | tf_op jit(solution)/shard_map/ppermute | solution.py:45
  39.9 13.2 %collective-permute-start.13 = (bf16[8,128,256]{2,1,0:T(8,128)(2,1)S(1)}, bf16[8,128,256]{2,1,0:T(8,128)(2,1)S(1)}, u32[]{:S(2)}, u32[]{:S(2)}) collective-permute-start(bf16[8,128,256]{2,1,0:T(8,128)(2,1)S(1)} %shard_map.82.t0), channel_id=1, source_target_pairs={{0,12},{1,13},{2,14},{3,15},{4,8},{5,9},{6,10},{7,11},{8,4},{9,5},... | collective-permute-start | bytes 1572872 | tf_op jit(solution)/shard_map/ppermute | solution.py:45
  41.5 11.8 %copy-start.6 = (f32[1024,1]{0,1:T(1,128)S(1)}, f32[1024,1]{0,1:T(1,128)}, u32[]{:S(2)}) copy-start(f32[1024,1]{0,1:T(1,128)} %param.8) | copy-start | bytes 12292
  53.2 29.8 %collective-permute-start.22 = (bf16[32,128,256]{2,1,0:T(8,128)(2,1)S(1)}, bf16[32,128,256]{2,1,0:T(8,128)(2,1)S(1)}, u32[]{:S(2)}, u32[]{:S(2)}) collective-permute-start(bf16[32,128,256]{2,1,0:T(8,128)(2,1)S(1)} %shard_map.92.near_ref), channel_id=1, source_target_pairs={{0,4},{1,5},{2,6},{3,7},{4,0},{5,1},{6,2},{7,3},{8,12},{9,13},{10,... | collective-permute-start | bytes 6291464 | tf_op jit(solution)/shard_map/ppermute | solution.py:45
  58.0 12.6 %copy-start.5 = (f32[128]{0:T(128)S(1)}, f32[128]{0:T(128)}, u32[]{:S(2)}) copy-start(f32[128]{0:T(128)} %param.12) | copy-start | bytes 1540
  58.1 1.8 %collective-permute-start.18 = (bf16[128,256]{1,0:T(8,128)(2,1)S(1)}, bf16[128,256]{1,0:T(8,128)(2,1)S(1)}, u32[]{:S(2)}, u32[]{:S(2)}) collective-permute-start(bf16[128,256]{1,0:T(8,128)(2,1)S(1)} %get-tuple-element.66), channel_id=1, source_target_pairs={{0,16},{16,0},{32,48},{48,32},{64,80},{80,64},{96,112},{112,96},{1... | collective-permute-start | bytes 196616 | tf_op jit(solution)/shard_map/ppermute | solution.py:376
  60.0 8.8 %collective-permute-start.21 = (bf16[128,256]{1,0:T(8,128)(2,1)S(1)}, bf16[128,256]{1,0:T(8,128)(2,1)S(1)}, u32[]{:S(2)}, u32[]{:S(2)}) collective-permute-start(bf16[128,256]{1,0:T(8,128)(2,1)S(1)} %shard_map.90), channel_id=1, source_target_pairs={{0,32},{16,48},{32,64},{48,80},{64,96},{80,112},{1,33},{17,49},{33... | collective-permute-start | bytes 196616 | tf_op jit(solution)/shard_map/ppermute | solution.py:382
  62.6 6.7 %collective-permute-start.20 = (bf16[128,256]{1,0:T(8,128)(2,1)S(1)}, bf16[128,256]{1,0:T(8,128)(2,1)S(1)}, u32[]{:S(2)}, u32[]{:S(2)}) collective-permute-start(bf16[128,256]{1,0:T(8,128)(2,1)S(1)} %shard_map.90), channel_id=1, source_target_pairs={{0,64},{16,80},{32,96},{48,112},{1,65},{17,81},{33,97},{49,113},{2... | collective-permute-start | bytes 196616 | tf_op jit(solution)/shard_map/ppermute | solution.py:382
  67.5 3.2 %collective-permute-start.19 = (bf16[128,256]{1,0:T(8,128)(2,1)S(1)}, bf16[128,256]{1,0:T(8,128)(2,1)S(1)}, u32[]{:S(2)}, u32[]{:S(2)}) collective-permute-start(bf16[128,256]{1,0:T(8,128)(2,1)S(1)} %shard_map.90), channel_id=1, source_target_pairs={{0,96},{16,112},{1,97},{17,113},{2,98},{18,114},{3,99},{19,115},{4... | collective-permute-start | bytes 196616 | tf_op jit(solution)/shard_map/ppermute | solution.py:382
  83.9 7.7 %collective-permute-start.23 = (bf16[64,2048]{1,0:T(8,128)(2,1)S(1)}, bf16[64,2048]{1,0:T(8,128)(2,1)S(1)}, u32[]{:S(2)}, u32[]{:S(2)}) collective-permute-start(bf16[64,2048]{1,0:T(8,128)(2,1)S(1)} %shard_map.94), channel_id=1, source_target_pairs={{0,12},{1,13},{2,14},{3,15},{4,8},{5,9},{6,10},{7,11},{8,4},{9,5},... | collective-permute-start | bytes 786440 | tf_op jit(solution)/shard_map/ppermute | solution.py:45

commit v3 on v2

--- a/solution.py
+++ b/solution.py
@@ -30,6 +30,13 @@
     return tuple((odd, even) for even, odd in masks)
 
 
+OPPOSITE = (12, 4)
+
+
+def flipped(masks):
+    return tuple((odd, even) for even, odd in masks)
+
+
 STREAMS = (
     ALONG_X + ALONG_Z,
     ALONG_Z + ALONG_X,
@@ -38,6 +45,14 @@
 )
 
 
+STREAMS = (
+    ALONG_X + ALONG_Z,
+    ALONG_Z + ALONG_X,
+    ALONG_X + flipped(ALONG_Z),
+    ALONG_Z + flipped(ALONG_X),
+)
+
+
 def swap(value, masks, ctx, heads):
     pairs = [
         (c * heads + h, c * heads + (h ^ masks[c % 2])) for c in range(ctx) for h in range(heads)
@@ -66,26 +81,21 @@
         return [self.head ^ self.by_core(a, b) for a, b in zip(offsets(masks, 0), offsets(masks, 1))]
 
 
-def pack_kernel(tokens_ref, w_ref, p0, p1, p2, p3, sems):
+def pack_kernel(tokens_ref, a_ref, b_ref):
+    for stream, out in enumerate((a_ref, b_ref)):
+        for i in range(4):
+            start = (2 * stream + i % 2 + 4 * (i // 2)) * DK
+            at = (i % 2) * DK
+            out[i // 2, :, at : at + DK] = tokens_ref[start : start + DK, :]
+
+
+def pack_with_w_kernel(piece_ref, w_ref, out_ref):
     place = Place()
     quarter = place.core * 2 + lax.rem(place.y, 2)
-    copies = []
-    for stream, out in enumerate((p0, p1, p2, p3)):
-        for i in range(2):
-            start = (2 * stream + i) * DK
-            copies.append(
-                (tokens_ref.at[start : start + DK, :], out.at[0, :, i * DK : (i + 1) * DK])
-            )
-    for i in range(2):
-        start = pl.multiple_of(quarter * 512 + i * 256, 256)
-        copies.append((w_ref.at[:, pl.ds(start, 256)], p0.at[1 + i]))
-    started = []
-    for n, (source, target) in enumerate(copies):
-        copy = pltpu.make_async_copy(source, target, sems.at[n])
-        copy.start()
-        started.append(copy)
-    for copy in started:
-        copy.wait()
+    out_ref[:2] = piece_ref[...]
+    for k in range(2):
+        start = pl.multiple_of(quarter * 512 + k * 256, 256)
+        out_ref[2 + k] = w_ref[:, pl.ds(start, 256)]
 
 
 def join_kernel(*refs):
@@ -95,12 +105,14 @@
         at += ref.shape[0]
 
 
-def split_kernel(one_ref, two_ref, tokens_ref, w_ref):
+def split_kernel(one_ref, two_ref, first_ref, second_ref, *w_ref):
+    width = one_ref.shape[0] // 2
     for i in range(4):
-        source, at = (one_ref, two_ref)[i // 2], 3 * (i % 2)
-        tokens_ref[i] = source[at]
-        w_ref[2 * i] = source[at + 1]
-        w_ref[2 * i + 1] = source[at + 2]
+        source, at = (one_ref, two_ref)[i // 2], width * (i % 2)
+        first_ref[i] = source[at]
+        second_ref[i] = source[at + 1]
+        if w_ref:
+            w_ref[0][2 * i : 2 * i + 2] = source[at + 2 : at + 4]
 
 
 def project_part(heads, pieces_ref, weights):
@@ -219,6 +231,10 @@
     )
 
 
+def apply(step, state):
+    return dot(step[:, :DK], state) + step[:, DK:]
+
+
 def chip_kernel(mine_ref, other_ref, chip_ref):
     mine, other = mine_ref[...], other_ref[...].astype(F32)
     second = Place().core == 1
@@ -227,15 +243,21 @@
     ).astype(BF16)
 
 
-def finish_kernel(
-    third_ref, second_ref, first_ref, other_ref, query_ref, out_ref, gain_ref, normed_ref
-):
+def pair_kernel(mine_ref, other_ref, sent_ref):
+    mine, other = mine_ref[...].astype(F32), other_ref[...].astype(F32)
+    odd = lax.rem(Place().y, 2) == 1
+    sent_ref[...] = apply(jnp.where(odd, mine, other), jnp.where(odd, other, mine)[:, DK:]).astype(
+        BF16
+    )
+
+
+def finish_kernel(pair_ref, chip_ref, core_ref, query_ref, out_ref, gain_ref, normed_ref):
     place = Place()
-    entering = third_ref[:, DK:].astype(F32)
-    for earlier in (second_ref, first_ref):
-        entering = dot(earlier[:, :DK], entering) + earlier[:, DK:].astype(F32)
-    after_other = dot(other_ref[:, :DK], entering) + other_ref[:, DK:].astype(F32)
-    entering = jnp.where(place.core == 1, after_other, entering)
+    entering = jnp.where(place.y >= 2, pair_ref[...].astype(F32), 0.0)
+    entering = jnp.where(
+        lax.rem(place.y, 2) == 1, apply(chip_ref[...].astype(F32), entering), entering
+    )
+    entering = jnp.where(place.core == 1, apply(core_ref[...].astype(F32), entering), entering)
     recurrent = out_ref[...] + dot(query_ref[...], entering)
     scale = lax.rsqrt(jnp.mean(recurrent * recurrent, axis=-1, keepdims=True) + 1e-5)
     normed = (recurrent * scale * gain_ref[...]).astype(BF16)
@@ -250,10 +272,10 @@
         normed_ref[pl.ds(start, 64), :] = normed[b * 64 : (b + 1) * 64, :]
 
 
-def mix_rows(x_ref, near_ref, far_ref, rows, out_ref, dtype):
+def mix_rows(x_ref, refs, rows, out_ref, dtype):
     place = Place()
     seat = place.by_core(lax.rem(place.z, 2), lax.div(place.z, 2))
-    along_x = [offsets(STREAMS[0][:2], core) for core in range(2)]
+    along_x = [offsets(ALONG_X, c) for c in range(2)]
     even = lax.rem(place.y, 2)
     for side in range(2):
         core = place.core if side == 0 else 1 - place.core
@@ -267,26 +289,25 @@
                 lefts[group, j] = jnp.concatenate(
                     [x_ref[base + order[j], rows, :], x_ref[base + order[j + 1], rows, :]], axis=1
                 )
-        for quarter in range(2):
-            column = (core * 2 + (even if quarter == 0 else 1 - even)) * 512
-            for slab in range(2):
-                total = None
-                for group, ref in enumerate((near_ref, far_ref)):
-                    at = side * 16 + quarter * 8 + slab
-                    for j in (0, 2):
-                        right = jnp.concatenate([ref[at + 2 * j], ref[at + 2 * j + 2]], axis=0)
-                        term = jnp.dot(lefts[group, j], right, preferred_element_type=F32)
-                        total = term if total is None else total + term
-                start = pl.multiple_of(column + slab * 256, 256)
-                out_ref[:, pl.ds(start, 256)] = total.astype(dtype)
-
-
-def mix_partner_kernel(x_ref, near_ref, far_ref, out_ref):
-    mix_rows(x_ref, near_ref, far_ref, slice(64, 128), out_ref, BF16)
-
-
-def mix_own_kernel(x_ref, near_ref, far_ref, out_ref):
-    mix_rows(x_ref, near_ref, far_ref, slice(0, 64), out_ref, F32)
+        for slab in range(4):
+            total = None
+            for group, ref in enumerate((refs[side], refs[2 + side])):
+                for j in (0, 2):
+                    at = (slab // 2) * 8 + j * 2 + slab % 2
+                    right = jnp.concatenate([ref[at], ref[at + 2]], axis=0)
+                    term = jnp.dot(lefts[group, j], right, preferred_element_type=F32)
+                    total = term if total is None else total + term
+            parity = even if slab < 2 else 1 - even
+            start = pl.multiple_of((core * 2 + parity) * 512 + (slab % 2) * 256, 256)
+            out_ref[:, pl.ds(start, 256)] = total.astype(dtype)
+
+
+def mix_partner_kernel(x_ref, *refs):
+    mix_rows(x_ref, refs[:4], slice(64, 128), refs[4], BF16)
+
+
+def mix_own_kernel(x_ref, *refs):
+    mix_rows(x_ref, refs[:4], slice(0, 64), refs[4], F32)
 
 
 def sum_kernel(own_ref, other_ref, mixed_ref):
@@ -320,37 +341,31 @@
     weights = (w_query, w_key, w_value)
 
     slab = (DK, 2 * DK)
-    pieces = pl.pallas_call(
-        pack_kernel,
-        out_shape=tuple(struct((n,) + slab, BF16) for n in (3, 1, 1, 1)),
-        in_specs=[pl.BlockSpec(memory_space=pltpu.HBM)] * 2,
-        out_specs=(VMEM,) * 4,
-        scratch_shapes=[pltpu.SemaphoreType.DMA((10,))],
-        compiler_params=pltpu.CompilerParams(vmem_limit_bytes=LIMIT),
-    )(tokens, w_out)
-    arrived = [swap(p, masks[0], ctx, heads) for p, masks in zip(pieces, STREAMS)]
-    arrived = lax.optimization_barrier(arrived)
-    pieces = [join(p, n) for p, n in zip(pieces, arrived)]
-    arrived = [swap(p, masks[1], ctx, heads) for p, masks in zip(pieces, STREAMS)]
-    arrived = lax.optimization_barrier(arrived)
-    first, w = call(
-        split_kernel, (struct((4,) + slab, BF16), struct((8,) + slab, BF16)), 2, size=2 << 20
-    )(pieces[0], arrived[0])
-    pieces = [first] + [join(p, n) for p, n in zip(pieces[1:], arrived[1:])]
+    a, b = call(pack_kernel, (struct((2,) + slab, BF16),) * 2, 1, size=1 << 19)(tokens)
+    a = call(pack_with_w_kernel, struct((4,) + slab, BF16), 2, size=1 << 20)(a, w_out)
+    na, nb = swap(a, STREAMS[0][0], ctx, heads), swap(b, STREAMS[1][0], ctx, heads)
+    na, nb = lax.optimization_barrier((na, nb))
+    a, b = join(a, na), join(b, nb)
+    na, nb = swap(a, STREAMS[0][1], ctx, heads), swap(b, STREAMS[1][1], ctx, heads)
+    four = struct((4,) + slab, BF16)
+    pieces = [None] * 4
+    pieces[0], pieces[2], w = call(
+        split_kernel, (four, four, struct((8,) + slab, BF16)), 2, size=2 << 20
+    )(a, na)
+    pieces[1], pieces[3] = call(split_kernel, (four, four), 2, size=1 << 20)(b, nb)
+    *_, w = lax.optimization_barrier((*pieces, w))
+    other_core = [(c, c ^ 1) for c in range(ctx)]
     w_next = lax.ppermute(w, "ctx", [(c, c ^ 2) for c in range(ctx)])
     arrived = [swap(p, masks[2], ctx, heads) for p, masks in zip(pieces, STREAMS)]
-    *arrived, w_next = lax.optimization_barrier((*arrived, w_next))
-    w = join(w, w_next)
-    other_core = [(c, c ^ 1) for c in range(ctx)]
     pieces = [join(p, n) for p, n in zip(pieces, arrived)]
     arrived = [swap(p, masks[3], ctx, heads) for p, masks in zip(pieces, STREAMS)]
     raw = call(
         first_half_kernel, struct((rows, 3 * DK), F32), 7, flops=rows * 1024 * 768, size=5 << 20
     )(*pieces, *weights)
+    *arrived, w_next, raw = lax.optimization_barrier((*arrived, w_next, raw))
+    w = join(w, w_next)
+    far_a = swap(w, (4, 12), ctx, heads)
     w_next = lax.ppermute(w, "ctx", other_core)
-    *arrived, w_next, raw = lax.optimization_barrier((*arrived, w_next, raw))
-    near = join(w, w_next)
-    far = swap(near, (4, 12), ctx, heads)
 
     query, key, wu, states, last, sent = call(
         transition_kernel,
@@ -373,19 +388,19 @@
         flops=rows * 2048 * 256, size=4 << 20,
     )(query, key, wu, states)
 
-    other = lax.ppermute(sent, "ctx", other_core)
-    other, eff_query, partial = lax.optimization_barrier((other, eff_query, partial))
+    _, w_next = lax.optimization_barrier((sent, w_next))
+    far_b = swap(w_next, (4, 12), ctx, heads)
+    of_core = lax.ppermute(sent, "ctx", other_core)
     chip = call(
         chip_kernel, struct((DK, 2 * DK), BF16), 2, flops=1 << 23, size=1 << 18
-    )(last, other)
-    one, two, three = [
-        lax.ppermute(chip, "ctx", [(c, c + 2 * k) for c in range(ctx - 2 * k)])
-        for k in (1, 2, 3)
-    ]
-
+    )(last, of_core)
+    of_chip = lax.ppermute(chip, "ctx", [(c, c ^ 2) for c in range(ctx)])
+    of_chip, eff_query, partial = lax.optimization_barrier((of_chip, eff_query, partial))
+    pair = call(pair_kernel, struct((DK, DK), BF16), 2, flops=1 << 23, size=1 << 18)(chip, of_chip)
+    of_pair = lax.ppermute(pair, "ctx", [(c, c ^ 6) for c in range(ctx)])
     normed = call(
-        finish_kernel, struct((rows, DK), BF16), 7, flops=rows * 128 * 256, size=2 << 20
-    )(three, two, one, other, eff_query, partial, gain[None, :])
+        finish_kernel, struct((rows, DK), BF16), 6, flops=rows * 128 * 256, size=2 << 20
+    )(of_pair, of_chip, of_core, eff_query, partial, gain[None, :])
     pairs = (((0, 1), (2, 3)), ((0, 3), (1, 2)))
     groups = [
         [c * heads + z * 4 + x for z in pair for x in range(4)]
@@ -396,13 +411,13 @@
         normed, ("ctx", "head"), 0, 0, tiled=True, axis_index_groups=groups
     ).reshape(8, 2 * rows // heads, DK)
 
-    operands = (spread_rows, near, far)
+    operands = (spread_rows, w, w_next, far_a, far_b)
     leaving = call(
-        mix_partner_kernel, struct((64, 2048), BF16), 3, flops=64 * 2048 * 2048, size=4 << 20
+        mix_partner_kernel, struct((64, 2048), BF16), 5, flops=64 * 2048 * 2048, size=4 << 20
     )(*operands)
     entering = swap(leaving, OPPOSITE, ctx, heads)
     own = call(
-        mix_own_kernel, struct((64, 2048), F32), 3, flops=64 * 2048 * 2048, size=4 << 20
+        mix_own_kernel, struct((64, 2048), F32), 5, flops=64 * 2048 * 2048, size=4 << 20
     )(*operands)
     return call(sum_kernel, struct((64, 2048), BF16), 2, size=1 << 20)(own, entering)
 

time: 93.1 us -> 84.4 us (0.907)
  waiting for transfers between devices: 33.6 us -> 28.8 us
  starting transfers between devices: 33.3 us -> 30.2 us
    ppermute x18 -> x15, waiting for transfers between devices: 31.7 us -> 21.7 us  [swap(): return lax.ppermute(value, ('ctx', 'head'), pairs)]
    ppermute x4 -> x3, starting transfers between devices: 9.01 us -> 3.82 us  [the longest x1 2.22 us: local(): of_pair = lax.ppermute(pair, 'ctx', [(c, c ^ 6) for c in range(ctx)])]
    ppermute x4 -> x3, waiting for transfers between devices: 1.88 us -> 6.26 us  [the longest x1 2.95 us: local(): of_pair = lax.ppermute(pair, 'ctx', [(c, c ^ 6) for c in range(ctx)])]
    ppermute x18 -> x15, starting transfers between devices: 22.5 us -> 24.7 us  [swap(): return lax.ppermute(value, ('ctx', 'head'), pairs)]
    pallas_call x5 -> x8, Pallas kernels: 2.69 us -> 2.67 us  [the longest x1 0.85 us: local(): call(mix_partner_kernel, struct((64, 2048), BF16), 5, flops=64 * 2048 * 2...]
  transfers between devices with their start and end apart: 24 -> 20, of which waited for: 17 -> 12; matrix products, arithmetic and copies ran while one was open for 0% -> 0% of each run, Pallas kernels for 10% -> 11%
where the time goes in v3:
time: 84.4 us; the launch traced here: 84.2 us
  starting transfers between devices  30.2 us (36%)
  waiting for transfers between devices  28.8 us (34%)
  blocking collectives  11.8 us (14%)
  Pallas kernels  11.2 us (13%)
  local copies, waits for them, and re-layouts  2.02 us (2%)
    ppermute x15, starting transfers between devices, swap(): return lax.ppermute(value, ('ctx', 'head'), pairs)  24.7 us
    ppermute x15, waiting for transfers between devices, swap(): return lax.ppermute(value, ('ctx', 'head'), pairs)  21.7 us
    all_to_all x1, blocking collectives, local(): lax.all_to_all(normed, ('ctx', 'head'), 0, 0, tiled=True, axis_index_grou...  11.8 us
    pallas_call x1, Pallas kernels, local(): call(transition_kernel, (struct((rows, DK), BF16), struct((rows, DK), BF1...  4.65 us
    ppermute x1, waiting for transfers between devices, local(): of_pair = lax.ppermute(pair, 'ctx', [(c, c ^ 6) for c in range(ctx)])  2.95 us
    ppermute x1, waiting for transfers between devices, local(): of_chip = lax.ppermute(chip, 'ctx', [(c, c ^ 2) for c in range(ctx)])  2.41 us
    ppermute x1, starting transfers between devices, local(): of_pair = lax.ppermute(pair, 'ctx', [(c, c ^ 6) for c in range(ctx)])  2.22 us
    unnamed x14, local copies, waits for them, and re-layouts  2.02 us
  transfers between devices with their start and end apart: 20, of which 12 were waited for; matrix products, arithmetic and copies ran while one was open for 0% of the time, Pallas kernels for 11%

profile of v3, /device:TPU:0, one launch (start us, length us, event | category | flops | bytes accessed | tf_op | source)
XLA Modules:
  0.0 84.2 jit_solution(412145159355691849)
XLA Ops:
  0.0 0.9 %copy-done.4 = bf16[1024,128]{1,0:T(8,128)(2,1)S(1)} copy-done((bf16[1024,128]{1,0:T(8,128)(2,1)S(1)}, bf16[1024,128]{1,0:T(8,128)(2,1)}, u32[]{:S(2)}) %copy-start.4) | copy-done | bytes 262168
  1.0 0.0 copy-start.3
  1.0 1.0 %copy-done.3 = bf16[128,2048]{1,0:T(8,128)(2,1)S(1)} copy-done((bf16[128,2048]{1,0:T(8,128)(2,1)S(1)}, bf16[128,2048]{1,0:T(8,128)(2,1)}, u32[]{:S(2)}) %copy-start.3) | copy-done | bytes 524312
  2.1 1.7 %collective-permute-start = (bf16[4,128,256]{2,1,0:T(8,128)(2,1)S(1)}, bf16[4,128,256]{2,1,0:T(8,128)(2,1)S(1)}, u32[]{:S(2)}, u32[]{:S(2)}) collective-permute-start(bf16[4,128,256]{2,1,0:T(8,128)(2,1)S(1)} %shard_map.74.refs_0_), channel_id=1, source_target_pairs={{0,1},{1,0},{2,3},{3,2},{4,5},{5,4},{6,7},{7,6},{8,9},{9,8},{10,11... | collective-permute-start | bytes 786440 | tf_op jit(solution)/shard_map/ppermute | solution.py:60
  3.7 1.9 %collective-permute-start.1 = (bf16[2,128,256]{2,1,0:T(8,128)(2,1)S(1)}, bf16[2,128,256]{2,1,0:T(8,128)(2,1)S(1)}, u32[]{:S(2)}, u32[]{:S(2)}) collective-permute-start(bf16[2,128,256]{2,1,0:T(8,128)(2,1)S(1)} %get-tuple-element.34.refs_0_), channel_id=1, source_target_pairs={{0,4},{1,5},{2,6},{3,7},{4,0},{5,1},{6,2},{7,3},{8,12},{9,13},{10,... | collective-permute-start | bytes 393224 | tf_op jit(solution)/shard_map/ppermute | solution.py:60
  5.7 3.0 %collective-permute-done.1.refs_1_ = bf16[2,128,256]{2,1,0:T(8,128)(2,1)S(1)} collective-permute-done((bf16[2,128,256]{2,1,0:T(8,128)(2,1)S(1)}, bf16[2,128,256]{2,1,0:T(8,128)(2,1)S(1)}, u32[]{:S(2)}, u32[]{:S(2)}) %collective-permute-start.1) | collective-permute-done | bytes 131104 | tf_op jit(solution)/shard_map/ppermute | solution.py:60
  8.7 0.0 collective-permute-done.refs_1_
  8.7 2.7 %collective-permute-start.2 = (bf16[8,128,256]{2,1,0:T(8,128)(2,1)S(1)}, bf16[8,128,256]{2,1,0:T(8,128)(2,1)S(1)}, u32[]{:S(2)}, u32[]{:S(2)}) collective-permute-start(bf16[8,128,256]{2,1,0:T(8,128)(2,1)S(1)} %shard_map.75.one_ref), channel_id=1, source_target_pairs={{0,3},{1,2},{2,1},{3,0},{4,7},{5,6},{6,5},{7,4},{8,11},{9,10},{10,... | collective-permute-start | bytes 1572872 | tf_op jit(solution)/shard_map/ppermute | solution.py:60
  11.5 4.1 %collective-permute-start.5 = (bf16[4,128,256]{2,1,0:T(8,128)(2,1)S(1)}, bf16[4,128,256]{2,1,0:T(8,128)(2,1)S(1)}, u32[]{:S(2)}, u32[]{:S(2)}) collective-permute-start(bf16[4,128,256]{2,1,0:T(8,128)(2,1)S(1)} %shard_map.78.one_ref), channel_id=1, source_target_pairs={{0,12},{1,13},{2,14},{3,15},{4,8},{5,9},{6,10},{7,11},{8,4},{9,5},... | collective-permute-start | bytes 786440 | tf_op jit(solution)/shard_map/ppermute | solution.py:60
  15.6 4.4 %collective-permute-done.5.two_ref = bf16[4,128,256]{2,1,0:T(8,128)(2,1)S(1)} collective-permute-done((bf16[4,128,256]{2,1,0:T(8,128)(2,1)S(1)}, bf16[4,128,256]{2,1,0:T(8,128)(2,1)S(1)}, u32[]{:S(2)}, u32[]{:S(2)}) %collective-permute-start.5) | collective-permute-done | bytes 262176 | tf_op jit(solution)/shard_map/ppermute | solution.py:60
  20.0 0.6 collective-permute-start.10
  20.7 0.2 collective-permute-start.6
  20.9 0.0 collective-permute-done.2.two_ref
  20.9 0.1 shard_map.76
  20.9 3.3 %collective-permute-start.8 = (bf16[4,128,256]{2,1,0:T(8,128)(2,1)S(1)}, bf16[4,128,256]{2,1,0:T(8,128)(2,1)S(1)}, u32[]{:S(2)}, u32[]{:S(2)}) collective-permute-start(bf16[4,128,256]{2,1,0:T(8,128)(2,1)S(1)} %get-tuple-element.39.refs_0_), channel_id=1, source_target_pairs={{0,12},{1,13},{2,14},{3,15},{4,8},{5,9},{6,10},{7,11},{8,4},{9,5},... | collective-permute-start | bytes 786440 | tf_op jit(solution)/shard_map/ppermute | solution.py:60
  24.2 0.0 collective-permute-start.3
  24.3 4.7 %collective-permute-done.10.refs_1_ = bf16[4,128,256]{2,1,0:T(8,128)(2,1)S(1)} collective-permute-done((bf16[4,128,256]{2,1,0:T(8,128)(2,1)S(1)}, bf16[4,128,256]{2,1,0:T(8,128)(2,1)S(1)}, u32[]{:S(2)}, u32[]{:S(2)}) %collective-permute-start.10) | collective-permute-done | bytes 262176 | tf_op jit(solution)/shard_map/ppermute | solution.py:60
  29.0 0.0 copy-start
  29.0 0.0 copy-start.1
  29.1 0.0 copy-start.2
  29.1 0.1 collective-permute-start.11
  29.2 0.0 collective-permute-done.6.refs_1_
  29.2 2.1 %collective-permute-start.7 = (bf16[8,128,256]{2,1,0:T(8,128)(2,1)S(1)}, bf16[8,128,256]{2,1,0:T(8,128)(2,1)S(1)}, u32[]{:S(2)}, u32[]{:S(2)}) collective-permute-start(bf16[8,128,256]{2,1,0:T(8,128)(2,1)S(1)} %shard_map.80.t1), channel_id=1, source_target_pairs={{0,3},{1,2},{2,1},{3,0},{4,7},{5,6},{6,5},{7,4},{8,11},{9,10},{10,... | collective-permute-start | bytes 1572872 | tf_op jit(solution)/shard_map/ppermute | solution.py:60
  31.3 1.6 %collective-permute-start.12 = (bf16[8,128,256]{2,1,0:T(8,128)(2,1)S(1)}, bf16[8,128,256]{2,1,0:T(8,128)(2,1)S(1)}, u32[]{:S(2)}, u32[]{:S(2)}) collective-permute-start(bf16[8,128,256]{2,1,0:T(8,128)(2,1)S(1)} %get-tuple-element.42.refs_0_), channel_id=1, source_target_pairs={{0,32},{16,48},{32,0},{48,16},{64,96},{80,112},{96,64},{112,80},{1... | collective-permute-start | bytes 1572872 | tf_op jit(solution)/shard_map/ppermute | solution.py:358
  32.9 0.0 collective-permute-done.8.refs_1_
  32.9 0.1 collective-permute-start.9
  33.0 0.0 collective-permute-done.3.refs_1_
  33.1 2.7 %collective-permute-start.4 = (bf16[8,128,256]{2,1,0:T(8,128)(2,1)S(1)}, bf16[8,128,256]{2,1,0:T(8,128)(2,1)S(1)}, u32[]{:S(2)}, u32[]{:S(2)}) collective-permute-start(bf16[8,128,256]{2,1,0:T(8,128)(2,1)S(1)} %shard_map.77.t0), channel_id=1, source_target_pairs={{0,12},{1,13},{2,14},{3,15},{4,8},{5,9},{6,10},{7,11},{8,4},{9,5},... | collective-permute-start | bytes 1572872 | tf_op jit(solution)/shard_map/ppermute | solution.py:60
  35.8 0.0 copy-done
  35.8 0.0 copy-done.1
  35.8 0.0 copy-done.2
  35.8 1.3 %shard_map.83.raw_ref = f32[1024,384]{1,0:T(8,128)S(1)} custom-call(bf16[8,128,256]{2,1,0:T(8,128)(2,1)S(1)} %shard_map.77.t0, bf16[8,128,256]{2,1,0:T(8,128)(2,1)S(1)} %shard_map.80.t1, bf16[8,128,256]{2,1,0:T(8,128)(2,1)S(1)} %shard_map.81.t2, bf16[8,128,256]{2,1,0:T(8,128)(2,1)S(1)} %shard_map.82.t3, bf16[2048,128]{1,0:T(8,128)(2,1)S(1)} %copy-done, ...), custom_call_target="tpu_custom_call" | custom-call | flops 805306368 | bytes 5242880 | tf_op jit(solution)/shard_map/pallas_call | solution.py:362
  37.1 0.0 copy-start.6
  37.1 1.3 %collective-permute-done.11.t3 = bf16[8,128,256]{2,1,0:T(8,128)(2,1)S(1)} collective-permute-done((bf16[8,128,256]{2,1,0:T(8,128)(2,1)S(1)}, bf16[8,128,256]{2,1,0:T(8,128)(2,1)S(1)}, u32[]{:S(2)}, u32[]{:S(2)}) %collective-permute-start.11) | collective-permute-done | bytes 524320 | tf_op jit(solution)/shard_map/ppermute | solution.py:60
  38.4 1.3 %collective-permute-done.7.t1 = bf16[8,128,256]{2,1,0:T(8,128)(2,1)S(1)} collective-permute-done((bf16[8,128,256]{2,1,0:T(8,128)(2,1)S(1)}, bf16[8,128,256]{2,1,0:T(8,128)(2,1)S(1)}, u32[]{:S(2)}, u32[]{:S(2)}) %collective-permute-start.7) | collective-permute-done | bytes 524320 | tf_op jit(solution)/shard_map/ppermute | solution.py:60
  39.7 0.8 collective-permute-done.12.refs_1_
  40.5 2.2 %collective-permute-done.9.t2 = bf16[8,128,256]{2,1,0:T(8,128)(2,1)S(1)} collective-permute-done((bf16[8,128,256]{2,1,0:T(8,128)(2,1)S(1)}, bf16[8,128,256]{2,1,0:T(8,128)(2,1)S(1)}, u32[]{:S(2)}, u32[]{:S(2)}) %collective-permute-start.9) | collective-permute-done | bytes 524320 | tf_op jit(solution)/shard_map/ppermute | solution.py:60
  42.7 0.9 %collective-permute-done.4.t0 = bf16[8,128,256]{2,1,0:T(8,128)(2,1)S(1)} collective-permute-done((bf16[8,128,256]{2,1,0:T(8,128)(2,1)S(1)}, bf16[8,128,256]{2,1,0:T(8,128)(2,1)S(1)}, u32[]{:S(2)}, u32[]{:S(2)}) %collective-permute-start.4) | collective-permute-done | bytes 524320 | tf_op jit(solution)/shard_map/ppermute | solution.py:60
  43.6 0.1 shard_map.89.refs_0_
  43.6 0.1 collective-permute-start.16
  43.7 0.9 %collective-permute-start.17 = (bf16[16,128,256]{2,1,0:T(8,128)(2,1)S(1)}, bf16[16,128,256]{2,1,0:T(8,128)(2,1)S(1)}, u32[]{:S(2)}, u32[]{:S(2)}) collective-permute-start(bf16[16,128,256]{2,1,0:T(8,128)(2,1)S(1)} %shard_map.89.refs_0_), channel_id=1, source_target_pairs={{0,4},{1,5},{2,6},{3,7},{4,0},{5,1},{6,2},{7,3},{8,12},{9,13},{10,... | collective-permute-start | bytes 3145736 | tf_op jit(solution)/shard_map/ppermute | solution.py:60
  44.6 0.0 copy-done.6
  44.6 4.7 %shard_map.84 = (bf16[1024,128]{1,0:T(8,128)(2,1)S(1)}, bf16[1024,128]{1,0:T(8,128)(2,1)S(1)}, bf16[1024,256]{1,0:T(8,128)(2,1)S(1)}, bf16[8,128,256]{2,1,0:T(8,...) custom-call(f32[1024,384]{1,0:T(8,128)S(1)} %shard_map.83.raw_ref, ...), custom_call_target="tpu_custom_call" | custom-call | flops 3221225472 | bytes 8388608 | tf_op jit(solution)/shard_map/pallas_call | solution.py:370
  49.3 0.0 copy-start.5
  49.3 0.0 collective-permute-done.16.refs_1_
  49.3 1.3 %collective-permute-start.18 = (bf16[16,128,256]{2,1,0:T(8,128)(2,1)S(1)}, bf16[16,128,256]{2,1,0:T(8,128)(2,1)S(1)}, u32[]{:S(2)}, u32[]{:S(2)}) collective-permute-start(bf16[16,128,256]{2,1,0:T(8,128)(2,1)S(1)} %collective-permute-done.16.refs_1_), channel_id=1, source_target_pairs={{0,4},{1,5},{2,6},{3,7},{4,0},{5,1},{6,2},{7,3},{8,12},{9,13},{10,... | collective-permute-start | bytes 3145736 | tf_op jit(solution)/shard_map/ppermute | solution.py:60
  50.6 1.1 %collective-permute-start.13 = (bf16[128,256]{1,0:T(8,128)(2,1)S(1)}, bf16[128,256]{1,0:T(8,128)(2,1)S(1)}, u32[]{:S(2)}, u32[]{:S(2)}) collective-permute-start(bf16[128,256]{1,0:T(8,128)(2,1)S(1)} %get-tuple-element.49), channel_id=1, source_target_pairs={{0,16},{16,0},{32,48},{48,32},{64,80},{80,64},{96,112},{112,96},{1... | collective-permute-start | bytes 196616 | tf_op jit(solution)/shard_map/ppermute | solution.py:393
  51.7 0.9 %collective-permute-done.13.other_ref.core_ref = bf16[128,256]{1,0:T(8,128)(2,1)S(1)} collective-permute-done((bf16[128,256]{1,0:T(8,128)(2,1)S(1)}, bf16[128,256]{1,0:T(8,128)(2,1)S(1)}, u32[]{:S(2)}, u32[]{:S(2)}) %collective-permute-start.13) | collective-permute-done | bytes 65568 | tf_op jit(solution)/shard_map/ppermute | solution.py:393
  52.6 0.2 shard_map.85.mine_ref
  52.7 0.5 collective-permute-start.14
  53.3 1.5 %shard_map.86 = (bf16[1024,128]{1,0:T(8,128)(2,1)S(1)}, f32[1024,128]{1,0:T(8,128)S(1)}) custom-call(bf16[1024,128]{1,0:T(8,128)(2,1)S(1)} %get-tuple-element.50.q_ref, bf16[1024,128]{1,0:T(8,128)(2,1)S(1)} %get-tuple-element.51.k_ref, bf16[1024,256]{1,0:T(8,128)(2,1)S(1)} %get-tuple-element.52.wu_ref, bf16[8,128,256]{2,1,0:T(8,128)(2,1)S(1)} %get-tuple-element.53.states_ref), custom_call_target="tpu_custom_call" | custom-call | flops 536870912 | bytes 4194304 | tf_op jit(solution)/shard_map/pallas_call | solution.py:384
  54.7 2.4 %collective-permute-done.14.other_ref.chip_ref = bf16[128,256]{1,0:T(8,128)(2,1)S(1)} collective-permute-done((bf16[128,256]{1,0:T(8,128)(2,1)S(1)}, bf16[128,256]{1,0:T(8,128)(2,1)S(1)}, u32[]{:S(2)}, u32[]{:S(2)}) %collective-permute-start.14) | collective-permute-done | bytes 65568 | tf_op jit(solution)/shard_map/ppermute | solution.py:397
  57.2 0.1 shard_map.87
  57.3 2.2 %collective-permute-start.15 = (bf16[128,128]{1,0:T(8,128)(2,1)S(1)}, bf16[128,128]{1,0:T(8,128)(2,1)S(1)}, u32[]{:S(2)}, u32[]{:S(2)}) collective-permute-start(bf16[128,128]{1,0:T(8,128)(2,1)S(1)} %shard_map.87), channel_id=1, source_target_pairs={{0,96},{16,112},{32,64},{48,80},{64,32},{80,48},{96,0},{112,16},{1... | collective-permute-start | bytes 98312 | tf_op jit(solution)/shard_map/ppermute | solution.py:400
  59.5 3.0 %collective-permute-done.15.pair_ref = bf16[128,128]{1,0:T(8,128)(2,1)S(1)} collective-permute-done((bf16[128,128]{1,0:T(8,128)(2,1)S(1)}, bf16[128,128]{1,0:T(8,128)(2,1)S(1)}, u32[]{:S(2)}, u32[]{:S(2)}) %collective-permute-start.15) | collective-permute-done | bytes 32800 | tf_op jit(solution)/shard_map/ppermute | solution.py:400
  62.5 0.6 shard_map.88
  63.1 11.8 %all_to_all.9.x_ref = bf16[8,128,128]{2,1,0:T(8,128)(2,1)S(1)} all-to-all(bf16[8,128,128]{2,1,0:T(8,128)(2,1)S(1)} %bitcast.3), channel_id=1, replica_groups={{0,1,2,3,4,5,6,7},{8,9,10,11,12,13,14,15},{16,17,18,19,28,29,30,31},{20..., dimensions={0} | all-to-all | bytes 524288 | tf_op jit(solution)/shard_map/all_to_all | solution.py:410
  74.9 0.0 collective-permute-done.17.refs_2_
  74.9 0.0 collective-permute-done.18.refs_3_
  74.9 0.8 %shard_map.91 = bf16[64,2048]{1,0:T(8,128)(2,1)S(1)} custom-call(bf16[8,128,128]{2,1,0:T(8,128)(2,1)S(1)} %all_to_all.9.x_ref, bf16[16,128,256]{2,1,0:T(8,128)(2,1)S(1)} %shard_map.89.refs_0_, bf16[16,128,256]{2,1,0:T(8,128)(2,1)S(1)} %collective-permute-done.16.refs_1_, bf16[16,128,256]{2,1,0:T(8,128)(2,1)S(1)} %collective-permute-done.17.refs_2_, ...), custom_call_target="tpu_custom_call" | custom-call | flops 268435456 | bytes 4194304 | tf_op jit(solution)/shard_map/pallas_call | solution.py:415
  75.7 2.9 %collective-permute-start.19 = (bf16[64,2048]{1,0:T(8,128)(2,1)S(1)}, bf16[64,2048]{1,0:T(8,128)(2,1)S(1)}, u32[]{:S(2)}, u32[]{:S(2)}) collective-permute-start(bf16[64,2048]{1,0:T(8,128)(2,1)S(1)} %shard_map.91), channel_id=1, source_target_pairs={{0,12},{1,13},{2,14},{3,15},{4,8},{5,9},{6,10},{7,11},{8,4},{9,5},... | collective-permute-start | bytes 786440 | tf_op jit(solution)/shard_map/ppermute | solution.py:60
  78.7 0.8 %shard_map.90.own_ref = f32[64,2048]{1,0:T(8,128)S(1)} custom-call(bf16[8,128,128]{2,1,0:T(8,128)(2,1)S(1)} %all_to_all.9.x_ref, bf16[16,128,256]{2,1,0:T(8,128)(2,1)S(1)} %shard_map.89.refs_0_, bf16[16,128,256]{2,1,0:T(8,128)(2,1)S(1)} %collective-permute-done.16.refs_1_, bf16[16,128,256]{2,1,0:T(8,128)(2,1)S(1)} %collective-permute-done.17.refs_2_, ...), custom_call_target="tpu_custom_call" | custom-call | flops 268435456 | bytes 4194304 | tf_op jit(solution)/shard_map/pallas_call | solution.py:419
  79.5 3.9 %collective-permute-done.19.other_ref = bf16[64,2048]{1,0:T(8,128)(2,1)S(1)} collective-permute-done((bf16[64,2048]{1,0:T(8,128)(2,1)S(1)}, bf16[64,2048]{1,0:T(8,128)(2,1)S(1)}, u32[]{:S(2)}, u32[]{:S(2)}) %collective-permute-start.19) | collective-permute-done | bytes 262176 | tf_op jit(solution)/shard_map/ppermute | solution.py:60
  83.4 0.7 shard_map.92
  (11 shorter events, 0.3 us)
Async XLA Ops:
  0.0 0.9 %copy-start.4 = (bf16[1024,128]{1,0:T(8,128)(2,1)S(1)}, bf16[1024,128]{1,0:T(8,128)(2,1)}, u32[]{:S(2)}) copy-start(bf16[1024,128]{1,0:T(8,128)(2,1)} %tokens_ref.1) | copy-start | bytes 786436
  1.0 1.0 %copy-start.3 = (bf16[128,2048]{1,0:T(8,128)(2,1)S(1)}, bf16[128,2048]{1,0:T(8,128)(2,1)}, u32[]{:S(2)}) copy-start(bf16[128,2048]{1,0:T(8,128)(2,1)} %w_ref.1) | copy-start | bytes 1572868
  2.1 6.6 %collective-permute-start = (bf16[4,128,256]{2,1,0:T(8,128)(2,1)S(1)}, bf16[4,128,256]{2,1,0:T(8,128)(2,1)S(1)}, u32[]{:S(2)}, u32[]{:S(2)}) collective-permute-start(bf16[4,128,256]{2,1,0:T(8,128)(2,1)S(1)} %shard_map.74.refs_0_), channel_id=1, source_target_pairs={{0,1},{1,0},{2,3},{3,2},{4,5},{5,4},{6,7},{7,6},{8,9},{9,8},{10,11... | collective-permute-start | bytes 786440 | tf_op jit(solution)/shard_map/ppermute | solution.py:60
  3.7 5.0 %collective-permute-start.1 = (bf16[2,128,256]{2,1,0:T(8,128)(2,1)S(1)}, bf16[2,128,256]{2,1,0:T(8,128)(2,1)S(1)}, u32[]{:S(2)}, u32[]{:S(2)}) collective-permute-start(bf16[2,128,256]{2,1,0:T(8,128)(2,1)S(1)} %get-tuple-element.34.refs_0_), channel_id=1, source_target_pairs={{0,4},{1,5},{2,6},{3,7},{4,0},{5,1},{6,2},{7,3},{8,12},{9,13},{10,... | collective-permute-start | bytes 393224 | tf_op jit(solution)/shard_map/ppermute | solution.py:60
  8.7 12.1 %collective-permute-start.2 = (bf16[8,128,256]{2,1,0:T(8,128)(2,1)S(1)}, bf16[8,128,256]{2,1,0:T(8,128)(2,1)S(1)}, u32[]{:S(2)}, u32[]{:S(2)}) collective-permute-start(bf16[8,128,256]{2,1,0:T(8,128)(2,1)S(1)} %shard_map.75.one_ref), channel_id=1, source_target_pairs={{0,3},{1,2},{2,1},{3,0},{4,7},{5,6},{6,5},{7,4},{8,11},{9,10},{10,... | collective-permute-start | bytes 1572872 | tf_op jit(solution)/shard_map/ppermute | solution.py:60
  11.5 8.5 %collective-permute-start.5 = (bf16[4,128,256]{2,1,0:T(8,128)(2,1)S(1)}, bf16[4,128,256]{2,1,0:T(8,128)(2,1)S(1)}, u32[]{:S(2)}, u32[]{:S(2)}) collective-permute-start(bf16[4,128,256]{2,1,0:T(8,128)(2,1)S(1)} %shard_map.78.one_ref), channel_id=1, source_target_pairs={{0,12},{1,13},{2,14},{3,15},{4,8},{5,9},{6,10},{7,11},{8,4},{9,5},... | collective-permute-start | bytes 786440 | tf_op jit(solution)/shard_map/ppermute | solution.py:60
  20.0 9.0 %collective-permute-start.10 = (bf16[4,128,256]{2,1,0:T(8,128)(2,1)S(1)}, bf16[4,128,256]{2,1,0:T(8,128)(2,1)S(1)}, u32[]{:S(2)}, u32[]{:S(2)}) collective-permute-start(bf16[4,128,256]{2,1,0:T(8,128)(2,1)S(1)} %get-tuple-element.40.refs_0_), channel_id=1, source_target_pairs={{0,3},{1,2},{2,1},{3,0},{4,7},{5,6},{6,5},{7,4},{8,11},{9,10},{10,... | collective-permute-start | bytes 786440 | tf_op jit(solution)/shard_map/ppermute | solution.py:60
  20.7 8.5 %collective-permute-start.6 = (bf16[4,128,256]{2,1,0:T(8,128)(2,1)S(1)}, bf16[4,128,256]{2,1,0:T(8,128)(2,1)S(1)}, u32[]{:S(2)}, u32[]{:S(2)}) collective-permute-start(bf16[4,128,256]{2,1,0:T(8,128)(2,1)S(1)} %get-tuple-element.38.refs_0_), channel_id=1, source_target_pairs={{0,1},{1,0},{2,3},{3,2},{4,5},{5,4},{6,7},{7,6},{8,9},{9,8},{10,11... | collective-permute-start | bytes 786440 | tf_op jit(solution)/shard_map/ppermute | solution.py:60
  20.9 12.0 %collective-permute-start.8 = (bf16[4,128,256]{2,1,0:T(8,128)(2,1)S(1)}, bf16[4,128,256]{2,1,0:T(8,128)(2,1)S(1)}, u32[]{:S(2)}, u32[]{:S(2)}) collective-permute-start(bf16[4,128,256]{2,1,0:T(8,128)(2,1)S(1)} %get-tuple-element.39.refs_0_), channel_id=1, source_target_pairs={{0,12},{1,13},{2,14},{3,15},{4,8},{5,9},{6,10},{7,11},{8,4},{9,5},... | collective-permute-start | bytes 786440 | tf_op jit(solution)/shard_map/ppermute | solution.py:60
  24.2 8.8 %collective-permute-start.3 = (bf16[4,128,256]{2,1,0:T(8,128)(2,1)S(1)}, bf16[4,128,256]{2,1,0:T(8,128)(2,1)S(1)}, u32[]{:S(2)}, u32[]{:S(2)}) collective-permute-start(bf16[4,128,256]{2,1,0:T(8,128)(2,1)S(1)} %get-tuple-element.36.refs_0_), channel_id=1, source_target_pairs={{0,4},{1,5},{2,6},{3,7},{4,0},{5,1},{6,2},{7,3},{8,12},{9,13},{10,... | collective-permute-start | bytes 786440 | tf_op jit(solution)/shard_map/ppermute | solution.py:60
  29.0 6.8 %copy-start = (bf16[2048,128]{1,0:T(8,128)(2,1)S(1)}, bf16[2048,128]{1,0:T(8,128)(2,1)}, u32[]{:S(2)}) copy-start(bf16[2048,128]{1,0:T(8,128)(2,1)} %wq.3) | copy-start | bytes 1572868
  29.0 6.8 %copy-start.1 = (bf16[2048,128]{1,0:T(8,128)(2,1)S(1)}, bf16[2048,128]{1,0:T(8,128)(2,1)}, u32[]{:S(2)}) copy-start(bf16[2048,128]{1,0:T(8,128)(2,1)} %wk.3) | copy-start | bytes 1572868
  29.1 6.8 %copy-start.2 = (bf16[2048,128]{1,0:T(8,128)(2,1)S(1)}, bf16[2048,128]{1,0:T(8,128)(2,1)}, u32[]{:S(2)}) copy-start(bf16[2048,128]{1,0:T(8,128)(2,1)} %wv.3) | copy-start | bytes 1572868
  29.1 9.3 %collective-permute-start.11 = (bf16[8,128,256]{2,1,0:T(8,128)(2,1)S(1)}, bf16[8,128,256]{2,1,0:T(8,128)(2,1)S(1)}, u32[]{:S(2)}, u32[]{:S(2)}) collective-permute-start(bf16[8,128,256]{2,1,0:T(8,128)(2,1)S(1)} %shard_map.82.t3), channel_id=1, source_target_pairs={{0,1},{1,0},{2,3},{3,2},{4,5},{5,4},{6,7},{7,6},{8,9},{9,8},{10,11... | collective-permute-start | bytes 1572872 | tf_op jit(solution)/shard_map/ppermute | solution.py:60
  29.2 10.5 %collective-permute-start.7 = (bf16[8,128,256]{2,1,0:T(8,128)(2,1)S(1)}, bf16[8,128,256]{2,1,0:T(8,128)(2,1)S(1)}, u32[]{:S(2)}, u32[]{:S(2)}) collective-permute-start(bf16[8,128,256]{2,1,0:T(8,128)(2,1)S(1)} %shard_map.80.t1), channel_id=1, source_target_pairs={{0,3},{1,2},{2,1},{3,0},{4,7},{5,6},{6,5},{7,4},{8,11},{9,10},{10,... | collective-permute-start | bytes 1572872 | tf_op jit(solution)/shard_map/ppermute | solution.py:60
  31.3 9.2 %collective-permute-start.12 = (bf16[8,128,256]{2,1,0:T(8,128)(2,1)S(1)}, bf16[8,128,256]{2,1,0:T(8,128)(2,1)S(1)}, u32[]{:S(2)}, u32[]{:S(2)}) collective-permute-start(bf16[8,128,256]{2,1,0:T(8,128)(2,1)S(1)} %get-tuple-element.42.refs_0_), channel_id=1, source_target_pairs={{0,32},{16,48},{32,0},{48,16},{64,96},{80,112},{96,64},{112,80},{1... | collective-permute-start | bytes 1572872 | tf_op jit(solution)/shard_map/ppermute | solution.py:358
  32.9 9.7 %collective-permute-start.9 = (bf16[8,128,256]{2,1,0:T(8,128)(2,1)S(1)}, bf16[8,128,256]{2,1,0:T(8,128)(2,1)S(1)}, u32[]{:S(2)}, u32[]{:S(2)}) collective-permute-start(bf16[8,128,256]{2,1,0:T(8,128)(2,1)S(1)} %shard_map.81.t2), channel_id=1, source_target_pairs={{0,4},{1,5},{2,6},{3,7},{4,0},{5,1},{6,2},{7,3},{8,12},{9,13},{10,... | collective-permute-start | bytes 1572872 | tf_op jit(solution)/shard_map/ppermute | solution.py:60
  33.1 10.5 %collective-permute-start.4 = (bf16[8,128,256]{2,1,0:T(8,128)(2,1)S(1)}, bf16[8,128,256]{2,1,0:T(8,128)(2,1)S(1)}, u32[]{:S(2)}, u32[]{:S(2)}) collective-permute-start(bf16[8,128,256]{2,1,0:T(8,128)(2,1)S(1)} %shard_map.77.t0), channel_id=1, source_target_pairs={{0,12},{1,13},{2,14},{3,15},{4,8},{5,9},{6,10},{7,11},{8,4},{9,5},... | collective-permute-start | bytes 1572872 | tf_op jit(solution)/shard_map/ppermute | solution.py:60
  37.1 7.5 %copy-start.6 = (f32[1024,1]{0,1:T(1,128)S(1)}, f32[1024,1]{0,1:T(1,128)}, u32[]{:S(2)}) copy-start(f32[1024,1]{0,1:T(1,128)} %param.8) | copy-start | bytes 12292
  43.6 5.7 %collective-permute-start.16 = (bf16[16,128,256]{2,1,0:T(8,128)(2,1)S(1)}, bf16[16,128,256]{2,1,0:T(8,128)(2,1)S(1)}, u32[]{:S(2)}, u32[]{:S(2)}) collective-permute-start(bf16[16,128,256]{2,1,0:T(8,128)(2,1)S(1)} %shard_map.89.refs_0_), channel_id=1, source_target_pairs={{0,16},{16,0},{32,48},{48,32},{64,80},{80,64},{96,112},{112,96},{1... | collective-permute-start | bytes 3145736 | tf_op jit(solution)/shard_map/ppermute | solution.py:368
  43.7 31.2 %collective-permute-start.17 = (bf16[16,128,256]{2,1,0:T(8,128)(2,1)S(1)}, bf16[16,128,256]{2,1,0:T(8,128)(2,1)S(1)}, u32[]{:S(2)}, u32[]{:S(2)}) collective-permute-start(bf16[16,128,256]{2,1,0:T(8,128)(2,1)S(1)} %shard_map.89.refs_0_), channel_id=1, source_target_pairs={{0,4},{1,5},{2,6},{3,7},{4,0},{5,1},{6,2},{7,3},{8,12},{9,13},{10,... | collective-permute-start | bytes 3145736 | tf_op jit(solution)/shard_map/ppermute | solution.py:60
  49.3 13.2 %copy-start.5 = (f32[128]{0:T(128)S(1)}, f32[128]{0:T(128)}, u32[]{:S(2)}) copy-start(f32[128]{0:T(128)} %param.12) | copy-start | bytes 1540
  49.3 25.6 %collective-permute-start.18 = (bf16[16,128,256]{2,1,0:T(8,128)(2,1)S(1)}, bf16[16,128,256]{2,1,0:T(8,128)(2,1)S(1)}, u32[]{:S(2)}, u32[]{:S(2)}) collective-permute-start(bf16[16,128,256]{2,1,0:T(8,128)(2,1)S(1)} %collective-permute-done.16.refs_1_), channel_id=1, source_target_pairs={{0,4},{1,5},{2,6},{3,7},{4,0},{5,1},{6,2},{7,3},{8,12},{9,13},{10,... | collective-permute-start | bytes 3145736 | tf_op jit(solution)/shard_map/ppermute | solution.py:60
  50.6 2.0 %collective-permute-start.13 = (bf16[128,256]{1,0:T(8,128)(2,1)S(1)}, bf16[128,256]{1,0:T(8,128)(2,1)S(1)}, u32[]{:S(2)}, u32[]{:S(2)}) collective-permute-start(bf16[128,256]{1,0:T(8,128)(2,1)S(1)} %get-tuple-element.49), channel_id=1, source_target_pairs={{0,16},{16,0},{32,48},{48,32},{64,80},{80,64},{96,112},{112,96},{1... | collective-permute-start | bytes 196616 | tf_op jit(solution)/shard_map/ppermute | solution.py:393
  52.7 4.4 %collective-permute-start.14 = (bf16[128,256]{1,0:T(8,128)(2,1)S(1)}, bf16[128,256]{1,0:T(8,128)(2,1)S(1)}, u32[]{:S(2)}, u32[]{:S(2)}) collective-permute-start(bf16[128,256]{1,0:T(8,128)(2,1)S(1)} %shard_map.85.mine_ref), channel_id=1, source_target_pairs={{0,32},{16,48},{32,0},{48,16},{64,96},{80,112},{96,64},{112,80},{1... | collective-permute-start | bytes 196616 | tf_op jit(solution)/shard_map/ppermute | solution.py:397
  57.3 5.2 %collective-permute-start.15 = (bf16[128,128]{1,0:T(8,128)(2,1)S(1)}, bf16[128,128]{1,0:T(8,128)(2,1)S(1)}, u32[]{:S(2)}, u32[]{:S(2)}) collective-permute-start(bf16[128,128]{1,0:T(8,128)(2,1)S(1)} %shard_map.87), channel_id=1, source_target_pairs={{0,96},{16,112},{32,64},{48,80},{64,32},{80,48},{96,0},{112,16},{1... | collective-permute-start | bytes 98312 | tf_op jit(solution)/shard_map/ppermute | solution.py:400
  75.7 7.7 %collective-permute-start.19 = (bf16[64,2048]{1,0:T(8,128)(2,1)S(1)}, bf16[64,2048]{1,0:T(8,128)(2,1)S(1)}, u32[]{:S(2)}, u32[]{:S(2)}) collective-permute-start(bf16[64,2048]{1,0:T(8,128)(2,1)S(1)} %shard_map.91), channel_id=1, source_target_pairs={{0,12},{1,13},{2,14},{3,15},{4,8},{5,9},{6,10},{7,11},{8,4},{9,5},... | collective-permute-start | bytes 786440 | tf_op jit(solution)/shard_map/ppermute | solution.py:60

commit v4 on v3

--- a/solution.py
+++ b/solution.py
@@ -149,8 +149,8 @@
 
 
 def transition_kernel(
-    raw_ref, t0, t1, t2, t3, wq, wk, wv, beta_ref,
-    q_ref, k_ref, wu_ref, states_ref, last_ref, sent_ref, total_ref,
+    raw_ref, t0, t1, t2, t3, wk, wv, beta_ref,
+    k_ref, wu_ref, states_ref, last_ref, sent_ref, total_ref,
 ):
     rows = raw_ref.shape[0]
     count = rows // CHUNK
@@ -158,7 +158,7 @@
     for i, pieces in enumerate((t0, t1, t2, t3)):
         part = slice(i * 256, (i + 1) * 256)
         heads = place.piece_heads(STREAMS[i])[8:]
-        total_ref[part, :] = raw_ref[part, :] + project_part(heads, pieces, (wq, wk, wv))
+        total_ref[part, :] = raw_ref[part, DK:] + project_part(heads, pieces, (wk, wv))
     row = lax.broadcasted_iota(jnp.int32, (CHUNK, CHUNK), 0)
     col = lax.broadcasted_iota(jnp.int32, (CHUNK, CHUNK), 1)
     eye = (row == col).astype(F32)
@@ -171,8 +171,7 @@
     keys, rates, lowers, inverses = [], [], [], []
     for b in range(count):
         part = slice(b * CHUNK, (b + 1) * CHUNK)
-        q_ref[part, :] = unit_silu(total_ref[part, :DK]).astype(BF16)
-        key = unit_silu(total_ref[part, DK : 2 * DK])
+        key = unit_silu(total_ref[part, :DK])
         key16 = key.astype(BF16)
         k_ref[part, :] = key16
         rate = jnp.transpose(jnp.broadcast_to(beta_ref[b : b + 1, :], (CHUNK, CHUNK)))
@@ -191,36 +190,52 @@
     maps = []
     for b in range(count):
         part = slice(b * CHUNK, (b + 1) * CHUNK)
-        value = total_ref[part, 2 * DK :]
+        value = total_ref[part, DK:]
         both = jnp.concatenate([rates[b] * keys[b], rates[b] * value], axis=1)
         wu = dot(inverses[b], both).astype(BF16)
         wu_ref[part, :] = wu
         maps.append(dot(k_ref[part, :], wu, ((0,), (0,))))
     zeros = jnp.zeros((DK, DK), F32)
-    state = jnp.concatenate([eye, zeros], axis=1)
-    for b in range(count):
-        state16 = state.astype(BF16)
-        states_ref[b] = state16
-        state = (
-            state
-            - dot(maps[b][:, :DK], state16)
-            + jnp.concatenate([zeros, maps[b][:, DK:]], axis=1)
-        )
-    last_ref[...] = state
-    sent_ref[...] = state.astype(BF16)
-
-
-def outputs_kernel(q_ref, k_ref, wu_ref, states_ref, query_ref, out_ref):
-    rows = q_ref.shape[0]
+    half = count // 2
+    states = [jnp.concatenate([eye, zeros], axis=1)] * 2
+    for b in range(half):
+        for side in range(2):
+            chunk = side * half + b
+            state16 = states[side].astype(BF16)
+            states_ref[chunk] = states[side]
+            states[side] = (
+                states[side]
+                - dot(maps[chunk][:, :DK], state16)
+                + jnp.concatenate([zeros, maps[chunk][:, DK:]], axis=1)
+            )
+    states_ref[count] = states[0]
+    last = compose(states[1], states[0])
+    last_ref[...] = last
+    sent_ref[...] = last.astype(BF16)
+
+
+def outputs_kernel(
+    raw_ref, t0, t1, t2, t3, wq, k_ref, wu_ref, states_ref, query_ref, out_ref, total_ref
+):
+    rows = raw_ref.shape[0]
+    count = rows // CHUNK
+    place = Place()
+    for i, pieces in enumerate((t0, t1, t2, t3)):
+        part = slice(i * 256, (i + 1) * 256)
+        heads = place.piece_heads(STREAMS[i])[8:]
+        total_ref[part, :] = raw_ref[part, :DK] + project_part(heads, pieces, (wq,))
     row = lax.broadcasted_iota(jnp.int32, (CHUNK, CHUNK), 0)
     col = lax.broadcasted_iota(jnp.int32, (CHUNK, CHUNK), 1)
-    for b in range(rows // CHUNK):
+    for b in range(count):
         part = slice(b * CHUNK, (b + 1) * CHUNK)
-        query = q_ref[part, :]
+        query = unit_silu(total_ref[part, :])
         scores = jnp.where(row >= col, dot(query, k_ref[part, :], ((1,), (1,))), 0.0)
         local = dot(scores, wu_ref[part, :])
-        effective = query.astype(F32) - local[:, :DK]
-        result = dot(effective, states_ref[b])
+        effective = query - local[:, :DK]
+        state = states_ref[b]
+        if b >= count // 2:
+            state = compose(state, states_ref[count])
+        result = dot(effective, state)
         query_ref[part, :] = result[:, :DK].astype(BF16)
         out_ref[part, :] = result[:, DK:] + local[:, DK:]
 
@@ -367,26 +382,26 @@
     far_a = swap(w, (4, 12), ctx, heads)
     w_next = lax.ppermute(w, "ctx", other_core)
 
-    query, key, wu, states, last, sent = call(
+    key, wu, states, last, sent = call(
         transition_kernel,
         (
             struct((rows, DK), BF16),
-            struct((rows, DK), BF16),
             struct((rows, 2 * DK), BF16),
-            struct((rows // CHUNK, DK, 2 * DK), BF16),
+            struct((rows // CHUNK + 1, DK, 2 * DK), F32),
             struct((DK, 2 * DK), F32),
             struct((DK, 2 * DK), BF16),
         ),
-        9,
-        scratch=[pltpu.VMEM((rows, 3 * DK), F32)],
+        8,
+        scratch=[pltpu.VMEM((rows, 2 * DK), F32)],
         flops=rows * 4096 * 768, size=8 << 20,
-    )(raw, *arrived, *weights, beta.reshape(rows // CHUNK, CHUNK))
+    )(raw, *arrived, w_key, w_value, beta.reshape(rows // CHUNK, CHUNK))
     eff_query, partial = call(
         outputs_kernel,
         (struct((rows, DK), BF16), struct((rows, DK), F32)),
-        4,
+        9,
+        scratch=[pltpu.VMEM((rows, DK), F32)],
         flops=rows * 2048 * 256, size=4 << 20,
-    )(query, key, wu, states)
+    )(raw, *arrived, w_query, key, wu, states)
 
     _, w_next = lax.optimization_barrier((sent, w_next))
     far_b = swap(w_next, (4, 12), ctx, heads)

time: 84.4 us -> 83.2 us (0.986)
  blocking collectives: 11.8 us -> 10.2 us
  starting transfers between devices: 30.2 us -> 31.4 us
    ppermute x15, waiting for transfers between devices: 21.7 us -> 24.3 us  [swap(): return lax.ppermute(value, ('ctx', 'head'), pairs)]
    ppermute x1, waiting for transfers between devices: 2.41 us -> 0.61 us  [local(): of_chip = lax.ppermute(chip, 'ctx', [(c, c ^ 2) for c in range(ctx)])]
    all_to_all x1, blocking collectives: 11.8 us -> 10.2 us  [local(): lax.all_to_all(normed, ('ctx', 'head'), 0, 0, tiled=True, axis_index_grou...]
    ppermute x1, starting transfers between devices: 0.53 us -> 1.65 us  [local(): of_chip = lax.ppermute(chip, 'ctx', [(c, c ^ 2) for c in range(ctx)])]
    pallas_call x1, Pallas kernels: 4.65 us -> 3.81 us  [local(): call(transition_kernel, (struct((rows, DK), BF16), struct((rows, 2 * DK),...]
  transfers between devices with their start and end apart: 20 -> 20, of which waited for: 12 -> 11; matrix products, arithmetic and copies ran while one was open for 0% -> 0% of each run, Pallas kernels for 11% -> 11%
where the time goes in v4:
time: 83.2 us; the launch traced here: 82.9 us
  starting transfers between devices  31.4 us (38%)
  waiting for transfers between devices  28.1 us (34%)
  Pallas kernels  11 us (13%)
  blocking collectives  10.2 us (12%)
  local copies, waits for them, and re-layouts  2.02 us (2%)
    ppermute x15, waiting for transfers between devices, swap(): return lax.ppermute(value, ('ctx', 'head'), pairs)  24.3 us
    ppermute x15, starting transfers between devices, swap(): return lax.ppermute(value, ('ctx', 'head'), pairs)  24 us
    all_to_all x1, blocking collectives, local(): lax.all_to_all(normed, ('ctx', 'head'), 0, 0, tiled=True, axis_index_grou...  10.2 us
    pallas_call x1, Pallas kernels, local(): call(transition_kernel, (struct((rows, DK), BF16), struct((rows, 2 * DK),...  3.81 us
    ppermute x1, starting transfers between devices, local(): of_pair = lax.ppermute(pair, 'ctx', [(c, c ^ 6) for c in range(ctx)])  3.06 us
    pallas_call x1, Pallas kernels, local(): call(outputs_kernel, (struct((rows, DK), BF16), struct((rows, DK), F32)),...  2.17 us
    ppermute x1, waiting for transfers between devices, local(): of_pair = lax.ppermute(pair, 'ctx', [(c, c ^ 6) for c in range(ctx)])  2.12 us
    unnamed x14, local copies, waits for them, and re-layouts  2.02 us
  transfers between devices with their start and end apart: 20, of which 11 were waited for; matrix products, arithmetic and copies ran while one was open for 0% of the time, Pallas kernels for 11%

profile of v4, /device:TPU:0, one launch (start us, length us, event | category | flops | bytes accessed | tf_op | source)
XLA Modules:
  0.0 82.9 jit_solution(5990038916287841198)
XLA Ops:
  0.0 0.9 %copy-done.4 = bf16[1024,128]{1,0:T(8,128)(2,1)S(1)} copy-done((bf16[1024,128]{1,0:T(8,128)(2,1)S(1)}, bf16[1024,128]{1,0:T(8,128)(2,1)}, u32[]{:S(2)}) %copy-start.4) | copy-done | bytes 262168
  1.0 0.0 copy-start.3
  1.0 1.0 %copy-done.3 = bf16[128,2048]{1,0:T(8,128)(2,1)S(1)} copy-done((bf16[128,2048]{1,0:T(8,128)(2,1)S(1)}, bf16[128,2048]{1,0:T(8,128)(2,1)}, u32[]{:S(2)}) %copy-start.3) | copy-done | bytes 524312
  2.1 1.7 %collective-permute-start = (bf16[4,128,256]{2,1,0:T(8,128)(2,1)S(1)}, bf16[4,128,256]{2,1,0:T(8,128)(2,1)S(1)}, u32[]{:S(2)}, u32[]{:S(2)}) collective-permute-start(bf16[4,128,256]{2,1,0:T(8,128)(2,1)S(1)} %shard_map.74.refs_0_), channel_id=1, source_target_pairs={{0,1},{1,0},{2,3},{3,2},{4,5},{5,4},{6,7},{7,6},{8,9},{9,8},{10,11... | collective-permute-start | bytes 786440 | tf_op jit(solution)/shard_map/ppermute | solution.py:60
  3.7 1.9 %collective-permute-start.1 = (bf16[2,128,256]{2,1,0:T(8,128)(2,1)S(1)}, bf16[2,128,256]{2,1,0:T(8,128)(2,1)S(1)}, u32[]{:S(2)}, u32[]{:S(2)}) collective-permute-start(bf16[2,128,256]{2,1,0:T(8,128)(2,1)S(1)} %get-tuple-element.33.refs_0_), channel_id=1, source_target_pairs={{0,4},{1,5},{2,6},{3,7},{4,0},{5,1},{6,2},{7,3},{8,12},{9,13},{10,... | collective-permute-start | bytes 393224 | tf_op jit(solution)/shard_map/ppermute | solution.py:60
  5.7 3.0 %collective-permute-done.1.refs_1_ = bf16[2,128,256]{2,1,0:T(8,128)(2,1)S(1)} collective-permute-done((bf16[2,128,256]{2,1,0:T(8,128)(2,1)S(1)}, bf16[2,128,256]{2,1,0:T(8,128)(2,1)S(1)}, u32[]{:S(2)}, u32[]{:S(2)}) %collective-permute-start.1) | collective-permute-done | bytes 131104 | tf_op jit(solution)/shard_map/ppermute | solution.py:60
  8.7 0.0 collective-permute-done.refs_1_
  8.7 2.7 %collective-permute-start.2 = (bf16[8,128,256]{2,1,0:T(8,128)(2,1)S(1)}, bf16[8,128,256]{2,1,0:T(8,128)(2,1)S(1)}, u32[]{:S(2)}, u32[]{:S(2)}) collective-permute-start(bf16[8,128,256]{2,1,0:T(8,128)(2,1)S(1)} %shard_map.75.one_ref), channel_id=1, source_target_pairs={{0,3},{1,2},{2,1},{3,0},{4,7},{5,6},{6,5},{7,4},{8,11},{9,10},{10,... | collective-permute-start | bytes 1572872 | tf_op jit(solution)/shard_map/ppermute | solution.py:60
  11.5 4.1 %collective-permute-start.5 = (bf16[4,128,256]{2,1,0:T(8,128)(2,1)S(1)}, bf16[4,128,256]{2,1,0:T(8,128)(2,1)S(1)}, u32[]{:S(2)}, u32[]{:S(2)}) collective-permute-start(bf16[4,128,256]{2,1,0:T(8,128)(2,1)S(1)} %shard_map.78.one_ref), channel_id=1, source_target_pairs={{0,12},{1,13},{2,14},{3,15},{4,8},{5,9},{6,10},{7,11},{8,4},{9,5},... | collective-permute-start | bytes 786440 | tf_op jit(solution)/shard_map/ppermute | solution.py:60
  15.6 4.4 %collective-permute-done.5.two_ref = bf16[4,128,256]{2,1,0:T(8,128)(2,1)S(1)} collective-permute-done((bf16[4,128,256]{2,1,0:T(8,128)(2,1)S(1)}, bf16[4,128,256]{2,1,0:T(8,128)(2,1)S(1)}, u32[]{:S(2)}, u32[]{:S(2)}) %collective-permute-start.5) | collective-permute-done | bytes 262176 | tf_op jit(solution)/shard_map/ppermute | solution.py:60
  20.0 0.3 collective-permute-start.6
  20.3 1.1 %collective-permute-start.10 = (bf16[4,128,256]{2,1,0:T(8,128)(2,1)S(1)}, bf16[4,128,256]{2,1,0:T(8,128)(2,1)S(1)}, u32[]{:S(2)}, u32[]{:S(2)}) collective-permute-start(bf16[4,128,256]{2,1,0:T(8,128)(2,1)S(1)} %get-tuple-element.39.refs_0_), channel_id=1, source_target_pairs={{0,3},{1,2},{2,1},{3,0},{4,7},{5,6},{6,5},{7,4},{8,11},{9,10},{10,... | collective-permute-start | bytes 786440 | tf_op jit(solution)/shard_map/ppermute | solution.py:60
  21.5 0.0 collective-permute-done.2.two_ref
  21.5 0.1 shard_map.76
  21.5 0.2 collective-permute-start.3
  21.7 3.2 %collective-permute-start.8 = (bf16[4,128,256]{2,1,0:T(8,128)(2,1)S(1)}, bf16[4,128,256]{2,1,0:T(8,128)(2,1)S(1)}, u32[]{:S(2)}, u32[]{:S(2)}) collective-permute-start(bf16[4,128,256]{2,1,0:T(8,128)(2,1)S(1)} %get-tuple-element.38.refs_0_), channel_id=1, source_target_pairs={{0,12},{1,13},{2,14},{3,15},{4,8},{5,9},{6,10},{7,11},{8,4},{9,5},... | collective-permute-start | bytes 786440 | tf_op jit(solution)/shard_map/ppermute | solution.py:60
  24.9 2.2 %collective-permute-done.6.refs_1_ = bf16[4,128,256]{2,1,0:T(8,128)(2,1)S(1)} collective-permute-done((bf16[4,128,256]{2,1,0:T(8,128)(2,1)S(1)}, bf16[4,128,256]{2,1,0:T(8,128)(2,1)S(1)}, u32[]{:S(2)}, u32[]{:S(2)}) %collective-permute-start.6) | collective-permute-done | bytes 262176 | tf_op jit(solution)/shard_map/ppermute | solution.py:60
  27.2 0.0 copy-start
  27.2 0.0 copy-start.1
  27.2 0.0 copy-start.2
  27.2 1.0 %collective-permute-start.7 = (bf16[8,128,256]{2,1,0:T(8,128)(2,1)S(1)}, bf16[8,128,256]{2,1,0:T(8,128)(2,1)S(1)}, u32[]{:S(2)}, u32[]{:S(2)}) collective-permute-start(bf16[8,128,256]{2,1,0:T(8,128)(2,1)S(1)} %shard_map.80.t1), channel_id=1, source_target_pairs={{0,3},{1,2},{2,1},{3,0},{4,7},{5,6},{6,5},{7,4},{8,11},{9,10},{10,... | collective-permute-start | bytes 1572872 | tf_op jit(solution)/shard_map/ppermute | solution.py:60
  28.3 0.2 collective-permute-done.10.refs_1_
  28.5 1.2 %collective-permute-start.11 = (bf16[8,128,256]{2,1,0:T(8,128)(2,1)S(1)}, bf16[8,128,256]{2,1,0:T(8,128)(2,1)S(1)}, u32[]{:S(2)}, u32[]{:S(2)}) collective-permute-start(bf16[8,128,256]{2,1,0:T(8,128)(2,1)S(1)} %shard_map.82.t3), channel_id=1, source_target_pairs={{0,1},{1,0},{2,3},{3,2},{4,5},{5,4},{6,7},{7,6},{8,9},{9,8},{10,11... | collective-permute-start | bytes 1572872 | tf_op jit(solution)/shard_map/ppermute | solution.py:60
  29.7 1.6 %collective-permute-start.12 = (bf16[8,128,256]{2,1,0:T(8,128)(2,1)S(1)}, bf16[8,128,256]{2,1,0:T(8,128)(2,1)S(1)}, u32[]{:S(2)}, u32[]{:S(2)}) collective-permute-start(bf16[8,128,256]{2,1,0:T(8,128)(2,1)S(1)} %get-tuple-element.41.refs_0_), channel_id=1, source_target_pairs={{0,32},{16,48},{32,0},{48,16},{64,96},{80,112},{96,64},{112,80},{1... | collective-permute-start | bytes 1572872 | tf_op jit(solution)/shard_map/ppermute | solution.py:373
  31.3 0.0 collective-permute-done.3.refs_1_
  31.4 3.0 %collective-permute-start.4 = (bf16[8,128,256]{2,1,0:T(8,128)(2,1)S(1)}, bf16[8,128,256]{2,1,0:T(8,128)(2,1)S(1)}, u32[]{:S(2)}, u32[]{:S(2)}) collective-permute-start(bf16[8,128,256]{2,1,0:T(8,128)(2,1)S(1)} %shard_map.77.t0), channel_id=1, source_target_pairs={{0,12},{1,13},{2,14},{3,15},{4,8},{5,9},{6,10},{7,11},{8,4},{9,5},... | collective-permute-start | bytes 1572872 | tf_op jit(solution)/shard_map/ppermute | solution.py:60
  34.4 0.0 collective-permute-done.8.refs_1_
  34.4 0.1 collective-permute-start.9
  34.5 0.0 copy-done
  34.5 0.0 copy-done.1
  34.5 0.0 copy-done.2
  34.6 1.3 %shard_map.83.raw_ref = f32[1024,384]{1,0:T(8,128)S(1)} custom-call(bf16[8,128,256]{2,1,0:T(8,128)(2,1)S(1)} %shard_map.77.t0, bf16[8,128,256]{2,1,0:T(8,128)(2,1)S(1)} %shard_map.80.t1, bf16[8,128,256]{2,1,0:T(8,128)(2,1)S(1)} %shard_map.81.t2, bf16[8,128,256]{2,1,0:T(8,128)(2,1)S(1)} %shard_map.82.t3, bf16[2048,128]{1,0:T(8,128)(2,1)S(1)} %copy-done, ...), custom_call_target="tpu_custom_call" | custom-call | flops 805306368 | bytes 5242880 | tf_op jit(solution)/shard_map/pallas_call | solution.py:377
  35.8 0.0 copy-start.6
  35.8 3.3 %collective-permute-done.7.t1 = bf16[8,128,256]{2,1,0:T(8,128)(2,1)S(1)} collective-permute-done((bf16[8,128,256]{2,1,0:T(8,128)(2,1)S(1)}, bf16[8,128,256]{2,1,0:T(8,128)(2,1)S(1)}, u32[]{:S(2)}, u32[]{:S(2)}) %collective-permute-start.7) | collective-permute-done | bytes 524320 | tf_op jit(solution)/shard_map/ppermute | solution.py:60
  39.1 0.0 collective-permute-done.11.t3
  39.1 0.1 collective-permute-done.12.refs_1_
  39.3 5.5 %collective-permute-done.4.t0 = bf16[8,128,256]{2,1,0:T(8,128)(2,1)S(1)} collective-permute-done((bf16[8,128,256]{2,1,0:T(8,128)(2,1)S(1)}, bf16[8,128,256]{2,1,0:T(8,128)(2,1)S(1)}, u32[]{:S(2)}, u32[]{:S(2)}) %collective-permute-start.4) | collective-permute-done | bytes 524320 | tf_op jit(solution)/shard_map/ppermute | solution.py:60
  44.8 0.0 collective-permute-done.9.t2
  44.8 0.1 shard_map.89.refs_0_
  44.9 0.1 collective-permute-start.16
  45.0 0.1 collective-permute-start.17
  45.1 0.0 copy-done.6
  45.1 3.8 %shard_map.84 = (bf16[1024,128]{1,0:T(8,128)(2,1)S(1)}, bf16[1024,256]{1,0:T(8,128)(2,1)S(1)}, f32[9,128,256]{2,1,0:T(8,128)S(1)}, f32[128,256]{1,0:T(8,128)S(1)}, bf16[128,256]{1,0:T(8,128)(2,1)S(1)}) custom-call(f32[1024,384]{1,0:T(8,128)S(1)} %shard_map.83.raw_ref, bf16[8,128,256]{2,1,0:T(8,128)(2,1)S(1)} %collective-permute-done.4.t0, ...), custom_call_target="tpu_custom_call" | custom-call | flops 3221225472 | bytes 8388608 | tf_op jit(solution)/shard_map/pallas_call | solution.py:385
  48.9 0.0 collective-permute-done.16.refs_1_
  48.9 2.1 %collective-permute-start.18 = (bf16[16,128,256]{2,1,0:T(8,128)(2,1)S(1)}, bf16[16,128,256]{2,1,0:T(8,128)(2,1)S(1)}, u32[]{:S(2)}, u32[]{:S(2)}) collective-permute-start(bf16[16,128,256]{2,1,0:T(8,128)(2,1)S(1)} %collective-permute-done.16.refs_1_), channel_id=1, source_target_pairs={{0,4},{1,5},{2,6},{3,7},{4,0},{5,1},{6,2},{7,3},{8,12},{9,13},{10,... | collective-permute-start | bytes 3145736 | tf_op jit(solution)/shard_map/ppermute | solution.py:60
  51.0 1.1 %collective-permute-start.13 = (bf16[128,256]{1,0:T(8,128)(2,1)S(1)}, bf16[128,256]{1,0:T(8,128)(2,1)S(1)}, u32[]{:S(2)}, u32[]{:S(2)}) collective-permute-start(bf16[128,256]{1,0:T(8,128)(2,1)S(1)} %get-tuple-element.48), channel_id=1, source_target_pairs={{0,16},{16,0},{32,48},{48,32},{64,80},{80,64},{96,112},{112,96},{1... | collective-permute-start | bytes 196616 | tf_op jit(solution)/shard_map/ppermute | solution.py:408
  52.1 0.9 %collective-permute-done.13.other_ref.core_ref = bf16[128,256]{1,0:T(8,128)(2,1)S(1)} collective-permute-done((bf16[128,256]{1,0:T(8,128)(2,1)S(1)}, bf16[128,256]{1,0:T(8,128)(2,1)S(1)}, u32[]{:S(2)}, u32[]{:S(2)}) %collective-permute-start.13) | collective-permute-done | bytes 65568 | tf_op jit(solution)/shard_map/ppermute | solution.py:408
  53.0 0.2 shard_map.85.mine_ref
  53.1 1.6 %collective-permute-start.14 = (bf16[128,256]{1,0:T(8,128)(2,1)S(1)}, bf16[128,256]{1,0:T(8,128)(2,1)S(1)}, u32[]{:S(2)}, u32[]{:S(2)}) collective-permute-start(bf16[128,256]{1,0:T(8,128)(2,1)S(1)} %shard_map.85.mine_ref), channel_id=1, source_target_pairs={{0,32},{16,48},{32,0},{48,16},{64,96},{80,112},{96,64},{112,80},{1... | collective-permute-start | bytes 196616 | tf_op jit(solution)/shard_map/ppermute | solution.py:412
  54.8 2.2 %shard_map.86 = (bf16[1024,128]{1,0:T(8,128)(2,1)S(1)}, f32[1024,128]{1,0:T(8,128)S(1)}) custom-call(f32[1024,384]{1,0:T(8,128)S(1)} %shard_map.83.raw_ref, bf16[8,128,256]{2,1,0:T(8,128)(2,1)S(1)} %collective-permute-done.4.t0, bf16[8,128,256]{2,1,0:T(8,128)(2,1)S(1)} %collective-permute-done.7.t1, bf16[8,128,256]{2,1,0:T(8,128)(2,1)S(1)} %collective-permute-done.9.t2, ...), custom_call_target="tpu_custom_call" | custom-call | flops 536870912 | bytes 4194304 | tf_op jit(solution)/shard_map/pallas_call | solution.py:398
  57.0 0.6 collective-permute-done.14.other_ref.chip_ref
  57.6 0.1 shard_map.87
  57.7 3.1 %collective-permute-start.15 = (bf16[128,128]{1,0:T(8,128)(2,1)S(1)}, bf16[128,128]{1,0:T(8,128)(2,1)S(1)}, u32[]{:S(2)}, u32[]{:S(2)}) collective-permute-start(bf16[128,128]{1,0:T(8,128)(2,1)S(1)} %shard_map.87), channel_id=1, source_target_pairs={{0,96},{16,112},{32,64},{48,80},{64,32},{80,48},{96,0},{112,16},{1... | collective-permute-start | bytes 98312 | tf_op jit(solution)/shard_map/ppermute | solution.py:415
  60.8 2.1 %collective-permute-done.15.pair_ref = bf16[128,128]{1,0:T(8,128)(2,1)S(1)} collective-permute-done((bf16[128,128]{1,0:T(8,128)(2,1)S(1)}, bf16[128,128]{1,0:T(8,128)(2,1)S(1)}, u32[]{:S(2)}, u32[]{:S(2)}) %collective-permute-start.15) | collective-permute-done | bytes 32800 | tf_op jit(solution)/shard_map/ppermute | solution.py:415
  62.9 0.0 copy-done.5
  62.9 0.6 shard_map.88
  63.5 10.2 %all_to_all.9.x_ref = bf16[8,128,128]{2,1,0:T(8,128)(2,1)S(1)} all-to-all(bf16[8,128,128]{2,1,0:T(8,128)(2,1)S(1)} %bitcast.3), channel_id=1, replica_groups={{0,1,2,3,4,5,6,7},{8,9,10,11,12,13,14,15},{16,17,18,19,28,29,30,31},{20..., dimensions={0} | all-to-all | bytes 524288 | tf_op jit(solution)/shard_map/all_to_all | solution.py:425
  73.7 0.0 collective-permute-done.17.refs_2_
  73.7 0.0 collective-permute-done.18.refs_3_
  73.7 0.8 %shard_map.91 = bf16[64,2048]{1,0:T(8,128)(2,1)S(1)} custom-call(bf16[8,128,128]{2,1,0:T(8,128)(2,1)S(1)} %all_to_all.9.x_ref, bf16[16,128,256]{2,1,0:T(8,128)(2,1)S(1)} %shard_map.89.refs_0_, bf16[16,128,256]{2,1,0:T(8,128)(2,1)S(1)} %collective-permute-done.16.refs_1_, bf16[16,128,256]{2,1,0:T(8,128)(2,1)S(1)} %collective-permute-done.17.refs_2_, ...), custom_call_target="tpu_custom_call" | custom-call | flops 268435456 | bytes 4194304 | tf_op jit(solution)/shard_map/pallas_call | solution.py:430
  74.5 1.2 %collective-permute-start.19 = (bf16[64,2048]{1,0:T(8,128)(2,1)S(1)}, bf16[64,2048]{1,0:T(8,128)(2,1)S(1)}, u32[]{:S(2)}, u32[]{:S(2)}) collective-permute-start(bf16[64,2048]{1,0:T(8,128)(2,1)S(1)} %shard_map.91), channel_id=1, source_target_pairs={{0,12},{1,13},{2,14},{3,15},{4,8},{5,9},{6,10},{7,11},{8,4},{9,5},... | collective-permute-start | bytes 786440 | tf_op jit(solution)/shard_map/ppermute | solution.py:60
  75.7 0.8 %shard_map.90.own_ref = f32[64,2048]{1,0:T(8,128)S(1)} custom-call(bf16[8,128,128]{2,1,0:T(8,128)(2,1)S(1)} %all_to_all.9.x_ref, bf16[16,128,256]{2,1,0:T(8,128)(2,1)S(1)} %shard_map.89.refs_0_, bf16[16,128,256]{2,1,0:T(8,128)(2,1)S(1)} %collective-permute-done.16.refs_1_, bf16[16,128,256]{2,1,0:T(8,128)(2,1)S(1)} %collective-permute-done.17.refs_2_, ...), custom_call_target="tpu_custom_call" | custom-call | flops 268435456 | bytes 4194304 | tf_op jit(solution)/shard_map/pallas_call | solution.py:434
  76.6 5.6 %collective-permute-done.19.other_ref = bf16[64,2048]{1,0:T(8,128)(2,1)S(1)} collective-permute-done((bf16[64,2048]{1,0:T(8,128)(2,1)S(1)}, bf16[64,2048]{1,0:T(8,128)(2,1)S(1)}, u32[]{:S(2)}, u32[]{:S(2)}) %collective-permute-start.19) | collective-permute-done | bytes 262176 | tf_op jit(solution)/shard_map/ppermute | solution.py:60
  82.2 0.7 shard_map.92
  (11 shorter events, 0.3 us)
Async XLA Ops:
  0.0 0.9 %copy-start.4 = (bf16[1024,128]{1,0:T(8,128)(2,1)S(1)}, bf16[1024,128]{1,0:T(8,128)(2,1)}, u32[]{:S(2)}) copy-start(bf16[1024,128]{1,0:T(8,128)(2,1)} %tokens_ref.1) | copy-start | bytes 786436
  1.0 1.0 %copy-start.3 = (bf16[128,2048]{1,0:T(8,128)(2,1)S(1)}, bf16[128,2048]{1,0:T(8,128)(2,1)}, u32[]{:S(2)}) copy-start(bf16[128,2048]{1,0:T(8,128)(2,1)} %w_ref.1) | copy-start | bytes 1572868
  2.1 6.6 %collective-permute-start = (bf16[4,128,256]{2,1,0:T(8,128)(2,1)S(1)}, bf16[4,128,256]{2,1,0:T(8,128)(2,1)S(1)}, u32[]{:S(2)}, u32[]{:S(2)}) collective-permute-start(bf16[4,128,256]{2,1,0:T(8,128)(2,1)S(1)} %shard_map.74.refs_0_), channel_id=1, source_target_pairs={{0,1},{1,0},{2,3},{3,2},{4,5},{5,4},{6,7},{7,6},{8,9},{9,8},{10,11... | collective-permute-start | bytes 786440 | tf_op jit(solution)/shard_map/ppermute | solution.py:60
  3.7 5.0 %collective-permute-start.1 = (bf16[2,128,256]{2,1,0:T(8,128)(2,1)S(1)}, bf16[2,128,256]{2,1,0:T(8,128)(2,1)S(1)}, u32[]{:S(2)}, u32[]{:S(2)}) collective-permute-start(bf16[2,128,256]{2,1,0:T(8,128)(2,1)S(1)} %get-tuple-element.33.refs_0_), channel_id=1, source_target_pairs={{0,4},{1,5},{2,6},{3,7},{4,0},{5,1},{6,2},{7,3},{8,12},{9,13},{10,... | collective-permute-start | bytes 393224 | tf_op jit(solution)/shard_map/ppermute | solution.py:60
  8.7 12.7 %collective-permute-start.2 = (bf16[8,128,256]{2,1,0:T(8,128)(2,1)S(1)}, bf16[8,128,256]{2,1,0:T(8,128)(2,1)S(1)}, u32[]{:S(2)}, u32[]{:S(2)}) collective-permute-start(bf16[8,128,256]{2,1,0:T(8,128)(2,1)S(1)} %shard_map.75.one_ref), channel_id=1, source_target_pairs={{0,3},{1,2},{2,1},{3,0},{4,7},{5,6},{6,5},{7,4},{8,11},{9,10},{10,... | collective-permute-start | bytes 1572872 | tf_op jit(solution)/shard_map/ppermute | solution.py:60
  11.5 8.5 %collective-permute-start.5 = (bf16[4,128,256]{2,1,0:T(8,128)(2,1)S(1)}, bf16[4,128,256]{2,1,0:T(8,128)(2,1)S(1)}, u32[]{:S(2)}, u32[]{:S(2)}) collective-permute-start(bf16[4,128,256]{2,1,0:T(8,128)(2,1)S(1)} %shard_map.78.one_ref), channel_id=1, source_target_pairs={{0,12},{1,13},{2,14},{3,15},{4,8},{5,9},{6,10},{7,11},{8,4},{9,5},... | collective-permute-start | bytes 786440 | tf_op jit(solution)/shard_map/ppermute | solution.py:60
  20.0 7.1 %collective-permute-start.6 = (bf16[4,128,256]{2,1,0:T(8,128)(2,1)S(1)}, bf16[4,128,256]{2,1,0:T(8,128)(2,1)S(1)}, u32[]{:S(2)}, u32[]{:S(2)}) collective-permute-start(bf16[4,128,256]{2,1,0:T(8,128)(2,1)S(1)} %get-tuple-element.37.refs_0_), channel_id=1, source_target_pairs={{0,1},{1,0},{2,3},{3,2},{4,5},{5,4},{6,7},{7,6},{8,9},{9,8},{10,11... | collective-permute-start | bytes 786440 | tf_op jit(solution)/shard_map/ppermute | solution.py:60
  20.3 8.1 %collective-permute-start.10 = (bf16[4,128,256]{2,1,0:T(8,128)(2,1)S(1)}, bf16[4,128,256]{2,1,0:T(8,128)(2,1)S(1)}, u32[]{:S(2)}, u32[]{:S(2)}) collective-permute-start(bf16[4,128,256]{2,1,0:T(8,128)(2,1)S(1)} %get-tuple-element.39.refs_0_), channel_id=1, source_target_pairs={{0,3},{1,2},{2,1},{3,0},{4,7},{5,6},{6,5},{7,4},{8,11},{9,10},{10,... | collective-permute-start | bytes 786440 | tf_op jit(solution)/shard_map/ppermute | solution.py:60
  21.5 9.8 %collective-permute-start.3 = (bf16[4,128,256]{2,1,0:T(8,128)(2,1)S(1)}, bf16[4,128,256]{2,1,0:T(8,128)(2,1)S(1)}, u32[]{:S(2)}, u32[]{:S(2)}) collective-permute-start(bf16[4,128,256]{2,1,0:T(8,128)(2,1)S(1)} %get-tuple-element.35.refs_0_), channel_id=1, source_target_pairs={{0,4},{1,5},{2,6},{3,7},{4,0},{5,1},{6,2},{7,3},{8,12},{9,13},{10,... | collective-permute-start | bytes 786440 | tf_op jit(solution)/shard_map/ppermute | solution.py:60
  21.7 12.7 %collective-permute-start.8 = (bf16[4,128,256]{2,1,0:T(8,128)(2,1)S(1)}, bf16[4,128,256]{2,1,0:T(8,128)(2,1)S(1)}, u32[]{:S(2)}, u32[]{:S(2)}) collective-permute-start(bf16[4,128,256]{2,1,0:T(8,128)(2,1)S(1)} %get-tuple-element.38.refs_0_), channel_id=1, source_target_pairs={{0,12},{1,13},{2,14},{3,15},{4,8},{5,9},{6,10},{7,11},{8,4},{9,5},... | collective-permute-start | bytes 786440 | tf_op jit(solution)/shard_map/ppermute | solution.py:60
  27.2 7.3 %copy-start = (bf16[2048,128]{1,0:T(8,128)(2,1)S(1)}, bf16[2048,128]{1,0:T(8,128)(2,1)}, u32[]{:S(2)}) copy-start(bf16[2048,128]{1,0:T(8,128)(2,1)} %wq.3) | copy-start | bytes 1572868
  27.2 7.3 %copy-start.1 = (bf16[2048,128]{1,0:T(8,128)(2,1)S(1)}, bf16[2048,128]{1,0:T(8,128)(2,1)}, u32[]{:S(2)}) copy-start(bf16[2048,128]{1,0:T(8,128)(2,1)} %wk.3) | copy-start | bytes 1572868
  27.2 7.3 %copy-start.2 = (bf16[2048,128]{1,0:T(8,128)(2,1)S(1)}, bf16[2048,128]{1,0:T(8,128)(2,1)}, u32[]{:S(2)}) copy-start(bf16[2048,128]{1,0:T(8,128)(2,1)} %wv.3) | copy-start | bytes 1572868
  27.2 11.9 %collective-permute-start.7 = (bf16[8,128,256]{2,1,0:T(8,128)(2,1)S(1)}, bf16[8,128,256]{2,1,0:T(8,128)(2,1)S(1)}, u32[]{:S(2)}, u32[]{:S(2)}) collective-permute-start(bf16[8,128,256]{2,1,0:T(8,128)(2,1)S(1)} %shard_map.80.t1), channel_id=1, source_target_pairs={{0,3},{1,2},{2,1},{3,0},{4,7},{5,6},{6,5},{7,4},{8,11},{9,10},{10,... | collective-permute-start | bytes 1572872 | tf_op jit(solution)/shard_map/ppermute | solution.py:60
  28.5 10.7 %collective-permute-start.11 = (bf16[8,128,256]{2,1,0:T(8,128)(2,1)S(1)}, bf16[8,128,256]{2,1,0:T(8,128)(2,1)S(1)}, u32[]{:S(2)}, u32[]{:S(2)}) collective-permute-start(bf16[8,128,256]{2,1,0:T(8,128)(2,1)S(1)} %shard_map.82.t3), channel_id=1, source_target_pairs={{0,1},{1,0},{2,3},{3,2},{4,5},{5,4},{6,7},{7,6},{8,9},{9,8},{10,11... | collective-permute-start | bytes 1572872 | tf_op jit(solution)/shard_map/ppermute | solution.py:60
  29.7 9.6 %collective-permute-start.12 = (bf16[8,128,256]{2,1,0:T(8,128)(2,1)S(1)}, bf16[8,128,256]{2,1,0:T(8,128)(2,1)S(1)}, u32[]{:S(2)}, u32[]{:S(2)}) collective-permute-start(bf16[8,128,256]{2,1,0:T(8,128)(2,1)S(1)} %get-tuple-element.41.refs_0_), channel_id=1, source_target_pairs={{0,32},{16,48},{32,0},{48,16},{64,96},{80,112},{96,64},{112,80},{1... | collective-permute-start | bytes 1572872 | tf_op jit(solution)/shard_map/ppermute | solution.py:373
  31.4 13.5 %collective-permute-start.4 = (bf16[8,128,256]{2,1,0:T(8,128)(2,1)S(1)}, bf16[8,128,256]{2,1,0:T(8,128)(2,1)S(1)}, u32[]{:S(2)}, u32[]{:S(2)}) collective-permute-start(bf16[8,128,256]{2,1,0:T(8,128)(2,1)S(1)} %shard_map.77.t0), channel_id=1, source_target_pairs={{0,12},{1,13},{2,14},{3,15},{4,8},{5,9},{6,10},{7,11},{8,4},{9,5},... | collective-permute-start | bytes 1572872 | tf_op jit(solution)/shard_map/ppermute | solution.py:60
  34.4 10.4 %collective-permute-start.9 = (bf16[8,128,256]{2,1,0:T(8,128)(2,1)S(1)}, bf16[8,128,256]{2,1,0:T(8,128)(2,1)S(1)}, u32[]{:S(2)}, u32[]{:S(2)}) collective-permute-start(bf16[8,128,256]{2,1,0:T(8,128)(2,1)S(1)} %shard_map.81.t2), channel_id=1, source_target_pairs={{0,4},{1,5},{2,6},{3,7},{4,0},{5,1},{6,2},{7,3},{8,12},{9,13},{10,... | collective-permute-start | bytes 1572872 | tf_op jit(solution)/shard_map/ppermute | solution.py:60
  35.8 9.3 %copy-start.6 = (f32[1024,1]{0,1:T(1,128)S(1)}, f32[1024,1]{0,1:T(1,128)}, u32[]{:S(2)}) copy-start(f32[1024,1]{0,1:T(1,128)} %param.8) | copy-start | bytes 12292
  44.9 4.0 %collective-permute-start.16 = (bf16[16,128,256]{2,1,0:T(8,128)(2,1)S(1)}, bf16[16,128,256]{2,1,0:T(8,128)(2,1)S(1)}, u32[]{:S(2)}, u32[]{:S(2)}) collective-permute-start(bf16[16,128,256]{2,1,0:T(8,128)(2,1)S(1)} %shard_map.89.refs_0_), channel_id=1, source_target_pairs={{0,16},{16,0},{32,48},{48,32},{64,80},{80,64},{96,112},{112,96},{1... | collective-permute-start | bytes 3145736 | tf_op jit(solution)/shard_map/ppermute | solution.py:383
  45.0 28.7 %collective-permute-start.17 = (bf16[16,128,256]{2,1,0:T(8,128)(2,1)S(1)}, bf16[16,128,256]{2,1,0:T(8,128)(2,1)S(1)}, u32[]{:S(2)}, u32[]{:S(2)}) collective-permute-start(bf16[16,128,256]{2,1,0:T(8,128)(2,1)S(1)} %shard_map.89.refs_0_), channel_id=1, source_target_pairs={{0,4},{1,5},{2,6},{3,7},{4,0},{5,1},{6,2},{7,3},{8,12},{9,13},{10,... | collective-permute-start | bytes 3145736 | tf_op jit(solution)/shard_map/ppermute | solution.py:60
  48.9 24.8 %collective-permute-start.18 = (bf16[16,128,256]{2,1,0:T(8,128)(2,1)S(1)}, bf16[16,128,256]{2,1,0:T(8,128)(2,1)S(1)}, u32[]{:S(2)}, u32[]{:S(2)}) collective-permute-start(bf16[16,128,256]{2,1,0:T(8,128)(2,1)S(1)} %collective-permute-done.16.refs_1_), channel_id=1, source_target_pairs={{0,4},{1,5},{2,6},{3,7},{4,0},{5,1},{6,2},{7,3},{8,12},{9,13},{10,... | collective-permute-start | bytes 3145736 | tf_op jit(solution)/shard_map/ppermute | solution.py:60
  51.0 2.0 %collective-permute-start.13 = (bf16[128,256]{1,0:T(8,128)(2,1)S(1)}, bf16[128,256]{1,0:T(8,128)(2,1)S(1)}, u32[]{:S(2)}, u32[]{:S(2)}) collective-permute-start(bf16[128,256]{1,0:T(8,128)(2,1)S(1)} %get-tuple-element.48), channel_id=1, source_target_pairs={{0,16},{16,0},{32,48},{48,32},{64,80},{80,64},{96,112},{112,96},{1... | collective-permute-start | bytes 196616 | tf_op jit(solution)/shard_map/ppermute | solution.py:408
  53.1 4.4 %collective-permute-start.14 = (bf16[128,256]{1,0:T(8,128)(2,1)S(1)}, bf16[128,256]{1,0:T(8,128)(2,1)S(1)}, u32[]{:S(2)}, u32[]{:S(2)}) collective-permute-start(bf16[128,256]{1,0:T(8,128)(2,1)S(1)} %shard_map.85.mine_ref), channel_id=1, source_target_pairs={{0,32},{16,48},{32,0},{48,16},{64,96},{80,112},{96,64},{112,80},{1... | collective-permute-start | bytes 196616 | tf_op jit(solution)/shard_map/ppermute | solution.py:412
  54.8 8.1 %copy-start.5 = (f32[128]{0:T(128)S(1)}, f32[128]{0:T(128)}, u32[]{:S(2)}) copy-start(f32[128]{0:T(128)} %param.12) | copy-start | bytes 1540
  57.7 5.2 %collective-permute-start.15 = (bf16[128,128]{1,0:T(8,128)(2,1)S(1)}, bf16[128,128]{1,0:T(8,128)(2,1)S(1)}, u32[]{:S(2)}, u32[]{:S(2)}) collective-permute-start(bf16[128,128]{1,0:T(8,128)(2,1)S(1)} %shard_map.87), channel_id=1, source_target_pairs={{0,96},{16,112},{32,64},{48,80},{64,32},{80,48},{96,0},{112,16},{1... | collective-permute-start | bytes 98312 | tf_op jit(solution)/shard_map/ppermute | solution.py:415
  74.5 7.7 %collective-permute-start.19 = (bf16[64,2048]{1,0:T(8,128)(2,1)S(1)}, bf16[64,2048]{1,0:T(8,128)(2,1)S(1)}, u32[]{:S(2)}, u32[]{:S(2)}) collective-permute-start(bf16[64,2048]{1,0:T(8,128)(2,1)S(1)} %shard_map.91), channel_id=1, source_target_pairs={{0,12},{1,13},{2,14},{3,15},{4,8},{5,9},{6,10},{7,11},{8,4},{9,5},... | collective-permute-start | bytes 786440 | tf_op jit(solution)/shard_map/ppermute | solution.py:60

commit v5 on v4

--- a/solution.py
+++ b/solution.py
@@ -16,6 +16,21 @@
 def dot(left, right, contract=((1,), (0,))):
     return lax.dot_general(
         left.astype(BF16), right.astype(BF16), (contract, ((), ())), preferred_element_type=F32
+    )
+
+
+def halves(value):
+    high = value.astype(BF16)
+    return high, (value - high.astype(F32)).astype(BF16)
+
+
+def dot3(left, right, contract=((1,), (0,))):
+    (left_high, left_low), (right_high, right_low) = left, right
+    along_left, along_right = contract[0][0], contract[1][0]
+    return dot(
+        jnp.concatenate([left_high, left_high, left_low], axis=along_left),
+        jnp.concatenate([right_high, right_low, right_high], axis=along_right),
+        contract,
     )
 
 
@@ -172,12 +187,12 @@
     for b in range(count):
         part = slice(b * CHUNK, (b + 1) * CHUNK)
         key = unit_silu(total_ref[part, :DK])
-        key16 = key.astype(BF16)
-        k_ref[part, :] = key16
+        key_halves = halves(key)
+        k_ref[part, :] = key_halves[0]
         rate = jnp.transpose(jnp.broadcast_to(beta_ref[b : b + 1, :], (CHUNK, CHUNK)))
-        gram = dot(key16, key16, ((1,), (1,)))
+        gram = dot3(key_halves, key_halves, ((1,), (1,)))
         lower = jnp.where(row > col, rate * gram, 0.0)
-        keys.append(key)
+        keys.append((key, key_halves))
         rates.append(rate)
         lowers.append(lower)
         inverses.append(eye - jnp.where(below(1), lower, 0.0))
@@ -187,14 +202,21 @@
         inner = [dot(jnp.where(mask, lo, 0.0), inv) for lo, inv in zip(lowers, inverses)]
         inverses = [inv - dot(inv, x) for inv, x in zip(inverses, inner)]
         size *= 2
+    for b in range(count):
+        rough = inverses[b].astype(BF16)
+        product = dot(
+            jnp.concatenate(halves(lowers[b]), axis=1), jnp.concatenate([rough, rough], axis=0)
+        )
+        residual = eye - rough.astype(F32) - product
+        inverses[b] = rough.astype(F32) + dot(rough, residual)
     maps = []
     for b in range(count):
         part = slice(b * CHUNK, (b + 1) * CHUNK)
         value = total_ref[part, DK:]
-        both = jnp.concatenate([rates[b] * keys[b], rates[b] * value], axis=1)
-        wu = dot(inverses[b], both).astype(BF16)
+        both = jnp.concatenate([rates[b] * keys[b][0], rates[b] * value], axis=1)
+        wu = dot3(halves(inverses[b]), halves(both))
         wu_ref[part, :] = wu
-        maps.append(dot(k_ref[part, :], wu, ((0,), (0,))))
+        maps.append(dot3(keys[b][1], halves(wu), ((0,), (0,))))
     zeros = jnp.zeros((DK, DK), F32)
     half = count // 2
     states = [jnp.concatenate([eye, zeros], axis=1)] * 2
@@ -230,7 +252,7 @@
         part = slice(b * CHUNK, (b + 1) * CHUNK)
         query = unit_silu(total_ref[part, :])
         scores = jnp.where(row >= col, dot(query, k_ref[part, :], ((1,), (1,))), 0.0)
-        local = dot(scores, wu_ref[part, :])
+        local = dot3(halves(scores), halves(wu_ref[part, :]))
         effective = query - local[:, :DK]
         state = states_ref[b]
         if b >= count // 2:
@@ -386,7 +408,7 @@
         transition_kernel,
         (
             struct((rows, DK), BF16),
-            struct((rows, 2 * DK), BF16),
+            struct((rows, 2 * DK), F32),
             struct((rows // CHUNK + 1, DK, 2 * DK), F32),
             struct((DK, 2 * DK), F32),
             struct((DK, 2 * DK), BF16),

time: 83.2 us -> 85.2 us (1.024)
  Pallas kernels: 11 us -> 13.5 us
    pallas_call x1, Pallas kernels: 3.81 us -> 5.62 us  [local(): call(transition_kernel, (struct((rows, DK), BF16), struct((rows, 2 * DK),...]
  transfers between devices with their start and end apart: 20 -> 20, of which waited for: 11 -> 10; matrix products, arithmetic and copies ran while one was open for 0% -> 0% of each run, Pallas kernels for 11% -> 14%
where the time goes in v5:
time: 85.2 us; the launch traced here: 84.9 us
  starting transfers between devices  31.6 us (37%)
  waiting for transfers between devices  27.5 us (32%)
  Pallas kernels  13.5 us (16%)
  blocking collectives  10.1 us (12%)
  local copies, waits for them, and re-layouts  2.02 us (2%)
    ppermute x15, waiting for transfers between devices, swap(): return lax.ppermute(value, ('ctx', 'head'), pairs)  24.3 us
    ppermute x15, starting transfers between devices, swap(): return lax.ppermute(value, ('ctx', 'head'), pairs)  24 us
    all_to_all x1, blocking collectives, local(): lax.all_to_all(normed, ('ctx', 'head'), 0, 0, tiled=True, axis_index_grou...  10.1 us
    pallas_call x1, Pallas kernels, local(): call(transition_kernel, (struct((rows, DK), BF16), struct((rows, 2 * DK),...  5.62 us
    ppermute x1, starting transfers between devices, local(): of_pair = lax.ppermute(pair, 'ctx', [(c, c ^ 6) for c in range(ctx)])  3 us
    pallas_call x1, Pallas kernels, local(): call(outputs_kernel, (struct((rows, DK), BF16), struct((rows, DK), F32)),...  2.8 us
    ppermute x1, waiting for transfers between devices, local(): of_pair = lax.ppermute(pair, 'ctx', [(c, c ^ 6) for c in range(ctx)])  2.17 us
    unnamed x14, local copies, waits for them, and re-layouts  2.02 us
  transfers between devices with their start and end apart: 20, of which 10 were waited for; matrix products, arithmetic and copies ran while one was open for 0% of the time, Pallas kernels for 14%

profile of v5, /device:TPU:0, one launch (start us, length us, event | category | flops | bytes accessed | tf_op | source)
XLA Modules:
  0.0 84.9 jit_solution(8074000248914369267)
XLA Ops:
  0.0 0.9 %copy-done.4 = bf16[1024,128]{1,0:T(8,128)(2,1)S(1)} copy-done((bf16[1024,128]{1,0:T(8,128)(2,1)S(1)}, bf16[1024,128]{1,0:T(8,128)(2,1)}, u32[]{:S(2)}) %copy-start.4) | copy-done | bytes 262168
  1.0 0.0 copy-start.3
  1.0 1.0 %copy-done.3 = bf16[128,2048]{1,0:T(8,128)(2,1)S(1)} copy-done((bf16[128,2048]{1,0:T(8,128)(2,1)S(1)}, bf16[128,2048]{1,0:T(8,128)(2,1)}, u32[]{:S(2)}) %copy-start.3) | copy-done | bytes 524312
  2.1 1.7 %collective-permute-start = (bf16[4,128,256]{2,1,0:T(8,128)(2,1)S(1)}, bf16[4,128,256]{2,1,0:T(8,128)(2,1)S(1)}, u32[]{:S(2)}, u32[]{:S(2)}) collective-permute-start(bf16[4,128,256]{2,1,0:T(8,128)(2,1)S(1)} %shard_map.74.refs_0_), channel_id=1, source_target_pairs={{0,1},{1,0},{2,3},{3,2},{4,5},{5,4},{6,7},{7,6},{8,9},{9,8},{10,11... | collective-permute-start | bytes 786440 | tf_op jit(solution)/shard_map/ppermute | solution.py:75
  3.7 1.9 %collective-permute-start.1 = (bf16[2,128,256]{2,1,0:T(8,128)(2,1)S(1)}, bf16[2,128,256]{2,1,0:T(8,128)(2,1)S(1)}, u32[]{:S(2)}, u32[]{:S(2)}) collective-permute-start(bf16[2,128,256]{2,1,0:T(8,128)(2,1)S(1)} %get-tuple-element.33.refs_0_), channel_id=1, source_target_pairs={{0,4},{1,5},{2,6},{3,7},{4,0},{5,1},{6,2},{7,3},{8,12},{9,13},{10,... | collective-permute-start | bytes 393224 | tf_op jit(solution)/shard_map/ppermute | solution.py:75
  5.7 3.0 %collective-permute-done.1.refs_1_ = bf16[2,128,256]{2,1,0:T(8,128)(2,1)S(1)} collective-permute-done((bf16[2,128,256]{2,1,0:T(8,128)(2,1)S(1)}, bf16[2,128,256]{2,1,0:T(8,128)(2,1)S(1)}, u32[]{:S(2)}, u32[]{:S(2)}) %collective-permute-start.1) | collective-permute-done | bytes 131104 | tf_op jit(solution)/shard_map/ppermute | solution.py:75
  8.7 0.0 collective-permute-done.refs_1_
  8.7 2.7 %collective-permute-start.2 = (bf16[8,128,256]{2,1,0:T(8,128)(2,1)S(1)}, bf16[8,128,256]{2,1,0:T(8,128)(2,1)S(1)}, u32[]{:S(2)}, u32[]{:S(2)}) collective-permute-start(bf16[8,128,256]{2,1,0:T(8,128)(2,1)S(1)} %shard_map.75.one_ref), channel_id=1, source_target_pairs={{0,3},{1,2},{2,1},{3,0},{4,7},{5,6},{6,5},{7,4},{8,11},{9,10},{10,... | collective-permute-start | bytes 1572872 | tf_op jit(solution)/shard_map/ppermute | solution.py:75
  11.5 4.1 %collective-permute-start.5 = (bf16[4,128,256]{2,1,0:T(8,128)(2,1)S(1)}, bf16[4,128,256]{2,1,0:T(8,128)(2,1)S(1)}, u32[]{:S(2)}, u32[]{:S(2)}) collective-permute-start(bf16[4,128,256]{2,1,0:T(8,128)(2,1)S(1)} %shard_map.78.one_ref), channel_id=1, source_target_pairs={{0,12},{1,13},{2,14},{3,15},{4,8},{5,9},{6,10},{7,11},{8,4},{9,5},... | collective-permute-start | bytes 786440 | tf_op jit(solution)/shard_map/ppermute | solution.py:75
  15.6 4.4 %collective-permute-done.5.two_ref = bf16[4,128,256]{2,1,0:T(8,128)(2,1)S(1)} collective-permute-done((bf16[4,128,256]{2,1,0:T(8,128)(2,1)S(1)}, bf16[4,128,256]{2,1,0:T(8,128)(2,1)S(1)}, u32[]{:S(2)}, u32[]{:S(2)}) %collective-permute-start.5) | collective-permute-done | bytes 262176 | tf_op jit(solution)/shard_map/ppermute | solution.py:75
  20.0 0.3 collective-permute-start.6
  20.3 1.1 %collective-permute-start.10 = (bf16[4,128,256]{2,1,0:T(8,128)(2,1)S(1)}, bf16[4,128,256]{2,1,0:T(8,128)(2,1)S(1)}, u32[]{:S(2)}, u32[]{:S(2)}) collective-permute-start(bf16[4,128,256]{2,1,0:T(8,128)(2,1)S(1)} %get-tuple-element.39.refs_0_), channel_id=1, source_target_pairs={{0,3},{1,2},{2,1},{3,0},{4,7},{5,6},{6,5},{7,4},{8,11},{9,10},{10,... | collective-permute-start | bytes 786440 | tf_op jit(solution)/shard_map/ppermute | solution.py:75
  21.5 0.0 collective-permute-done.2.two_ref
  21.5 0.1 shard_map.76
  21.5 0.2 collective-permute-start.3
  21.7 3.2 %collective-permute-start.8 = (bf16[4,128,256]{2,1,0:T(8,128)(2,1)S(1)}, bf16[4,128,256]{2,1,0:T(8,128)(2,1)S(1)}, u32[]{:S(2)}, u32[]{:S(2)}) collective-permute-start(bf16[4,128,256]{2,1,0:T(8,128)(2,1)S(1)} %get-tuple-element.38.refs_0_), channel_id=1, source_target_pairs={{0,12},{1,13},{2,14},{3,15},{4,8},{5,9},{6,10},{7,11},{8,4},{9,5},... | collective-permute-start | bytes 786440 | tf_op jit(solution)/shard_map/ppermute | solution.py:75
  24.9 2.2 %collective-permute-done.6.refs_1_ = bf16[4,128,256]{2,1,0:T(8,128)(2,1)S(1)} collective-permute-done((bf16[4,128,256]{2,1,0:T(8,128)(2,1)S(1)}, bf16[4,128,256]{2,1,0:T(8,128)(2,1)S(1)}, u32[]{:S(2)}, u32[]{:S(2)}) %collective-permute-start.6) | collective-permute-done | bytes 262176 | tf_op jit(solution)/shard_map/ppermute | solution.py:75
  27.2 0.0 copy-start
  27.2 0.0 copy-start.1
  27.2 0.0 copy-start.2
  27.2 1.0 %collective-permute-start.7 = (bf16[8,128,256]{2,1,0:T(8,128)(2,1)S(1)}, bf16[8,128,256]{2,1,0:T(8,128)(2,1)S(1)}, u32[]{:S(2)}, u32[]{:S(2)}) collective-permute-start(bf16[8,128,256]{2,1,0:T(8,128)(2,1)S(1)} %shard_map.80.t1), channel_id=1, source_target_pairs={{0,3},{1,2},{2,1},{3,0},{4,7},{5,6},{6,5},{7,4},{8,11},{9,10},{10,... | collective-permute-start | bytes 1572872 | tf_op jit(solution)/shard_map/ppermute | solution.py:75
  28.3 0.2 collective-permute-done.10.refs_1_
  28.5 1.2 %collective-permute-start.11 = (bf16[8,128,256]{2,1,0:T(8,128)(2,1)S(1)}, bf16[8,128,256]{2,1,0:T(8,128)(2,1)S(1)}, u32[]{:S(2)}, u32[]{:S(2)}) collective-permute-start(bf16[8,128,256]{2,1,0:T(8,128)(2,1)S(1)} %shard_map.82.t3), channel_id=1, source_target_pairs={{0,1},{1,0},{2,3},{3,2},{4,5},{5,4},{6,7},{7,6},{8,9},{9,8},{10,11... | collective-permute-start | bytes 1572872 | tf_op jit(solution)/shard_map/ppermute | solution.py:75
  29.7 1.6 %collective-permute-start.12 = (bf16[8,128,256]{2,1,0:T(8,128)(2,1)S(1)}, bf16[8,128,256]{2,1,0:T(8,128)(2,1)S(1)}, u32[]{:S(2)}, u32[]{:S(2)}) collective-permute-start(bf16[8,128,256]{2,1,0:T(8,128)(2,1)S(1)} %get-tuple-element.41.refs_0_), channel_id=1, source_target_pairs={{0,32},{16,48},{32,0},{48,16},{64,96},{80,112},{96,64},{112,80},{1... | collective-permute-start | bytes 1572872 | tf_op jit(solution)/shard_map/ppermute | solution.py:395
  31.3 0.0 collective-permute-done.3.refs_1_
  31.4 3.0 %collective-permute-start.4 = (bf16[8,128,256]{2,1,0:T(8,128)(2,1)S(1)}, bf16[8,128,256]{2,1,0:T(8,128)(2,1)S(1)}, u32[]{:S(2)}, u32[]{:S(2)}) collective-permute-start(bf16[8,128,256]{2,1,0:T(8,128)(2,1)S(1)} %shard_map.77.t0), channel_id=1, source_target_pairs={{0,12},{1,13},{2,14},{3,15},{4,8},{5,9},{6,10},{7,11},{8,4},{9,5},... | collective-permute-start | bytes 1572872 | tf_op jit(solution)/shard_map/ppermute | solution.py:75
  34.4 0.0 collective-permute-done.8.refs_1_
  34.4 0.1 collective-permute-start.9
  34.5 0.0 copy-done
  34.5 0.0 copy-done.1
  34.5 0.0 copy-done.2
  34.6 1.3 %shard_map.83.raw_ref = f32[1024,384]{1,0:T(8,128)S(1)} custom-call(bf16[8,128,256]{2,1,0:T(8,128)(2,1)S(1)} %shard_map.77.t0, bf16[8,128,256]{2,1,0:T(8,128)(2,1)S(1)} %shard_map.80.t1, bf16[8,128,256]{2,1,0:T(8,128)(2,1)S(1)} %shard_map.81.t2, bf16[8,128,256]{2,1,0:T(8,128)(2,1)S(1)} %shard_map.82.t3, bf16[2048,128]{1,0:T(8,128)(2,1)S(1)} %copy-done, ...), custom_call_target="tpu_custom_call" | custom-call | flops 805306368 | bytes 5242880 | tf_op jit(solution)/shard_map/pallas_call | solution.py:399
  35.8 0.0 copy-start.6
  35.8 3.3 %collective-permute-done.7.t1 = bf16[8,128,256]{2,1,0:T(8,128)(2,1)S(1)} collective-permute-done((bf16[8,128,256]{2,1,0:T(8,128)(2,1)S(1)}, bf16[8,128,256]{2,1,0:T(8,128)(2,1)S(1)}, u32[]{:S(2)}, u32[]{:S(2)}) %collective-permute-start.7) | collective-permute-done | bytes 524320 | tf_op jit(solution)/shard_map/ppermute | solution.py:75
  39.1 0.0 collective-permute-done.11.t3
  39.1 0.1 collective-permute-done.12.refs_1_
  39.3 5.5 %collective-permute-done.4.t0 = bf16[8,128,256]{2,1,0:T(8,128)(2,1)S(1)} collective-permute-done((bf16[8,128,256]{2,1,0:T(8,128)(2,1)S(1)}, bf16[8,128,256]{2,1,0:T(8,128)(2,1)S(1)}, u32[]{:S(2)}, u32[]{:S(2)}) %collective-permute-start.4) | collective-permute-done | bytes 524320 | tf_op jit(solution)/shard_map/ppermute | solution.py:75
  44.8 0.0 collective-permute-done.9.t2
  44.8 0.1 shard_map.89.refs_0_
  44.9 0.1 collective-permute-start.16
  45.0 0.1 collective-permute-start.17
  45.1 0.0 copy-done.6
  45.1 5.6 %shard_map.84 = (bf16[1024,128]{1,0:T(8,128)(2,1)S(1)}, f32[1024,256]{1,0:T(8,128)S(1)}, f32[9,128,256]{2,1,0:T(8,128)S(1)}, f32[128,256]{1,0:T(8,128)S(1)}, bf16[128,256]{1,0:T(8,128)(2,1)S(1)}) custom-call(f32[1024,384]{1,0:T(8,128)S(1)} %shard_map.83.raw_ref, bf16[8,128,256]{2,1,0:T(8,128)(2,1)S(1)} %collective-permute-done.4.t0, ...), custom_call_target="tpu_custom_call" | custom-call | flops 3221225472 | bytes 8388608 | tf_op jit(solution)/shard_map/pallas_call | solution.py:407
  50.7 0.0 collective-permute-done.16.refs_1_
  50.7 2.1 %collective-permute-start.18 = (bf16[16,128,256]{2,1,0:T(8,128)(2,1)S(1)}, bf16[16,128,256]{2,1,0:T(8,128)(2,1)S(1)}, u32[]{:S(2)}, u32[]{:S(2)}) collective-permute-start(bf16[16,128,256]{2,1,0:T(8,128)(2,1)S(1)} %collective-permute-done.16.refs_1_), channel_id=1, source_target_pairs={{0,4},{1,5},{2,6},{3,7},{4,0},{5,1},{6,2},{7,3},{8,12},{9,13},{10,... | collective-permute-start | bytes 3145736 | tf_op jit(solution)/shard_map/ppermute | solution.py:75
  52.8 1.1 %collective-permute-start.13 = (bf16[128,256]{1,0:T(8,128)(2,1)S(1)}, bf16[128,256]{1,0:T(8,128)(2,1)S(1)}, u32[]{:S(2)}, u32[]{:S(2)}) collective-permute-start(bf16[128,256]{1,0:T(8,128)(2,1)S(1)} %get-tuple-element.48), channel_id=1, source_target_pairs={{0,16},{16,0},{32,48},{48,32},{64,80},{80,64},{96,112},{112,96},{1... | collective-permute-start | bytes 196616 | tf_op jit(solution)/shard_map/ppermute | solution.py:430
  53.9 0.9 %collective-permute-done.13.other_ref.core_ref = bf16[128,256]{1,0:T(8,128)(2,1)S(1)} collective-permute-done((bf16[128,256]{1,0:T(8,128)(2,1)S(1)}, bf16[128,256]{1,0:T(8,128)(2,1)S(1)}, u32[]{:S(2)}, u32[]{:S(2)}) %collective-permute-start.13) | collective-permute-done | bytes 65568 | tf_op jit(solution)/shard_map/ppermute | solution.py:430
  54.8 0.2 shard_map.85.mine_ref
  54.9 1.8 %collective-permute-start.14 = (bf16[128,256]{1,0:T(8,128)(2,1)S(1)}, bf16[128,256]{1,0:T(8,128)(2,1)S(1)}, u32[]{:S(2)}, u32[]{:S(2)}) collective-permute-start(bf16[128,256]{1,0:T(8,128)(2,1)S(1)} %shard_map.85.mine_ref), channel_id=1, source_target_pairs={{0,32},{16,48},{32,0},{48,16},{64,96},{80,112},{96,64},{112,80},{1... | collective-permute-start | bytes 196616 | tf_op jit(solution)/shard_map/ppermute | solution.py:434
  56.8 2.8 %shard_map.86 = (bf16[1024,128]{1,0:T(8,128)(2,1)S(1)}, f32[1024,128]{1,0:T(8,128)S(1)}) custom-call(f32[1024,384]{1,0:T(8,128)S(1)} %shard_map.83.raw_ref, bf16[8,128,256]{2,1,0:T(8,128)(2,1)S(1)} %collective-permute-done.4.t0, bf16[8,128,256]{2,1,0:T(8,128)(2,1)S(1)} %collective-permute-done.7.t1, bf16[8,128,256]{2,1,0:T(8,128)(2,1)S(1)} %collective-permute-done.9.t2, ...), custom_call_target="tpu_custom_call" | custom-call | flops 536870912 | bytes 4194304 | tf_op jit(solution)/shard_map/pallas_call | solution.py:420
  59.6 0.0 collective-permute-done.14.other_ref.chip_ref
  59.6 0.2 shard_map.87
  59.8 3.0 %collective-permute-start.15 = (bf16[128,128]{1,0:T(8,128)(2,1)S(1)}, bf16[128,128]{1,0:T(8,128)(2,1)S(1)}, u32[]{:S(2)}, u32[]{:S(2)}) collective-permute-start(bf16[128,128]{1,0:T(8,128)(2,1)S(1)} %shard_map.87), channel_id=1, source_target_pairs={{0,96},{16,112},{32,64},{48,80},{64,32},{80,48},{96,0},{112,16},{1... | collective-permute-start | bytes 98312 | tf_op jit(solution)/shard_map/ppermute | solution.py:437
  62.8 2.2 %collective-permute-done.15.pair_ref = bf16[128,128]{1,0:T(8,128)(2,1)S(1)} collective-permute-done((bf16[128,128]{1,0:T(8,128)(2,1)S(1)}, bf16[128,128]{1,0:T(8,128)(2,1)S(1)}, u32[]{:S(2)}, u32[]{:S(2)}) %collective-permute-start.15) | collective-permute-done | bytes 32800 | tf_op jit(solution)/shard_map/ppermute | solution.py:437
  64.9 0.0 copy-done.5
  64.9 0.6 shard_map.88
  65.6 10.1 %all_to_all.9.x_ref = bf16[8,128,128]{2,1,0:T(8,128)(2,1)S(1)} all-to-all(bf16[8,128,128]{2,1,0:T(8,128)(2,1)S(1)} %bitcast.3), channel_id=1, replica_groups={{0,1,2,3,4,5,6,7},{8,9,10,11,12,13,14,15},{16,17,18,19,28,29,30,31},{20..., dimensions={0} | all-to-all | bytes 524288 | tf_op jit(solution)/shard_map/all_to_all | solution.py:447
  75.7 0.0 collective-permute-done.17.refs_2_
  75.7 0.0 collective-permute-done.18.refs_3_
  75.7 0.8 shard_map.91
  76.5 1.2 %collective-permute-start.19 = (bf16[64,2048]{1,0:T(8,128)(2,1)S(1)}, bf16[64,2048]{1,0:T(8,128)(2,1)S(1)}, u32[]{:S(2)}, u32[]{:S(2)}) collective-permute-start(bf16[64,2048]{1,0:T(8,128)(2,1)S(1)} %shard_map.91), channel_id=1, source_target_pairs={{0,12},{1,13},{2,14},{3,15},{4,8},{5,9},{6,10},{7,11},{8,4},{9,5},... | collective-permute-start | bytes 786440 | tf_op jit(solution)/shard_map/ppermute | solution.py:75
  77.7 0.8 shard_map.90.own_ref
  78.6 5.6 %collective-permute-done.19.other_ref = bf16[64,2048]{1,0:T(8,128)(2,1)S(1)} collective-permute-done((bf16[64,2048]{1,0:T(8,128)(2,1)S(1)}, bf16[64,2048]{1,0:T(8,128)(2,1)S(1)}, u32[]{:S(2)}, u32[]{:S(2)}) %collective-permute-start.19) | collective-permute-done | bytes 262176 | tf_op jit(solution)/shard_map/ppermute | solution.py:75
  84.2 0.7 shard_map.92
  (11 shorter events, 0.3 us)
Async XLA Ops:
  0.0 0.9 %copy-start.4 = (bf16[1024,128]{1,0:T(8,128)(2,1)S(1)}, bf16[1024,128]{1,0:T(8,128)(2,1)}, u32[]{:S(2)}) copy-start(bf16[1024,128]{1,0:T(8,128)(2,1)} %tokens_ref.1) | copy-start | bytes 786436
  1.0 1.0 %copy-start.3 = (bf16[128,2048]{1,0:T(8,128)(2,1)S(1)}, bf16[128,2048]{1,0:T(8,128)(2,1)}, u32[]{:S(2)}) copy-start(bf16[128,2048]{1,0:T(8,128)(2,1)} %w_ref.1) | copy-start | bytes 1572868
  2.1 6.6 %collective-permute-start = (bf16[4,128,256]{2,1,0:T(8,128)(2,1)S(1)}, bf16[4,128,256]{2,1,0:T(8,128)(2,1)S(1)}, u32[]{:S(2)}, u32[]{:S(2)}) collective-permute-start(bf16[4,128,256]{2,1,0:T(8,128)(2,1)S(1)} %shard_map.74.refs_0_), channel_id=1, source_target_pairs={{0,1},{1,0},{2,3},{3,2},{4,5},{5,4},{6,7},{7,6},{8,9},{9,8},{10,11... | collective-permute-start | bytes 786440 | tf_op jit(solution)/shard_map/ppermute | solution.py:75
  3.7 5.0 %collective-permute-start.1 = (bf16[2,128,256]{2,1,0:T(8,128)(2,1)S(1)}, bf16[2,128,256]{2,1,0:T(8,128)(2,1)S(1)}, u32[]{:S(2)}, u32[]{:S(2)}) collective-permute-start(bf16[2,128,256]{2,1,0:T(8,128)(2,1)S(1)} %get-tuple-element.33.refs_0_), channel_id=1, source_target_pairs={{0,4},{1,5},{2,6},{3,7},{4,0},{5,1},{6,2},{7,3},{8,12},{9,13},{10,... | collective-permute-start | bytes 393224 | tf_op jit(solution)/shard_map/ppermute | solution.py:75
  8.7 12.7 %collective-permute-start.2 = (bf16[8,128,256]{2,1,0:T(8,128)(2,1)S(1)}, bf16[8,128,256]{2,1,0:T(8,128)(2,1)S(1)}, u32[]{:S(2)}, u32[]{:S(2)}) collective-permute-start(bf16[8,128,256]{2,1,0:T(8,128)(2,1)S(1)} %shard_map.75.one_ref), channel_id=1, source_target_pairs={{0,3},{1,2},{2,1},{3,0},{4,7},{5,6},{6,5},{7,4},{8,11},{9,10},{10,... | collective-permute-start | bytes 1572872 | tf_op jit(solution)/shard_map/ppermute | solution.py:75
  11.5 8.5 %collective-permute-start.5 = (bf16[4,128,256]{2,1,0:T(8,128)(2,1)S(1)}, bf16[4,128,256]{2,1,0:T(8,128)(2,1)S(1)}, u32[]{:S(2)}, u32[]{:S(2)}) collective-permute-start(bf16[4,128,256]{2,1,0:T(8,128)(2,1)S(1)} %shard_map.78.one_ref), channel_id=1, source_target_pairs={{0,12},{1,13},{2,14},{3,15},{4,8},{5,9},{6,10},{7,11},{8,4},{9,5},... | collective-permute-start | bytes 786440 | tf_op jit(solution)/shard_map/ppermute | solution.py:75
  20.0 7.1 %collective-permute-start.6 = (bf16[4,128,256]{2,1,0:T(8,128)(2,1)S(1)}, bf16[4,128,256]{2,1,0:T(8,128)(2,1)S(1)}, u32[]{:S(2)}, u32[]{:S(2)}) collective-permute-start(bf16[4,128,256]{2,1,0:T(8,128)(2,1)S(1)} %get-tuple-element.37.refs_0_), channel_id=1, source_target_pairs={{0,1},{1,0},{2,3},{3,2},{4,5},{5,4},{6,7},{7,6},{8,9},{9,8},{10,11... | collective-permute-start | bytes 786440 | tf_op jit(solution)/shard_map/ppermute | solution.py:75
  20.3 8.1 %collective-permute-start.10 = (bf16[4,128,256]{2,1,0:T(8,128)(2,1)S(1)}, bf16[4,128,256]{2,1,0:T(8,128)(2,1)S(1)}, u32[]{:S(2)}, u32[]{:S(2)}) collective-permute-start(bf16[4,128,256]{2,1,0:T(8,128)(2,1)S(1)} %get-tuple-element.39.refs_0_), channel_id=1, source_target_pairs={{0,3},{1,2},{2,1},{3,0},{4,7},{5,6},{6,5},{7,4},{8,11},{9,10},{10,... | collective-permute-start | bytes 786440 | tf_op jit(solution)/shard_map/ppermute | solution.py:75
  21.5 9.8 %collective-permute-start.3 = (bf16[4,128,256]{2,1,0:T(8,128)(2,1)S(1)}, bf16[4,128,256]{2,1,0:T(8,128)(2,1)S(1)}, u32[]{:S(2)}, u32[]{:S(2)}) collective-permute-start(bf16[4,128,256]{2,1,0:T(8,128)(2,1)S(1)} %get-tuple-element.35.refs_0_), channel_id=1, source_target_pairs={{0,4},{1,5},{2,6},{3,7},{4,0},{5,1},{6,2},{7,3},{8,12},{9,13},{10,... | collective-permute-start | bytes 786440 | tf_op jit(solution)/shard_map/ppermute | solution.py:75
  21.7 12.7 %collective-permute-start.8 = (bf16[4,128,256]{2,1,0:T(8,128)(2,1)S(1)}, bf16[4,128,256]{2,1,0:T(8,128)(2,1)S(1)}, u32[]{:S(2)}, u32[]{:S(2)}) collective-permute-start(bf16[4,128,256]{2,1,0:T(8,128)(2,1)S(1)} %get-tuple-element.38.refs_0_), channel_id=1, source_target_pairs={{0,12},{1,13},{2,14},{3,15},{4,8},{5,9},{6,10},{7,11},{8,4},{9,5},... | collective-permute-start | bytes 786440 | tf_op jit(solution)/shard_map/ppermute | solution.py:75
  27.2 7.3 %copy-start = (bf16[2048,128]{1,0:T(8,128)(2,1)S(1)}, bf16[2048,128]{1,0:T(8,128)(2,1)}, u32[]{:S(2)}) copy-start(bf16[2048,128]{1,0:T(8,128)(2,1)} %wq.3) | copy-start | bytes 1572868
  27.2 7.3 %copy-start.1 = (bf16[2048,128]{1,0:T(8,128)(2,1)S(1)}, bf16[2048,128]{1,0:T(8,128)(2,1)}, u32[]{:S(2)}) copy-start(bf16[2048,128]{1,0:T(8,128)(2,1)} %wk.3) | copy-start | bytes 1572868
  27.2 7.3 %copy-start.2 = (bf16[2048,128]{1,0:T(8,128)(2,1)S(1)}, bf16[2048,128]{1,0:T(8,128)(2,1)}, u32[]{:S(2)}) copy-start(bf16[2048,128]{1,0:T(8,128)(2,1)} %wv.3) | copy-start | bytes 1572868
  27.2 11.9 %collective-permute-start.7 = (bf16[8,128,256]{2,1,0:T(8,128)(2,1)S(1)}, bf16[8,128,256]{2,1,0:T(8,128)(2,1)S(1)}, u32[]{:S(2)}, u32[]{:S(2)}) collective-permute-start(bf16[8,128,256]{2,1,0:T(8,128)(2,1)S(1)} %shard_map.80.t1), channel_id=1, source_target_pairs={{0,3},{1,2},{2,1},{3,0},{4,7},{5,6},{6,5},{7,4},{8,11},{9,10},{10,... | collective-permute-start | bytes 1572872 | tf_op jit(solution)/shard_map/ppermute | solution.py:75
  28.5 10.7 %collective-permute-start.11 = (bf16[8,128,256]{2,1,0:T(8,128)(2,1)S(1)}, bf16[8,128,256]{2,1,0:T(8,128)(2,1)S(1)}, u32[]{:S(2)}, u32[]{:S(2)}) collective-permute-start(bf16[8,128,256]{2,1,0:T(8,128)(2,1)S(1)} %shard_map.82.t3), channel_id=1, source_target_pairs={{0,1},{1,0},{2,3},{3,2},{4,5},{5,4},{6,7},{7,6},{8,9},{9,8},{10,11... | collective-permute-start | bytes 1572872 | tf_op jit(solution)/shard_map/ppermute | solution.py:75
  29.7 9.6 %collective-permute-start.12 = (bf16[8,128,256]{2,1,0:T(8,128)(2,1)S(1)}, bf16[8,128,256]{2,1,0:T(8,128)(2,1)S(1)}, u32[]{:S(2)}, u32[]{:S(2)}) collective-permute-start(bf16[8,128,256]{2,1,0:T(8,128)(2,1)S(1)} %get-tuple-element.41.refs_0_), channel_id=1, source_target_pairs={{0,32},{16,48},{32,0},{48,16},{64,96},{80,112},{96,64},{112,80},{1... | collective-permute-start | bytes 1572872 | tf_op jit(solution)/shard_map/ppermute | solution.py:395
  31.4 13.5 %collective-permute-start.4 = (bf16[8,128,256]{2,1,0:T(8,128)(2,1)S(1)}, bf16[8,128,256]{2,1,0:T(8,128)(2,1)S(1)}, u32[]{:S(2)}, u32[]{:S(2)}) collective-permute-start(bf16[8,128,256]{2,1,0:T(8,128)(2,1)S(1)} %shard_map.77.t0), channel_id=1, source_target_pairs={{0,12},{1,13},{2,14},{3,15},{4,8},{5,9},{6,10},{7,11},{8,4},{9,5},... | collective-permute-start | bytes 1572872 | tf_op jit(solution)/shard_map/ppermute | solution.py:75
  34.4 10.4 %collective-permute-start.9 = (bf16[8,128,256]{2,1,0:T(8,128)(2,1)S(1)}, bf16[8,128,256]{2,1,0:T(8,128)(2,1)S(1)}, u32[]{:S(2)}, u32[]{:S(2)}) collective-permute-start(bf16[8,128,256]{2,1,0:T(8,128)(2,1)S(1)} %shard_map.81.t2), channel_id=1, source_target_pairs={{0,4},{1,5},{2,6},{3,7},{4,0},{5,1},{6,2},{7,3},{8,12},{9,13},{10,... | collective-permute-start | bytes 1572872 | tf_op jit(solution)/shard_map/ppermute | solution.py:75
  35.8 9.3 %copy-start.6 = (f32[1024,1]{0,1:T(1,128)S(1)}, f32[1024,1]{0,1:T(1,128)}, u32[]{:S(2)}) copy-start(f32[1024,1]{0,1:T(1,128)} %param.8) | copy-start | bytes 12292
  44.9 5.8 %collective-permute-start.16 = (bf16[16,128,256]{2,1,0:T(8,128)(2,1)S(1)}, bf16[16,128,256]{2,1,0:T(8,128)(2,1)S(1)}, u32[]{:S(2)}, u32[]{:S(2)}) collective-permute-start(bf16[16,128,256]{2,1,0:T(8,128)(2,1)S(1)} %shard_map.89.refs_0_), channel_id=1, source_target_pairs={{0,16},{16,0},{32,48},{48,32},{64,80},{80,64},{96,112},{112,96},{1... | collective-permute-start | bytes 3145736 | tf_op jit(solution)/shard_map/ppermute | solution.py:405
  45.0 30.7 %collective-permute-start.17 = (bf16[16,128,256]{2,1,0:T(8,128)(2,1)S(1)}, bf16[16,128,256]{2,1,0:T(8,128)(2,1)S(1)}, u32[]{:S(2)}, u32[]{:S(2)}) collective-permute-start(bf16[16,128,256]{2,1,0:T(8,128)(2,1)S(1)} %shard_map.89.refs_0_), channel_id=1, source_target_pairs={{0,4},{1,5},{2,6},{3,7},{4,0},{5,1},{6,2},{7,3},{8,12},{9,13},{10,... | collective-permute-start | bytes 3145736 | tf_op jit(solution)/shard_map/ppermute | solution.py:75
  50.7 24.9 %collective-permute-start.18 = (bf16[16,128,256]{2,1,0:T(8,128)(2,1)S(1)}, bf16[16,128,256]{2,1,0:T(8,128)(2,1)S(1)}, u32[]{:S(2)}, u32[]{:S(2)}) collective-permute-start(bf16[16,128,256]{2,1,0:T(8,128)(2,1)S(1)} %collective-permute-done.16.refs_1_), channel_id=1, source_target_pairs={{0,4},{1,5},{2,6},{3,7},{4,0},{5,1},{6,2},{7,3},{8,12},{9,13},{10,... | collective-permute-start | bytes 3145736 | tf_op jit(solution)/shard_map/ppermute | solution.py:75
  52.8 2.0 %collective-permute-start.13 = (bf16[128,256]{1,0:T(8,128)(2,1)S(1)}, bf16[128,256]{1,0:T(8,128)(2,1)S(1)}, u32[]{:S(2)}, u32[]{:S(2)}) collective-permute-start(bf16[128,256]{1,0:T(8,128)(2,1)S(1)} %get-tuple-element.48), channel_id=1, source_target_pairs={{0,16},{16,0},{32,48},{48,32},{64,80},{80,64},{96,112},{112,96},{1... | collective-permute-start | bytes 196616 | tf_op jit(solution)/shard_map/ppermute | solution.py:430
  54.9 4.7 %collective-permute-start.14 = (bf16[128,256]{1,0:T(8,128)(2,1)S(1)}, bf16[128,256]{1,0:T(8,128)(2,1)S(1)}, u32[]{:S(2)}, u32[]{:S(2)}) collective-permute-start(bf16[128,256]{1,0:T(8,128)(2,1)S(1)} %shard_map.85.mine_ref), channel_id=1, source_target_pairs={{0,32},{16,48},{32,0},{48,16},{64,96},{80,112},{96,64},{112,80},{1... | collective-permute-start | bytes 196616 | tf_op jit(solution)/shard_map/ppermute | solution.py:434
  56.8 8.2 %copy-start.5 = (f32[128]{0:T(128)S(1)}, f32[128]{0:T(128)}, u32[]{:S(2)}) copy-start(f32[128]{0:T(128)} %param.12) | copy-start | bytes 1540
  59.8 5.2 %collective-permute-start.15 = (bf16[128,128]{1,0:T(8,128)(2,1)S(1)}, bf16[128,128]{1,0:T(8,128)(2,1)S(1)}, u32[]{:S(2)}, u32[]{:S(2)}) collective-permute-start(bf16[128,128]{1,0:T(8,128)(2,1)S(1)} %shard_map.87), channel_id=1, source_target_pairs={{0,96},{16,112},{32,64},{48,80},{64,32},{80,48},{96,0},{112,16},{1... | collective-permute-start | bytes 98312 | tf_op jit(solution)/shard_map/ppermute | solution.py:437
  76.5 7.7 %collective-permute-start.19 = (bf16[64,2048]{1,0:T(8,128)(2,1)S(1)}, bf16[64,2048]{1,0:T(8,128)(2,1)S(1)}, u32[]{:S(2)}, u32[]{:S(2)}) collective-permute-start(bf16[64,2048]{1,0:T(8,128)(2,1)S(1)} %shard_map.91), channel_id=1, source_target_pairs={{0,12},{1,13},{2,14},{3,15},{4,8},{5,9},{6,10},{7,11},{8,4},{9,5},... | collective-permute-start | bytes 786440 | tf_op jit(solution)/shard_map/ppermute | solution.py:75

commit v6 on v5

--- a/solution.py
+++ b/solution.py
@@ -309,12 +309,12 @@
         normed_ref[pl.ds(start, 64), :] = normed[b * 64 : (b + 1) * 64, :]
 
 
-def mix_rows(x_ref, refs, rows, out_ref, dtype):
+def mix_rows(x_ref, refs, rows, out_ref, dtype, sides=(0, 1)):
     place = Place()
     seat = place.by_core(lax.rem(place.z, 2), lax.div(place.z, 2))
     along_x = [offsets(ALONG_X, c) for c in range(2)]
     even = lax.rem(place.y, 2)
-    for side in range(2):
+    for side in sides:
         core = place.core if side == 0 else 1 - place.core
         order = [
             place.x ^ place.by_core(along_x[side][j], along_x[1 - side][j]) for j in range(4)
@@ -335,20 +335,28 @@
                     term = jnp.dot(lefts[group, j], right, preferred_element_type=F32)
                     total = term if total is None else total + term
             parity = even if slab < 2 else 1 - even
-            start = pl.multiple_of((core * 2 + parity) * 512 + (slab % 2) * 256, 256)
+            column = core * 1024 if len(sides) == 2 else 0
+            start = pl.multiple_of(column + parity * 512 + (slab % 2) * 256, 256)
             out_ref[:, pl.ds(start, 256)] = total.astype(dtype)
 
 
-def mix_partner_kernel(x_ref, *refs):
-    mix_rows(x_ref, refs[:4], slice(64, 128), refs[4], BF16)
+def mix_partner_near_kernel(x_ref, near_ref, far_ref, out_ref):
+    mix_rows(x_ref, (near_ref, None, far_ref, None), slice(64, 128), out_ref, BF16, (0,))
+
+
+def mix_partner_other_kernel(x_ref, near_ref, far_ref, out_ref):
+    mix_rows(x_ref, (None, near_ref, None, far_ref), slice(64, 128), out_ref, BF16, (1,))
 
 
 def mix_own_kernel(x_ref, *refs):
     mix_rows(x_ref, refs[:4], slice(0, 64), refs[4], F32)
 
 
-def sum_kernel(own_ref, other_ref, mixed_ref):
-    mixed_ref[...] = (own_ref[...] + other_ref[...].astype(F32)).astype(BF16)
+def sum_kernel(own_ref, near_ref, other_ref, mixed_ref):
+    core = Place().core
+    for side, ref in ((core, near_ref), (1 - core, other_ref)):
+        columns = pl.ds(pl.multiple_of(side * 1024, 1024), 1024)
+        mixed_ref[:, columns] = (own_ref[:, columns] + ref[...].astype(F32)).astype(BF16)
 
 
 def call(kernel, shapes, n_vmem, scratch=(), flops=0, size=0):
@@ -449,14 +457,19 @@
     ).reshape(8, 2 * rows // heads, DK)
 
     operands = (spread_rows, w, w_next, far_a, far_b)
-    leaving = call(
-        mix_partner_kernel, struct((64, 2048), BF16), 5, flops=64 * 2048 * 2048, size=4 << 20
-    )(*operands)
-    entering = swap(leaving, OPPOSITE, ctx, heads)
+    half = struct((64, 1024), BF16)
+    near = call(mix_partner_near_kernel, half, 3, flops=64 * 2048 * 1024, size=2 << 20)(
+        spread_rows, w, far_a
+    )
+    near = swap(near, OPPOSITE, ctx, heads)
+    other = call(mix_partner_other_kernel, half, 3, flops=64 * 2048 * 1024, size=2 << 20)(
+        spread_rows, w_next, far_b
+    )
+    other = swap(other, OPPOSITE, ctx, heads)
     own = call(
         mix_own_kernel, struct((64, 2048), F32), 5, flops=64 * 2048 * 2048, size=4 << 20
     )(*operands)
-    return call(sum_kernel, struct((64, 2048), BF16), 2, size=1 << 20)(own, entering)
+    return call(sum_kernel, struct((64, 2048), BF16), 3, size=1 << 20)(own, near, other)
 
 
 def solution(mesh):

time: 85.2 us -> 85.1 us (level)
  waiting for transfers between devices: 27.5 us -> 25.1 us
  starting transfers between devices: 31.6 us -> 33.8 us
    ppermute x15 -> x16, waiting for transfers between devices: 24.3 us -> 21.9 us  [swap(): return lax.ppermute(value, ('ctx', 'head'), pairs)]
    ppermute x15 -> x16, starting transfers between devices: 24 us -> 26.2 us  [swap(): return lax.ppermute(value, ('ctx', 'head'), pairs)]
    pallas_call x2 -> x3, Pallas kernels: 1.59 us -> 1.71 us  [the longest x1 0.76 us: local(): call(sum_kernel, struct((64, 2048), BF16), 3, size=1 << 20)]
  transfers between devices with their start and end apart: 20 -> 21, of which waited for: 10 -> 11; matrix products, arithmetic and copies ran while one was open for 0% -> 0% of each run, Pallas kernels for 14% -> 15%
where the time goes in v6:
time: 85.1 us; the launch traced here: 84.8 us
  starting transfers between devices  33.8 us (40%)
  waiting for transfers between devices  25.1 us (29%)
  Pallas kernels  13.6 us (16%)
  blocking collectives  10.1 us (12%)
  local copies, waits for them, and re-layouts  2.02 us (2%)
    ppermute x16, starting transfers between devices, swap(): return lax.ppermute(value, ('ctx', 'head'), pairs)  26.2 us
    ppermute x16, waiting for transfers between devices, swap(): return lax.ppermute(value, ('ctx', 'head'), pairs)  21.9 us
    all_to_all x1, blocking collectives, local(): lax.all_to_all(normed, ('ctx', 'head'), 0, 0, tiled=True, axis_index_grou...  10.1 us
    pallas_call x1, Pallas kernels, local(): call(transition_kernel, (struct((rows, DK), BF16), struct((rows, 2 * DK),...  5.62 us
    ppermute x1, starting transfers between devices, local(): of_pair = lax.ppermute(pair, 'ctx', [(c, c ^ 6) for c in range(ctx)])  3 us
    pallas_call x1, Pallas kernels, local(): call(outputs_kernel, (struct((rows, DK), BF16), struct((rows, DK), F32)),...  2.8 us
    ppermute x1, waiting for transfers between devices, local(): of_pair = lax.ppermute(pair, 'ctx', [(c, c ^ 6) for c in range(ctx)])  2.17 us
    unnamed x14, local copies, waits for them, and re-layouts  2.02 us
  transfers between devices with their start and end apart: 21, of which 11 were waited for; matrix products, arithmetic and copies ran while one was open for 0% of the time, Pallas kernels for 15%

profile of v6, /device:TPU:0, one launch (start us, length us, event | category | flops | bytes accessed | tf_op | source)
XLA Modules:
  0.0 84.8 jit_solution(12601454126461515229)
XLA Ops:
  0.0 0.9 %copy-done.4 = bf16[1024,128]{1,0:T(8,128)(2,1)S(1)} copy-done((bf16[1024,128]{1,0:T(8,128)(2,1)S(1)}, bf16[1024,128]{1,0:T(8,128)(2,1)}, u32[]{:S(2)}) %copy-start.4) | copy-done | bytes 262168
  1.0 0.0 copy-start.3
  1.0 1.0 %copy-done.3 = bf16[128,2048]{1,0:T(8,128)(2,1)S(1)} copy-done((bf16[128,2048]{1,0:T(8,128)(2,1)S(1)}, bf16[128,2048]{1,0:T(8,128)(2,1)}, u32[]{:S(2)}) %copy-start.3) | copy-done | bytes 524312
  2.1 1.7 %collective-permute-start = (bf16[4,128,256]{2,1,0:T(8,128)(2,1)S(1)}, bf16[4,128,256]{2,1,0:T(8,128)(2,1)S(1)}, u32[]{:S(2)}, u32[]{:S(2)}) collective-permute-start(bf16[4,128,256]{2,1,0:T(8,128)(2,1)S(1)} %shard_map.74.refs_0_), channel_id=1, source_target_pairs={{0,1},{1,0},{2,3},{3,2},{4,5},{5,4},{6,7},{7,6},{8,9},{9,8},{10,11... | collective-permute-start | bytes 786440 | tf_op jit(solution)/shard_map/ppermute | solution.py:75
  3.7 1.9 %collective-permute-start.1 = (bf16[2,128,256]{2,1,0:T(8,128)(2,1)S(1)}, bf16[2,128,256]{2,1,0:T(8,128)(2,1)S(1)}, u32[]{:S(2)}, u32[]{:S(2)}) collective-permute-start(bf16[2,128,256]{2,1,0:T(8,128)(2,1)S(1)} %get-tuple-element.33.refs_0_), channel_id=1, source_target_pairs={{0,4},{1,5},{2,6},{3,7},{4,0},{5,1},{6,2},{7,3},{8,12},{9,13},{10,... | collective-permute-start | bytes 393224 | tf_op jit(solution)/shard_map/ppermute | solution.py:75
  5.7 3.0 %collective-permute-done.1.refs_1_ = bf16[2,128,256]{2,1,0:T(8,128)(2,1)S(1)} collective-permute-done((bf16[2,128,256]{2,1,0:T(8,128)(2,1)S(1)}, bf16[2,128,256]{2,1,0:T(8,128)(2,1)S(1)}, u32[]{:S(2)}, u32[]{:S(2)}) %collective-permute-start.1) | collective-permute-done | bytes 131104 | tf_op jit(solution)/shard_map/ppermute | solution.py:75
  8.7 0.0 collective-permute-done.refs_1_
  8.7 2.7 %collective-permute-start.2 = (bf16[8,128,256]{2,1,0:T(8,128)(2,1)S(1)}, bf16[8,128,256]{2,1,0:T(8,128)(2,1)S(1)}, u32[]{:S(2)}, u32[]{:S(2)}) collective-permute-start(bf16[8,128,256]{2,1,0:T(8,128)(2,1)S(1)} %shard_map.75.one_ref), channel_id=1, source_target_pairs={{0,3},{1,2},{2,1},{3,0},{4,7},{5,6},{6,5},{7,4},{8,11},{9,10},{10,... | collective-permute-start | bytes 1572872 | tf_op jit(solution)/shard_map/ppermute | solution.py:75
  11.5 4.1 %collective-permute-start.5 = (bf16[4,128,256]{2,1,0:T(8,128)(2,1)S(1)}, bf16[4,128,256]{2,1,0:T(8,128)(2,1)S(1)}, u32[]{:S(2)}, u32[]{:S(2)}) collective-permute-start(bf16[4,128,256]{2,1,0:T(8,128)(2,1)S(1)} %shard_map.78.one_ref), channel_id=1, source_target_pairs={{0,12},{1,13},{2,14},{3,15},{4,8},{5,9},{6,10},{7,11},{8,4},{9,5},... | collective-permute-start | bytes 786440 | tf_op jit(solution)/shard_map/ppermute | solution.py:75
  15.6 4.4 %collective-permute-done.5.two_ref = bf16[4,128,256]{2,1,0:T(8,128)(2,1)S(1)} collective-permute-done((bf16[4,128,256]{2,1,0:T(8,128)(2,1)S(1)}, bf16[4,128,256]{2,1,0:T(8,128)(2,1)S(1)}, u32[]{:S(2)}, u32[]{:S(2)}) %collective-permute-start.5) | collective-permute-done | bytes 262176 | tf_op jit(solution)/shard_map/ppermute | solution.py:75
  20.0 0.3 collective-permute-start.6
  20.3 1.1 %collective-permute-start.10 = (bf16[4,128,256]{2,1,0:T(8,128)(2,1)S(1)}, bf16[4,128,256]{2,1,0:T(8,128)(2,1)S(1)}, u32[]{:S(2)}, u32[]{:S(2)}) collective-permute-start(bf16[4,128,256]{2,1,0:T(8,128)(2,1)S(1)} %get-tuple-element.39.refs_0_), channel_id=1, source_target_pairs={{0,3},{1,2},{2,1},{3,0},{4,7},{5,6},{6,5},{7,4},{8,11},{9,10},{10,... | collective-permute-start | bytes 786440 | tf_op jit(solution)/shard_map/ppermute | solution.py:75
  21.5 0.0 collective-permute-done.2.two_ref
  21.5 0.1 shard_map.76
  21.5 0.2 collective-permute-start.3
  21.7 3.2 %collective-permute-start.8 = (bf16[4,128,256]{2,1,0:T(8,128)(2,1)S(1)}, bf16[4,128,256]{2,1,0:T(8,128)(2,1)S(1)}, u32[]{:S(2)}, u32[]{:S(2)}) collective-permute-start(bf16[4,128,256]{2,1,0:T(8,128)(2,1)S(1)} %get-tuple-element.38.refs_0_), channel_id=1, source_target_pairs={{0,12},{1,13},{2,14},{3,15},{4,8},{5,9},{6,10},{7,11},{8,4},{9,5},... | collective-permute-start | bytes 786440 | tf_op jit(solution)/shard_map/ppermute | solution.py:75
  24.9 2.2 %collective-permute-done.6.refs_1_ = bf16[4,128,256]{2,1,0:T(8,128)(2,1)S(1)} collective-permute-done((bf16[4,128,256]{2,1,0:T(8,128)(2,1)S(1)}, bf16[4,128,256]{2,1,0:T(8,128)(2,1)S(1)}, u32[]{:S(2)}, u32[]{:S(2)}) %collective-permute-start.6) | collective-permute-done | bytes 262176 | tf_op jit(solution)/shard_map/ppermute | solution.py:75
  27.2 0.0 copy-start
  27.2 0.0 copy-start.1
  27.2 0.0 copy-start.2
  27.2 1.0 %collective-permute-start.7 = (bf16[8,128,256]{2,1,0:T(8,128)(2,1)S(1)}, bf16[8,128,256]{2,1,0:T(8,128)(2,1)S(1)}, u32[]{:S(2)}, u32[]{:S(2)}) collective-permute-start(bf16[8,128,256]{2,1,0:T(8,128)(2,1)S(1)} %shard_map.80.t1), channel_id=1, source_target_pairs={{0,3},{1,2},{2,1},{3,0},{4,7},{5,6},{6,5},{7,4},{8,11},{9,10},{10,... | collective-permute-start | bytes 1572872 | tf_op jit(solution)/shard_map/ppermute | solution.py:75
  28.3 0.2 collective-permute-done.10.refs_1_
  28.5 1.2 %collective-permute-start.11 = (bf16[8,128,256]{2,1,0:T(8,128)(2,1)S(1)}, bf16[8,128,256]{2,1,0:T(8,128)(2,1)S(1)}, u32[]{:S(2)}, u32[]{:S(2)}) collective-permute-start(bf16[8,128,256]{2,1,0:T(8,128)(2,1)S(1)} %shard_map.82.t3), channel_id=1, source_target_pairs={{0,1},{1,0},{2,3},{3,2},{4,5},{5,4},{6,7},{7,6},{8,9},{9,8},{10,11... | collective-permute-start | bytes 1572872 | tf_op jit(solution)/shard_map/ppermute | solution.py:75
  29.7 1.6 %collective-permute-start.12 = (bf16[8,128,256]{2,1,0:T(8,128)(2,1)S(1)}, bf16[8,128,256]{2,1,0:T(8,128)(2,1)S(1)}, u32[]{:S(2)}, u32[]{:S(2)}) collective-permute-start(bf16[8,128,256]{2,1,0:T(8,128)(2,1)S(1)} %get-tuple-element.41.refs_0_), channel_id=1, source_target_pairs={{0,32},{16,48},{32,0},{48,16},{64,96},{80,112},{96,64},{112,80},{1... | collective-permute-start | bytes 1572872 | tf_op jit(solution)/shard_map/ppermute | solution.py:403
  31.3 0.0 collective-permute-done.3.refs_1_
  31.4 3.0 %collective-permute-start.4 = (bf16[8,128,256]{2,1,0:T(8,128)(2,1)S(1)}, bf16[8,128,256]{2,1,0:T(8,128)(2,1)S(1)}, u32[]{:S(2)}, u32[]{:S(2)}) collective-permute-start(bf16[8,128,256]{2,1,0:T(8,128)(2,1)S(1)} %shard_map.77.t0), channel_id=1, source_target_pairs={{0,12},{1,13},{2,14},{3,15},{4,8},{5,9},{6,10},{7,11},{8,4},{9,5},... | collective-permute-start | bytes 1572872 | tf_op jit(solution)/shard_map/ppermute | solution.py:75
  34.4 0.0 collective-permute-done.8.refs_1_
  34.4 0.1 collective-permute-start.9
  34.5 0.0 copy-done
  34.5 0.0 copy-done.1
  34.6 1.3 %shard_map.83.raw_ref = f32[1024,384]{1,0:T(8,128)S(1)} custom-call(bf16[8,128,256]{2,1,0:T(8,128)(2,1)S(1)} %shard_map.77.t0, bf16[8,128,256]{2,1,0:T(8,128)(2,1)S(1)} %shard_map.80.t1, bf16[8,128,256]{2,1,0:T(8,128)(2,1)S(1)} %shard_map.81.t2, bf16[8,128,256]{2,1,0:T(8,128)(2,1)S(1)} %shard_map.82.t3, bf16[2048,128]{1,0:T(8,128)(2,1)S(1)} %copy-done, ...), custom_call_target="tpu_custom_call" | custom-call | flops 805306368 | bytes 5242880 | tf_op jit(solution)/shard_map/pallas_call | solution.py:407
  35.8 0.0 copy-start.6
  35.8 3.3 %collective-permute-done.7.t1 = bf16[8,128,256]{2,1,0:T(8,128)(2,1)S(1)} collective-permute-done((bf16[8,128,256]{2,1,0:T(8,128)(2,1)S(1)}, bf16[8,128,256]{2,1,0:T(8,128)(2,1)S(1)}, u32[]{:S(2)}, u32[]{:S(2)}) %collective-permute-start.7) | collective-permute-done | bytes 524320 | tf_op jit(solution)/shard_map/ppermute | solution.py:75
  39.1 0.0 collective-permute-done.11.t3
  39.1 0.1 collective-permute-done.12.refs_1_
  39.3 5.5 %collective-permute-done.4.t0 = bf16[8,128,256]{2,1,0:T(8,128)(2,1)S(1)} collective-permute-done((bf16[8,128,256]{2,1,0:T(8,128)(2,1)S(1)}, bf16[8,128,256]{2,1,0:T(8,128)(2,1)S(1)}, u32[]{:S(2)}, u32[]{:S(2)}) %collective-permute-start.4) | collective-permute-done | bytes 524320 | tf_op jit(solution)/shard_map/ppermute | solution.py:75
  44.8 0.0 collective-permute-done.9.t2
  44.8 0.1 shard_map.89.refs_0_.near_ref
  44.9 0.1 collective-permute-start.16
  45.0 0.1 collective-permute-start.17
  45.1 5.6 %shard_map.84 = (bf16[1024,128]{1,0:T(8,128)(2,1)S(1)}, f32[1024,256]{1,0:T(8,128)S(1)}, f32[9,128,256]{2,1,0:T(8,128)S(1)}, f32[128,256]{1,0:T(8,128)S(1)}, bf16[128,256]{1,0:T(8,128)(2,1)S(1)}) custom-call(f32[1024,384]{1,0:T(8,128)S(1)} %shard_map.83.raw_ref, bf16[8,128,256]{2,1,0:T(8,128)(2,1)S(1)} %collective-permute-done.4.t0, ...), custom_call_target="tpu_custom_call" | custom-call | flops 3221225472 | bytes 8388608 | tf_op jit(solution)/shard_map/pallas_call | solution.py:415
  50.7 0.0 collective-permute-done.16.refs_1_.near_ref
  50.7 2.1 %collective-permute-start.18 = (bf16[16,128,256]{2,1,0:T(8,128)(2,1)S(1)}, bf16[16,128,256]{2,1,0:T(8,128)(2,1)S(1)}, u32[]{:S(2)}, u32[]{:S(2)}) collective-permute-start(bf16[16,128,256]{2,1,0:T(8,128)(2,1)S(1)} %collective-permute-done.16.refs_1_.near_ref), channel_id=1, source_target_pairs={{0,4},{1,5},{2,6},{3,7},{4,0},{5,1},{6,2},{7,3},{8,12},{9,13},{10,... | collective-permute-start | bytes 3145736 | tf_op jit(solution)/shard_map/ppermute | solution.py:75
  52.8 1.1 %collective-permute-start.13 = (bf16[128,256]{1,0:T(8,128)(2,1)S(1)}, bf16[128,256]{1,0:T(8,128)(2,1)S(1)}, u32[]{:S(2)}, u32[]{:S(2)}) collective-permute-start(bf16[128,256]{1,0:T(8,128)(2,1)S(1)} %get-tuple-element.48), channel_id=1, source_target_pairs={{0,16},{16,0},{32,48},{48,32},{64,80},{80,64},{96,112},{112,96},{1... | collective-permute-start | bytes 196616 | tf_op jit(solution)/shard_map/ppermute | solution.py:438
  53.9 0.9 %collective-permute-done.13.other_ref.core_ref = bf16[128,256]{1,0:T(8,128)(2,1)S(1)} collective-permute-done((bf16[128,256]{1,0:T(8,128)(2,1)S(1)}, bf16[128,256]{1,0:T(8,128)(2,1)S(1)}, u32[]{:S(2)}, u32[]{:S(2)}) %collective-permute-start.13) | collective-permute-done | bytes 65568 | tf_op jit(solution)/shard_map/ppermute | solution.py:438
  54.8 0.2 shard_map.85.mine_ref
  54.9 1.8 %collective-permute-start.14 = (bf16[128,256]{1,0:T(8,128)(2,1)S(1)}, bf16[128,256]{1,0:T(8,128)(2,1)S(1)}, u32[]{:S(2)}, u32[]{:S(2)}) collective-permute-start(bf16[128,256]{1,0:T(8,128)(2,1)S(1)} %shard_map.85.mine_ref), channel_id=1, source_target_pairs={{0,32},{16,48},{32,0},{48,16},{64,96},{80,112},{96,64},{112,80},{1... | collective-permute-start | bytes 196616 | tf_op jit(solution)/shard_map/ppermute | solution.py:442
  56.8 2.8 %shard_map.86 = (bf16[1024,128]{1,0:T(8,128)(2,1)S(1)}, f32[1024,128]{1,0:T(8,128)S(1)}) custom-call(f32[1024,384]{1,0:T(8,128)S(1)} %shard_map.83.raw_ref, bf16[8,128,256]{2,1,0:T(8,128)(2,1)S(1)} %collective-permute-done.4.t0, bf16[8,128,256]{2,1,0:T(8,128)(2,1)S(1)} %collective-permute-done.7.t1, bf16[8,128,256]{2,1,0:T(8,128)(2,1)S(1)} %collective-permute-done.9.t2, ...), custom_call_target="tpu_custom_call" | custom-call | flops 536870912 | bytes 4194304 | tf_op jit(solution)/shard_map/pallas_call | solution.py:428
  59.6 0.0 collective-permute-done.14.other_ref.chip_ref
  59.6 0.2 shard_map.87
  59.8 3.0 %collective-permute-start.15 = (bf16[128,128]{1,0:T(8,128)(2,1)S(1)}, bf16[128,128]{1,0:T(8,128)(2,1)S(1)}, u32[]{:S(2)}, u32[]{:S(2)}) collective-permute-start(bf16[128,128]{1,0:T(8,128)(2,1)S(1)} %shard_map.87), channel_id=1, source_target_pairs={{0,96},{16,112},{32,64},{48,80},{64,32},{80,48},{96,0},{112,16},{1... | collective-permute-start | bytes 98312 | tf_op jit(solution)/shard_map/ppermute | solution.py:445
  62.8 2.2 %collective-permute-done.15.pair_ref = bf16[128,128]{1,0:T(8,128)(2,1)S(1)} collective-permute-done((bf16[128,128]{1,0:T(8,128)(2,1)S(1)}, bf16[128,128]{1,0:T(8,128)(2,1)S(1)}, u32[]{:S(2)}, u32[]{:S(2)}) %collective-permute-start.15) | collective-permute-done | bytes 32800 | tf_op jit(solution)/shard_map/ppermute | solution.py:445
  64.9 0.6 shard_map.88
  65.6 10.1 %all_to_all.9.x_ref = bf16[8,128,128]{2,1,0:T(8,128)(2,1)S(1)} all-to-all(bf16[8,128,128]{2,1,0:T(8,128)(2,1)S(1)} %bitcast.3), channel_id=1, replica_groups={{0,1,2,3,4,5,6,7},{8,9,10,11,12,13,14,15},{16,17,18,19,28,29,30,31},{20..., dimensions={0} | all-to-all | bytes 524288 | tf_op jit(solution)/shard_map/all_to_all | solution.py:455
  75.7 0.0 collective-permute-done.17.refs_2_.far_ref
  75.7 0.5 shard_map.91
  76.2 1.2 %collective-permute-start.19 = (bf16[64,1024]{1,0:T(8,128)(2,1)S(1)}, bf16[64,1024]{1,0:T(8,128)(2,1)S(1)}, u32[]{:S(2)}, u32[]{:S(2)}) collective-permute-start(bf16[64,1024]{1,0:T(8,128)(2,1)S(1)} %shard_map.91), channel_id=1, source_target_pairs={{0,12},{1,13},{2,14},{3,15},{4,8},{5,9},{6,10},{7,11},{8,4},{9,5},... | collective-permute-start | bytes 393224 | tf_op jit(solution)/shard_map/ppermute | solution.py:75
  77.3 0.0 collective-permute-done.18.refs_3_.far_ref
  77.3 0.5 shard_map.92
  77.8 2.2 %collective-permute-start.20 = (bf16[64,1024]{1,0:T(8,128)(2,1)S(1)}, bf16[64,1024]{1,0:T(8,128)(2,1)S(1)}, u32[]{:S(2)}, u32[]{:S(2)}) collective-permute-start(bf16[64,1024]{1,0:T(8,128)(2,1)S(1)} %shard_map.92), channel_id=1, source_target_pairs={{0,12},{1,13},{2,14},{3,15},{4,8},{5,9},{6,10},{7,11},{8,4},{9,5},... | collective-permute-start | bytes 393224 | tf_op jit(solution)/shard_map/ppermute | solution.py:75
  80.0 0.8 shard_map.90.own_ref
  80.9 1.5 %collective-permute-done.19.near_ref = bf16[64,1024]{1,0:T(8,128)(2,1)S(1)} collective-permute-done((bf16[64,1024]{1,0:T(8,128)(2,1)S(1)}, bf16[64,1024]{1,0:T(8,128)(2,1)S(1)}, u32[]{:S(2)}, u32[]{:S(2)}) %collective-permute-start.19) | collective-permute-done | bytes 131104 | tf_op jit(solution)/shard_map/ppermute | solution.py:75
  82.4 1.7 %collective-permute-done.20.other_ref = bf16[64,1024]{1,0:T(8,128)(2,1)S(1)} collective-permute-done((bf16[64,1024]{1,0:T(8,128)(2,1)S(1)}, bf16[64,1024]{1,0:T(8,128)(2,1)S(1)}, u32[]{:S(2)}, u32[]{:S(2)}) %collective-permute-start.20) | collective-permute-done | bytes 131104 | tf_op jit(solution)/shard_map/ppermute | solution.py:75
  84.1 0.8 shard_map.93
  (14 shorter events, 0.3 us)
Async XLA Ops:
  0.0 0.9 %copy-start.4 = (bf16[1024,128]{1,0:T(8,128)(2,1)S(1)}, bf16[1024,128]{1,0:T(8,128)(2,1)}, u32[]{:S(2)}) copy-start(bf16[1024,128]{1,0:T(8,128)(2,1)} %tokens_ref.1) | copy-start | bytes 786436
  1.0 1.0 %copy-start.3 = (bf16[128,2048]{1,0:T(8,128)(2,1)S(1)}, bf16[128,2048]{1,0:T(8,128)(2,1)}, u32[]{:S(2)}) copy-start(bf16[128,2048]{1,0:T(8,128)(2,1)} %w_ref.1) | copy-start | bytes 1572868
  2.1 6.6 %collective-permute-start = (bf16[4,128,256]{2,1,0:T(8,128)(2,1)S(1)}, bf16[4,128,256]{2,1,0:T(8,128)(2,1)S(1)}, u32[]{:S(2)}, u32[]{:S(2)}) collective-permute-start(bf16[4,128,256]{2,1,0:T(8,128)(2,1)S(1)} %shard_map.74.refs_0_), channel_id=1, source_target_pairs={{0,1},{1,0},{2,3},{3,2},{4,5},{5,4},{6,7},{7,6},{8,9},{9,8},{10,11... | collective-permute-start | bytes 786440 | tf_op jit(solution)/shard_map/ppermute | solution.py:75
  3.7 5.0 %collective-permute-start.1 = (bf16[2,128,256]{2,1,0:T(8,128)(2,1)S(1)}, bf16[2,128,256]{2,1,0:T(8,128)(2,1)S(1)}, u32[]{:S(2)}, u32[]{:S(2)}) collective-permute-start(bf16[2,128,256]{2,1,0:T(8,128)(2,1)S(1)} %get-tuple-element.33.refs_0_), channel_id=1, source_target_pairs={{0,4},{1,5},{2,6},{3,7},{4,0},{5,1},{6,2},{7,3},{8,12},{9,13},{10,... | collective-permute-start | bytes 393224 | tf_op jit(solution)/shard_map/ppermute | solution.py:75
  8.7 12.7 %collective-permute-start.2 = (bf16[8,128,256]{2,1,0:T(8,128)(2,1)S(1)}, bf16[8,128,256]{2,1,0:T(8,128)(2,1)S(1)}, u32[]{:S(2)}, u32[]{:S(2)}) collective-permute-start(bf16[8,128,256]{2,1,0:T(8,128)(2,1)S(1)} %shard_map.75.one_ref), channel_id=1, source_target_pairs={{0,3},{1,2},{2,1},{3,0},{4,7},{5,6},{6,5},{7,4},{8,11},{9,10},{10,... | collective-permute-start | bytes 1572872 | tf_op jit(solution)/shard_map/ppermute | solution.py:75
  11.5 8.5 %collective-permute-start.5 = (bf16[4,128,256]{2,1,0:T(8,128)(2,1)S(1)}, bf16[4,128,256]{2,1,0:T(8,128)(2,1)S(1)}, u32[]{:S(2)}, u32[]{:S(2)}) collective-permute-start(bf16[4,128,256]{2,1,0:T(8,128)(2,1)S(1)} %shard_map.78.one_ref), channel_id=1, source_target_pairs={{0,12},{1,13},{2,14},{3,15},{4,8},{5,9},{6,10},{7,11},{8,4},{9,5},... | collective-permute-start | bytes 786440 | tf_op jit(solution)/shard_map/ppermute | solution.py:75
  20.0 7.1 %collective-permute-start.6 = (bf16[4,128,256]{2,1,0:T(8,128)(2,1)S(1)}, bf16[4,128,256]{2,1,0:T(8,128)(2,1)S(1)}, u32[]{:S(2)}, u32[]{:S(2)}) collective-permute-start(bf16[4,128,256]{2,1,0:T(8,128)(2,1)S(1)} %get-tuple-element.37.refs_0_), channel_id=1, source_target_pairs={{0,1},{1,0},{2,3},{3,2},{4,5},{5,4},{6,7},{7,6},{8,9},{9,8},{10,11... | collective-permute-start | bytes 786440 | tf_op jit(solution)/shard_map/ppermute | solution.py:75
  20.3 8.1 %collective-permute-start.10 = (bf16[4,128,256]{2,1,0:T(8,128)(2,1)S(1)}, bf16[4,128,256]{2,1,0:T(8,128)(2,1)S(1)}, u32[]{:S(2)}, u32[]{:S(2)}) collective-permute-start(bf16[4,128,256]{2,1,0:T(8,128)(2,1)S(1)} %get-tuple-element.39.refs_0_), channel_id=1, source_target_pairs={{0,3},{1,2},{2,1},{3,0},{4,7},{5,6},{6,5},{7,4},{8,11},{9,10},{10,... | collective-permute-start | bytes 786440 | tf_op jit(solution)/shard_map/ppermute | solution.py:75
  21.5 9.8 %collective-permute-start.3 = (bf16[4,128,256]{2,1,0:T(8,128)(2,1)S(1)}, bf16[4,128,256]{2,1,0:T(8,128)(2,1)S(1)}, u32[]{:S(2)}, u32[]{:S(2)}) collective-permute-start(bf16[4,128,256]{2,1,0:T(8,128)(2,1)S(1)} %get-tuple-element.35.refs_0_), channel_id=1, source_target_pairs={{0,4},{1,5},{2,6},{3,7},{4,0},{5,1},{6,2},{7,3},{8,12},{9,13},{10,... | collective-permute-start | bytes 786440 | tf_op jit(solution)/shard_map/ppermute | solution.py:75
  21.7 12.7 %collective-permute-start.8 = (bf16[4,128,256]{2,1,0:T(8,128)(2,1)S(1)}, bf16[4,128,256]{2,1,0:T(8,128)(2,1)S(1)}, u32[]{:S(2)}, u32[]{:S(2)}) collective-permute-start(bf16[4,128,256]{2,1,0:T(8,128)(2,1)S(1)} %get-tuple-element.38.refs_0_), channel_id=1, source_target_pairs={{0,12},{1,13},{2,14},{3,15},{4,8},{5,9},{6,10},{7,11},{8,4},{9,5},... | collective-permute-start | bytes 786440 | tf_op jit(solution)/shard_map/ppermute | solution.py:75
  27.2 7.3 %copy-start = (bf16[2048,128]{1,0:T(8,128)(2,1)S(1)}, bf16[2048,128]{1,0:T(8,128)(2,1)}, u32[]{:S(2)}) copy-start(bf16[2048,128]{1,0:T(8,128)(2,1)} %wq.3) | copy-start | bytes 1572868
  27.2 7.3 %copy-start.1 = (bf16[2048,128]{1,0:T(8,128)(2,1)S(1)}, bf16[2048,128]{1,0:T(8,128)(2,1)}, u32[]{:S(2)}) copy-start(bf16[2048,128]{1,0:T(8,128)(2,1)} %wk.3) | copy-start | bytes 1572868
  27.2 7.3 %copy-start.2 = (bf16[2048,128]{1,0:T(8,128)(2,1)S(1)}, bf16[2048,128]{1,0:T(8,128)(2,1)}, u32[]{:S(2)}) copy-start(bf16[2048,128]{1,0:T(8,128)(2,1)} %wv.3) | copy-start | bytes 1572868
  27.2 11.9 %collective-permute-start.7 = (bf16[8,128,256]{2,1,0:T(8,128)(2,1)S(1)}, bf16[8,128,256]{2,1,0:T(8,128)(2,1)S(1)}, u32[]{:S(2)}, u32[]{:S(2)}) collective-permute-start(bf16[8,128,256]{2,1,0:T(8,128)(2,1)S(1)} %shard_map.80.t1), channel_id=1, source_target_pairs={{0,3},{1,2},{2,1},{3,0},{4,7},{5,6},{6,5},{7,4},{8,11},{9,10},{10,... | collective-permute-start | bytes 1572872 | tf_op jit(solution)/shard_map/ppermute | solution.py:75
  28.5 10.7 %collective-permute-start.11 = (bf16[8,128,256]{2,1,0:T(8,128)(2,1)S(1)}, bf16[8,128,256]{2,1,0:T(8,128)(2,1)S(1)}, u32[]{:S(2)}, u32[]{:S(2)}) collective-permute-start(bf16[8,128,256]{2,1,0:T(8,128)(2,1)S(1)} %shard_map.82.t3), channel_id=1, source_target_pairs={{0,1},{1,0},{2,3},{3,2},{4,5},{5,4},{6,7},{7,6},{8,9},{9,8},{10,11... | collective-permute-start | bytes 1572872 | tf_op jit(solution)/shard_map/ppermute | solution.py:75
  29.7 9.6 %collective-permute-start.12 = (bf16[8,128,256]{2,1,0:T(8,128)(2,1)S(1)}, bf16[8,128,256]{2,1,0:T(8,128)(2,1)S(1)}, u32[]{:S(2)}, u32[]{:S(2)}) collective-permute-start(bf16[8,128,256]{2,1,0:T(8,128)(2,1)S(1)} %get-tuple-element.41.refs_0_), channel_id=1, source_target_pairs={{0,32},{16,48},{32,0},{48,16},{64,96},{80,112},{96,64},{112,80},{1... | collective-permute-start | bytes 1572872 | tf_op jit(solution)/shard_map/ppermute | solution.py:403
  31.4 13.5 %collective-permute-start.4 = (bf16[8,128,256]{2,1,0:T(8,128)(2,1)S(1)}, bf16[8,128,256]{2,1,0:T(8,128)(2,1)S(1)}, u32[]{:S(2)}, u32[]{:S(2)}) collective-permute-start(bf16[8,128,256]{2,1,0:T(8,128)(2,1)S(1)} %shard_map.77.t0), channel_id=1, source_target_pairs={{0,12},{1,13},{2,14},{3,15},{4,8},{5,9},{6,10},{7,11},{8,4},{9,5},... | collective-permute-start | bytes 1572872 | tf_op jit(solution)/shard_map/ppermute | solution.py:75
  34.4 10.4 %collective-permute-start.9 = (bf16[8,128,256]{2,1,0:T(8,128)(2,1)S(1)}, bf16[8,128,256]{2,1,0:T(8,128)(2,1)S(1)}, u32[]{:S(2)}, u32[]{:S(2)}) collective-permute-start(bf16[8,128,256]{2,1,0:T(8,128)(2,1)S(1)} %shard_map.81.t2), channel_id=1, source_target_pairs={{0,4},{1,5},{2,6},{3,7},{4,0},{5,1},{6,2},{7,3},{8,12},{9,13},{10,... | collective-permute-start | bytes 1572872 | tf_op jit(solution)/shard_map/ppermute | solution.py:75
  35.8 9.3 %copy-start.6 = (f32[1024,1]{0,1:T(1,128)S(1)}, f32[1024,1]{0,1:T(1,128)}, u32[]{:S(2)}) copy-start(f32[1024,1]{0,1:T(1,128)} %param.8) | copy-start | bytes 12292
  44.9 5.8 %collective-permute-start.16 = (bf16[16,128,256]{2,1,0:T(8,128)(2,1)S(1)}, bf16[16,128,256]{2,1,0:T(8,128)(2,1)S(1)}, u32[]{:S(2)}, u32[]{:S(2)}) collective-permute-start(bf16[16,128,256]{2,1,0:T(8,128)(2,1)S(1)} %shard_map.89.refs_0_.near_ref), channel_id=1, source_target_pairs={{0,16},{16,0},{32,48},{48,32},{64,80},{80,64},{96,112},{112,96},{1... | collective-permute-start | bytes 3145736 | tf_op jit(solution)/shard_map/ppermute | solution.py:413
  45.0 30.7 %collective-permute-start.17 = (bf16[16,128,256]{2,1,0:T(8,128)(2,1)S(1)}, bf16[16,128,256]{2,1,0:T(8,128)(2,1)S(1)}, u32[]{:S(2)}, u32[]{:S(2)}) collective-permute-start(bf16[16,128,256]{2,1,0:T(8,128)(2,1)S(1)} %shard_map.89.refs_0_.near_ref), channel_id=1, source_target_pairs={{0,4},{1,5},{2,6},{3,7},{4,0},{5,1},{6,2},{7,3},{8,12},{9,13},{10,... | collective-permute-start | bytes 3145736 | tf_op jit(solution)/shard_map/ppermute | solution.py:75
  50.7 26.6 %collective-permute-start.18 = (bf16[16,128,256]{2,1,0:T(8,128)(2,1)S(1)}, bf16[16,128,256]{2,1,0:T(8,128)(2,1)S(1)}, u32[]{:S(2)}, u32[]{:S(2)}) collective-permute-start(bf16[16,128,256]{2,1,0:T(8,128)(2,1)S(1)} %collective-permute-done.16.refs_1_.near_ref), channel_id=1, source_target_pairs={{0,4},{1,5},{2,6},{3,7},{4,0},{5,1},{6,2},{7,3},{8,12},{9,13},{10,... | collective-permute-start | bytes 3145736 | tf_op jit(solution)/shard_map/ppermute | solution.py:75
  52.8 2.0 %collective-permute-start.13 = (bf16[128,256]{1,0:T(8,128)(2,1)S(1)}, bf16[128,256]{1,0:T(8,128)(2,1)S(1)}, u32[]{:S(2)}, u32[]{:S(2)}) collective-permute-start(bf16[128,256]{1,0:T(8,128)(2,1)S(1)} %get-tuple-element.48), channel_id=1, source_target_pairs={{0,16},{16,0},{32,48},{48,32},{64,80},{80,64},{96,112},{112,96},{1... | collective-permute-start | bytes 196616 | tf_op jit(solution)/shard_map/ppermute | solution.py:438
  54.9 4.7 %collective-permute-start.14 = (bf16[128,256]{1,0:T(8,128)(2,1)S(1)}, bf16[128,256]{1,0:T(8,128)(2,1)S(1)}, u32[]{:S(2)}, u32[]{:S(2)}) collective-permute-start(bf16[128,256]{1,0:T(8,128)(2,1)S(1)} %shard_map.85.mine_ref), channel_id=1, source_target_pairs={{0,32},{16,48},{32,0},{48,16},{64,96},{80,112},{96,64},{112,80},{1... | collective-permute-start | bytes 196616 | tf_op jit(solution)/shard_map/ppermute | solution.py:442
  56.8 8.2 %copy-start.5 = (f32[128]{0:T(128)S(1)}, f32[128]{0:T(128)}, u32[]{:S(2)}) copy-start(f32[128]{0:T(128)} %param.12) | copy-start | bytes 1540
  59.8 5.2 %collective-permute-start.15 = (bf16[128,128]{1,0:T(8,128)(2,1)S(1)}, bf16[128,128]{1,0:T(8,128)(2,1)S(1)}, u32[]{:S(2)}, u32[]{:S(2)}) collective-permute-start(bf16[128,128]{1,0:T(8,128)(2,1)S(1)} %shard_map.87), channel_id=1, source_target_pairs={{0,96},{16,112},{32,64},{48,80},{64,32},{80,48},{96,0},{112,16},{1... | collective-permute-start | bytes 98312 | tf_op jit(solution)/shard_map/ppermute | solution.py:445
  76.2 6.3 %collective-permute-start.19 = (bf16[64,1024]{1,0:T(8,128)(2,1)S(1)}, bf16[64,1024]{1,0:T(8,128)(2,1)S(1)}, u32[]{:S(2)}, u32[]{:S(2)}) collective-permute-start(bf16[64,1024]{1,0:T(8,128)(2,1)S(1)} %shard_map.91), channel_id=1, source_target_pairs={{0,12},{1,13},{2,14},{3,15},{4,8},{5,9},{6,10},{7,11},{8,4},{9,5},... | collective-permute-start | bytes 393224 | tf_op jit(solution)/shard_map/ppermute | solution.py:75
  77.8 6.3 %collective-permute-start.20 = (bf16[64,1024]{1,0:T(8,128)(2,1)S(1)}, bf16[64,1024]{1,0:T(8,128)(2,1)S(1)}, u32[]{:S(2)}, u32[]{:S(2)}) collective-permute-start(bf16[64,1024]{1,0:T(8,128)(2,1)S(1)} %shard_map.92), channel_id=1, source_target_pairs={{0,12},{1,13},{2,14},{3,15},{4,8},{5,9},{6,10},{7,11},{8,4},{9,5},... | collective-permute-start | bytes 393224 | tf_op jit(solution)/shard_map/ppermute | solution.py:75
